TPU v7x, 32 devices: a whole 2x2x4 slice. The times are simulated.
32 devices in a mesh: lat: 8 (over z, x), lev: 4 (over y, core).
Axes of the slice: x: 2, y: 2, z: 4, core: 2. Of those that a mesh axis runs over, the one named last changes fastest.
Arguments:
- fields: float32 [2, 32, 64, 3072], P(None, 'lat', 'lev'), may hold values from -6 to 6
- courant: bfloat16 [2, 32, 64, 3072], P(None, 'lat', 'lev'), may hold values from -0.3984375 to 0.3984375
- cutoffs: int32 [32], replicated, may hold values from 1 to 1536, as said below
- surface: float32 [32, 3072], P('lat'), may hold values from -6 to 6
- remap_weights: float32 [64, 64], replicated, may hold values from -0.25 to 0.75
Outputs:
- remapped: float32 [2, 32, 64, 3072], P(None, 'lat', None, 'lev')
- geopotential: float32 [32, 64, 3072], P('lat', None, 'lev')
Inputs may be any that keep to these rules, and one draw needn't show every extreme that they name: cutoffs[j] is 1536 except on the first and the last 4 latitudes, where it lies between 1 and 127; it equals 127 on some latitude among the first 4.
All inputs are finite; a program needn't handle non-finite values.
Results may differ from a plain program's by a relative error of at most 0.0003.
Values may be sent and summed in bfloat16 or wider, within the bound.
No kernel may reach another device: no remote copies, remote signals or barrier semaphores. Data moves between devices by JAX's collectives and lax.ppermute only.
A program may use at most 64 MiB of HBM per device.

v0:
```python
import functools
import math

import jax
import jax.numpy as jnp
import ml_dtypes
import numpy as np
from jax import lax
from jax.experimental import pallas as pl
from jax.experimental.pallas import tpu as pltpu
from jax.sharding import PartitionSpec as P

KMAX = 128
LANE = 128
TOP = 32767.0
STEPS = 256.0
TINY = 2.0**-100
WIND = 81920.0
ROUND = 1.5 * 2.0**23
VMEM_LIMIT = 12 * 2**20
VMEM_MOST = 63 * 2**20 + 2**19


def rounded(values):
    return ((values + ROUND) - ROUND).astype(jnp.int32).astype(jnp.int16)


def lane_max(values):
    chunks = [jnp.abs(values[:, i : i + LANE]) for i in range(0, values.shape[1], LANE)]
    while len(chunks) > 1:
        pairs = [jnp.maximum(a, b) for a, b in zip(chunks[0::2], chunks[1::2])]
        chunks = pairs + chunks[2 * len(pairs) :]
    return chunks[0]


def tiled(tile, width):
    return jnp.concatenate([tile] * (width // LANE), axis=1)


def scale_code(largest):
    return jnp.ceil(jnp.log2(jnp.maximum(largest, TINY)) * STEPS)


def encoder(code):
    return TOP / jnp.exp2(code * (1.0 / STEPS))


def decoder(code16):
    code = code16.astype(jnp.int32).astype(jnp.float32)
    return jnp.exp2(code * (1.0 / STEPS)) * (1.0 / TOP)


def encode_row(values, out_ref, at):
    width = values.shape[1]
    code = scale_code(lane_max(values))
    out_ref[:, at : at + width] = rounded(values * tiled(encoder(code), width))
    out_ref[:, at + width : at + width + LANE] = code.astype(jnp.int32).astype(jnp.int16)


def decode_row(in_ref, at, width):
    scale = decoder(in_ref[:, at + width : at + width + LANE])
    values = in_ref[:, at : at + width].astype(jnp.int32).astype(jnp.float32)
    return values * tiled(scale, width)


def fold(wind):
    middle = wind.shape[1] // 2
    return jnp.concatenate([wind[:, :middle], wind[:, middle:]], axis=0)


def unfold(values):
    half = values.shape[0] // 2
    return jnp.concatenate([values[:half], values[half:]], axis=1)


def wind_codes(values):
    return rounded(values * WIND)


def wind_values(codes):
    return codes.astype(jnp.int32).astype(jnp.float32) * (1.0 / WIND)


class Sizes:
    def __init__(self, rows, levels, lon):
        self.rows, self.levels, self.lon = rows, levels, lon
        self.half = levels // 2
        self.band = 2 * rows
        self.pad = lon + 2 * LANE
        self.code = lon + LANE
        self.edge = 2 * self.code + lon // 2
        self.middle = self.edge + lon // 2
        self.last = 2 * lon + lon // 2


def put_padded(ref, index, values, lon):
    ref[index + (Ellipsis, slice(LANE, LANE + lon))] = values
    ref[index + (Ellipsis, slice(0, LANE))] = values[..., lon - LANE :]
    ref[index + (Ellipsis, slice(LANE + lon, 2 * LANE + lon))] = values[..., :LANE]


def level_half(z, wind, upper):
    wind = wind.astype(jnp.float32)
    return jnp.where(upper == 1, wind[z.half :], wind[: z.half])


def edge_kernel(z, fields_ref, courant_ref, edge_ref, rows_ref, wind_ref, sems):
    p = lax.rem(lax.axis_index("lat"), 2)
    give = pl.multiple_of((1 - p) * z.half, z.half)
    copies = [
        pltpu.make_async_copy(
            fields_ref.at[f, 2 * p + r, pl.ds(give, z.half)],
            rows_ref.at[r, pl.ds(f * z.half, z.half)],
            sems.at[2 * r + f],
        )
        for r in range(2)
        for f in range(2)
    ]
    copies.append(pltpu.make_async_copy(courant_ref.at[1, 3 * p], wind_ref, sems.at[4]))
    for copy in copies:
        copy.start()
    for r in range(2):
        copies[2 * r].wait()
        copies[2 * r + 1].wait()
        encode_row(rows_ref[r], edge_ref, r * z.code)
    copies[4].wait()
    edge_ref[:, 2 * z.code :] = wind_codes(fold(level_half(z, wind_ref[...], 1 - p)))


def rest_kernel(z, par_ref, fields_ref, courant_ref, middle_ref, last_ref, own_ref):
    p = par_ref[0]
    keep = pl.multiple_of(p * z.half, z.half)
    give = pl.multiple_of((1 - p) * z.half, z.half)

    def field_row(row, start):
        return jnp.concatenate([fields_ref[f, row, pl.ds(start, z.half)] for f in range(2)], axis=0)

    def wind(k, row, upper):
        return level_half(z, courant_ref[k, row], upper)

    edge, inner = 2 * p, 2 * (1 - p)
    outer, near = 3 * p, 3 * (1 - p)
    for r in range(2):
        encode_row(field_row(edge + r, keep), own_ref, r * z.code)
        encode_row(field_row(inner + r, give), middle_ref, r * z.code)
    own_ref[:, 2 * z.code :] = wind_codes(fold(wind(1, outer, p)))
    lon = z.lon
    middle_ref[:, 2 * z.code : z.edge] = wind_codes(fold(wind(1, near, 1 - p)))
    middle_ref[:, z.edge :] = wind_codes(fold(wind(0, near, 1 - p)))
    last_ref[:, 2 * lon :] = wind_codes(fold(wind(0, outer, 1 - p)))
    for r in range(2):
        both = jnp.concatenate([wind(k, 1 + r, 1 - p) for k in range(2)], axis=0)
        last_ref[:, r * lon : (r + 1) * lon] = wind_codes(both)


def shifted(pieces, shift, lanes):
    turned = [pltpu.roll(v, (-shift) % LANE, 1) for v in pieces]
    if shift > 0:
        return [jnp.where(lanes < LANE - shift, a, b) for a, b in zip(turned[1:-1], turned[2:])]
    return [jnp.where(lanes < -shift, a, b) for a, b in zip(turned[:-2], turned[1:-1])]


def substep(z, count_rows, base, row_of, winds_ref, write):
    count = next(n for n in (4, 3, 2, 1) if z.lon % (n * LANE) == 0)
    width = count * LANE
    lanes = lax.broadcasted_iota(jnp.int32, (z.half, LANE), 1)

    def part(at):
        def piece(k):
            return pl.ds(at + k * LANE, LANE)

        def row(j, f):
            return [row_of(j, f, piece(k + 1)) for k in range(count)]

        def start(j, f):
            pieces = [row_of(j + 2, f, piece(k)) for k in range(count + 2)]
            return [shifted(pieces, s, lanes) for s in (-2, -1, 1, 2)]

        def lon_part(j, u, moved):
            out = []
            for k in range(count):
                m2, m1, p1, p2 = (m[k] for m in moved)
                east = 7.0 * (u[k] + p1) - (m1 + p2)
                west = 7.0 * (m1 + u[k]) - (m2 + p1)
                east = winds_ref[base + j, :, piece(k)] * east
                out.append(east - winds_ref[z.rows + base + j, :, piece(k)] * west)
            return out

        for f in range(2):
            rows = [row(j, f) for j in range(4)]
            sums = [[a + b for a, b in zip(rows[j], rows[j + 1])] for j in range(3)]
            flux = None
            moved = start(0, f)
            for j in range(count_rows + 1):
                later = start(j, f) if 0 < j < count_rows else None
                new = [
                    winds_ref[2 * z.rows + base + j, :, piece(k)] * (8.0 * sums[1][k] - (sums[0][k] + sums[2][k]))
                    for k in range(count)
                ]
                if j > 0:
                    u = rows[1]
                    change = lon_part(j - 1, u, moved)
                    for k in range(count):
                        write(j - 1, f, at, k, u[k] - change[k] - (new[k] - flux[k]))
                    moved = later
                flux = new
                if j < count_rows:
                    above = row(j + 4, f)
                    rows = rows[1:] + [above]
                    sums = sums[1:] + [[a + b for a, b in zip(rows[2], rows[3])]]

    for i in range(z.lon // width):
        part(i * width)


def filter_tables(lon):
    half = lon // 2
    points = np.arange(half)
    forward, back = [], []
    for parity in range(2):
        waves = np.arange(parity, KMAX, 2)
        angle = (points[:, None] * waves[None, :] % lon) * (2.0 * math.pi / lon)
        table = np.concatenate([np.cos(angle), np.sin(angle)], axis=1).astype(np.float32)
        high = table.astype(ml_dtypes.bfloat16)
        low = (table - high.astype(np.float32)).astype(ml_dtypes.bfloat16)
        forward.append(np.concatenate([high, low], axis=1))
        turned = np.concatenate([high.T, low.T], axis=0)
        back.append(np.concatenate(np.split(turned, half // (2 * KMAX), axis=1), axis=0))
    return np.stack(forward + back)


def split(values):
    high = values.astype(jnp.bfloat16)
    return high, (values - high.astype(jnp.float32)).astype(jnp.bfloat16)


def low_pass(z, rows, cuts, table_ref):
    half = z.lon // 2
    count = len(rows)
    tall = 2 * z.half
    total = count * tall
    flat = [row.reshape(tall, z.lon) for row in rows]
    folded = []
    for parity in range(2):
        parts = [
            row[:, :half] + row[:, half:] if parity == 0 else row[:, :half] - row[:, half:]
            for row in flat
        ]
        high, low = split(jnp.concatenate(parts, axis=0))
        both = jnp.concatenate([high, low], axis=0)
        got = jnp.dot(both, table_ref[parity], preferred_element_type=jnp.float32)
        wave = got[:total, :KMAX] + got[:total, KMAX:] + (got[total:, :KMAX] + got[total:, KMAX:])
        number = 2 * (lax.broadcasted_iota(jnp.int32, (tall, KMAX), 1) % (KMAX // 2)) + parity
        doubled = jnp.where(number == 0, 1.0, 2.0) * (1.0 / z.lon)
        weight = jnp.concatenate([jnp.where(number <= cut, doubled, 0.0) for cut in cuts], axis=0)
        high, low = split(wave * weight)
        both = jnp.concatenate(
            [jnp.concatenate([high, high], axis=1), jnp.concatenate([low, low], axis=1)], axis=0
        )
        got = []
        for at in range(0, half, 2 * KMAX):
            block = table_ref[2 + parity, at : at + 2 * KMAX]
            sums = jnp.dot(both, block, preferred_element_type=jnp.float32)
            got.append(sums[:total] + sums[total:])
        folded.append(jnp.concatenate(got, axis=1))
    left, right = folded[0] + folded[1], folded[0] - folded[1]
    smooth = jnp.concatenate([left, right], axis=1)
    return [smooth[i * tall : (i + 1) * tall].reshape(2, z.half, z.lon) for i in range(count)]


def filter_rows(z, cut_ref, first_row, start, table_ref, load, store):
    nyquist = z.lon // 2
    cuts = [cut_ref[first_row + start + r] for r in range(z.rows)]
    some = functools.reduce(jnp.logical_or, [cut < nyquist for cut in cuts])

    @pl.when(some)
    def _():
        smooth = low_pass(z, [load(start + r) for r in range(z.rows)], cuts, table_ref)
        for r in range(z.rows):

            @pl.when(cuts[r] < nyquist)
            def _():
                store(start + r, smooth[r])


def north_wind(z, in_ref):
    return unfold(wind_values(in_ref[:, 2 * z.code : z.edge]))


def faces(z, cx_ref, cy_ref, winds_ref):
    lanes = lax.broadcasted_iota(jnp.int32, (z.half, LANE), 1)
    for j in range(z.rows):
        pieces = [cx_ref[j, :, i : i + LANE] * (1.0 / 24.0) for i in range(0, z.pad, LANE)]
        for out, shift in ((j, 1), (z.rows + j, -1)):
            for k, moved in enumerate(shifted(pieces, shift, lanes)):
                winds_ref[out, :, k * LANE : (k + 1) * LANE] = pieces[k + 1] + moved
    for j in range(z.rows + 1):
        winds_ref[2 * z.rows + j] = (cy_ref[j] + cy_ref[j + 1]) * (1.0 / 24.0)


def writer(new_ref):
    def write(row, f, at, k, values):
        new_ref[row, f, :, pl.ds(at + (k + 1) * LANE, LANE)] = values

    return write


def wrap(z, new_ref, rows):
    for j in rows:
        new_ref[j, :, :, 0:LANE] = new_ref[j, :, :, z.lon : z.lon + LANE]
        new_ref[j, :, :, LANE + z.lon :] = new_ref[j, :, :, LANE : 2 * LANE]


def encode_new(z, new_ref, row, out_ref):
    for r in range(2):
        values = new_ref[row + r, :, :, LANE : LANE + z.lon]
        encode_row(values.reshape(2 * z.half, z.lon), out_ref, r * z.code)


def place_row(z, u_ref, row, in_ref, r):
    values = decode_row(in_ref, r * z.code, z.lon)
    put_padded(u_ref, (row + r,), values.reshape(2, z.half, z.lon), z.lon)


def own_kernel(
    z, par_ref, fields_ref, courant_ref, edge_ref, middle_ref, near_ref, far_ref,
    new_ref, winds_ref, code_ref, u_ref, cx_ref, cy_ref,
):
    p = par_ref[0]
    lon, half = z.lon, z.half
    keep = pl.multiple_of(p * half, half)
    for r in range(z.rows):
        own = jnp.stack([fields_ref[f, r, pl.ds(keep, half)] for f in range(2)])
        put_padded(u_ref, (z.rows * p + r + 2,), own, lon)
        put_padded(cx_ref, (r,), level_half(z, courant_ref[0, r], p), lon)
        cy_ref[r + 1] = level_half(z, courant_ref[1, r], p)
    for r in range(2):
        place_row(z, u_ref, 6 * (1 - p) + 2, edge_ref, r)
        place_row(z, u_ref, 4 - 2 * p + 2, middle_ref, r)
        place_row(z, u_ref, 10 * (1 - p), near_ref, r)
        place_row(z, u_ref, 10 * p, far_ref, r)
    cy_ref[5 * (1 - p)] = north_wind(z, middle_ref)
    cy_ref[5 * p] = north_wind(z, far_ref)
    faces(z, cx_ref, cy_ref, winds_ref)
    start = z.rows * p
    substep(z, z.rows, 0, lambda j, f, piece: u_ref[start + j, f, :, piece], winds_ref, writer(new_ref))
    encode_new(z, new_ref, 2 * p, code_ref)
    wrap(z, new_ref, range(z.rows))


def other_kernel(
    z, par_ref, courant_ref, edge_ref, middle_ref, last_ref, near_ref, u_ref,
    new_ref, winds_ref, code_ref, cx_ref, cy_ref,
):
    p = par_ref[0]
    lon, half = z.lon, z.half
    for r in range(2):
        both = wind_values(last_ref[:, r * lon : (r + 1) * lon])
        put_padded(cx_ref, (1 + r,), both[:half], lon)
        cy_ref[2 + r] = both[half:]
    easts = (last_ref[:, 2 * lon :], middle_ref[:, z.edge :])
    for east, row, in_ref in zip(easts, (3 * (1 - p), 3 * p), (edge_ref, middle_ref)):
        put_padded(cx_ref, (row,), unfold(wind_values(east)), lon)
        cy_ref[row + 1] = north_wind(z, in_ref)
    cy_ref[5 * p] = level_half(z, courant_ref[1, 3 * (1 - p)], p)
    cy_ref[5 * (1 - p)] = north_wind(z, near_ref)
    faces(z, cx_ref, cy_ref, winds_ref)
    outer = 2 * (1 - p)
    start = z.rows * (1 - p) + outer
    substep(z, 2, outer, lambda j, f, piece: u_ref[start + j, f, :, piece], winds_ref, writer(new_ref))
    encode_new(z, new_ref, 0, code_ref)
    wrap(z, new_ref, range(2))


def inner_kernel(
    z, par_ref, cut_ref, own_ref, other_ref, u_ref, own_winds_ref, other_winds_ref, table_ref, new_ref, inner_ref
):
    p = par_ref[0]
    own, other = z.rows * p, z.rows * (1 - p)
    for j in range(z.rows):
        new_ref[own + j] = own_ref[j]
    for j in range(2):
        new_ref[other + 2 * (1 - p) + j] = other_ref[j]
    start = other + 2 * p

    def write(row, f, at, k, values):
        writer(new_ref)(start + row, f, at, k, values)

    substep(z, 2, 2 * p, lambda j, f, piece: u_ref[start + j, f, :, piece], other_winds_ref, write)
    wrap(z, new_ref, (start, start + 1))

    def store(row, values):
        put_padded(new_ref, (row,), values, z.lon)

    for part in range(2):
        filter_rows(
            z, cut_ref, par_ref[1], part * z.rows, table_ref,
            lambda row: new_ref[row, :, :, LANE : LANE + z.lon], store,
        )
    for i, (low, base, winds_ref) in enumerate(
        ((2 * p, 2 * (1 - p), own_winds_ref), (2 * (1 - p), 2 * p, other_winds_ref))
    ):

        def keep(row, f, at, k, values):
            inner_ref[2 * i + row, f, :, pl.ds(at + k * LANE, LANE)] = values

        substep(z, 2, base, lambda j, f, piece: new_ref[low + j, f, :, piece], winds_ref, keep)


def outer_kernel(
    z, parts, par_ref, cut_ref, new_ref, inner_ref, own_winds_ref, other_winds_ref, near_ref, far_ref, table_ref, *refs
):
    out_refs, (u_ref, v_ref) = refs[: 2 * parts], refs[2 * parts :]
    p = par_ref[0]
    outer_half(
        z, parts, 1 - p, 2, par_ref, cut_ref, new_ref, inner_ref, other_winds_ref, near_ref, table_ref,
        out_refs[:parts], u_ref, v_ref,
    )
    outer_half(
        z, parts, p, 0, par_ref, cut_ref, new_ref, inner_ref, own_winds_ref, far_ref, table_ref,
        out_refs[parts:], u_ref, v_ref,
    )


def outer_half(
    z, parts, side, inner_at, par_ref, cut_ref, new_ref, inner_ref, winds_ref, halo_ref, table_ref,
    out_refs, u_ref, v_ref,
):
    lon = z.lon
    tall = 2 * z.half
    base = z.rows * side
    for r in range(2):
        place_row(z, u_ref, 4 * side, halo_ref, r)
    for r in range(4):
        u_ref[2 * (1 - side) + r] = new_ref[base + r]
    for r in range(2):
        v_ref[2 * (1 - side) + r] = inner_ref[inner_at + r]

    def write(row, f, at, k, values):
        v_ref[2 * side + row, f, :, pl.ds(at + k * LANE, LANE)] = values

    substep(z, 2, 2 * side, lambda j, f, piece: u_ref[j, f, :, piece], winds_ref, write)

    def store(row, values):
        v_ref[row] = values

    filter_rows(z, cut_ref, par_ref[1] + base, 0, table_ref, lambda row: v_ref[row], store)
    column = lon // parts
    for b in range(parts):
        at = pl.multiple_of(jnp.bitwise_xor(par_ref[2], b) * column, LANE)
        values = jnp.concatenate(
            [v_ref[r, :, :, pl.ds(at, column)].reshape(tall, column) for r in range(z.rows)], axis=1
        )
        encode_row(values, out_refs[b], 0)


def scale_kernel(at, *refs):
    for i, ref in enumerate(refs[:-1]):
        refs[-1][i] = decoder(ref[:, at : at + LANE])


def column_kernel(z, parts, far, par_ref, *refs):
    got, refs = refs[: 2 * parts], refs[2 * parts :]
    scales_ref, remap_ref, upward_ref, surface_ref, out_ref, geo_ref, x_ref, sums_ref, geo_sums_ref, sems = refs
    p, lev = par_ref[0], par_ref[2]
    count, column = sums_ref.shape[-2:]
    high, low = split(remap_ref[...])
    remap = jnp.concatenate([high, low, high], axis=1)
    both = jnp.concatenate([remap, upward_ref[...].astype(jnp.bfloat16)], axis=0)
    scales = [
        scales_ref[far.index(i)] if i in far else decoder(ref[:, z.rows * column :])
        for i, ref in enumerate(got)
    ]
    copies = []
    for row in range(z.rows):
        for i, ref in enumerate(got):
            side = 1 - p if i < parts else p
            s = jnp.bitwise_xor(lev, i % parts)
            codes = ref[:, row * column : (row + 1) * column].astype(jnp.int32).astype(jnp.float32)
            values = codes * tiled(scales[i], column)
            level = pl.multiple_of(s * z.levels + side * z.half, z.half)
            for f in range(2):
                x_ref[row, f, pl.ds(level, z.half)] = values[f * z.half : (f + 1) * z.half]
        for f in range(2):
            high, low = split(x_ref[row, f])
            stacked = jnp.concatenate([high, high, low], axis=0)
            result = jnp.dot(both if f else remap, stacked, preferred_element_type=jnp.float32)
            sums_ref[f, row] = result[:count]
            if f:
                geo_sums_ref[row] = surface_ref[row] + result[count:] * (count**-0.5)
        parts_out = [(sums_ref.at[f, row], out_ref.at[f, row]) for f in range(2)]
        parts_out.append((geo_sums_ref.at[row], geo_ref.at[row]))
        for k, (a, b) in enumerate(parts_out):
            copies.append(pltpu.make_async_copy(a, b, sems.at[3 * row + k]))
            copies[-1].start()
    for copy in copies:
        copy.wait()


def whole():
    return pl.BlockSpec(memory_space=pltpu.VMEM)


def scalars():
    return pl.BlockSpec(memory_space=pltpu.SMEM)


def far_memory():
    return pl.BlockSpec(memory_space=pltpu.HBM)


def params(limit=VMEM_LIMIT):
    return pltpu.CompilerParams(vmem_limit_bytes=limit)


def cost(flops=1000, data=1000):
    return pl.CostEstimate(flops=flops, bytes_accessed=data, transcendentals=0)


def shards(fields, courant, cutoffs, surface, remap_weights):
    _, rows, levels, lon = fields.shape
    z = Sizes(rows, levels, lon)
    lats, parts = lax.axis_size("lat"), lax.axis_size("lev")
    me = lax.axis_index("lat")
    parity = me % 2
    lev = lax.axis_index("lev")
    place = jnp.stack([parity, (me - parity) * rows, lev]).astype(jnp.int32)
    tall = 2 * z.half
    i16, f32 = jnp.int16, jnp.float32
    swap = [(i, i ^ 1) for i in range(lats)]
    rising = [(i, i + 2) for i in range(lats - 2)]
    near_pairs = [(i, j) if i % 2 else (j, i) for i, j in rising]
    far_pairs = [(j, i) if i % 2 else (i, j) for i, j in rising]

    def shape(*dims):
        return jax.ShapeDtypeStruct(dims, f32)

    def codes(*dims):
        return jax.ShapeDtypeStruct(dims, i16)

    edge = pl.pallas_call(
        functools.partial(edge_kernel, z),
        name="edge",
        in_specs=[far_memory(), far_memory()],
        out_specs=whole(),
        out_shape=codes(tall, z.edge),
        scratch_shapes=[
            pltpu.VMEM((2, tall, lon), f32),
            pltpu.VMEM((levels, lon), courant.dtype),
            pltpu.SemaphoreType.DMA((5,)),
        ],
        compiler_params=params(VMEM_MOST),
        cost_estimate=cost(),
    )(fields, courant)
    edge = lax.ppermute(edge, "lat", swap)
    middle, last, own = pl.pallas_call(
        functools.partial(rest_kernel, z),
        name="rest",
        in_specs=[scalars(), whole(), whole()],
        out_specs=[whole()] * 3,
        out_shape=[codes(tall, z.middle), codes(tall, z.last), codes(tall, z.edge)],
        compiler_params=params(),
        cost_estimate=cost(),
    )(place, fields, courant)
    near = lax.ppermute(own, "lat", near_pairs)
    middle = lax.ppermute(middle, "lat", swap)
    far = lax.ppermute(edge, "lat", far_pairs)
    last = lax.ppermute(last, "lat", swap)

    half_scratch = [
        pltpu.VMEM((z.rows, z.half, z.pad), f32),
        pltpu.VMEM((z.rows + 2, z.half, lon), f32),
    ]
    mine, own_winds, own_code, u = pl.pallas_call(
        functools.partial(own_kernel, z),
        name="own",
        in_specs=[scalars()] + [whole()] * 6,
        out_specs=[whole()] * 4,
        out_shape=[
            shape(z.rows, 2, z.half, z.pad),
            shape(3 * z.rows + 1, z.half, lon),
            codes(tall, 2 * z.code),
            shape(z.band + 4, 2, z.half, z.pad),
        ],
        scratch_shapes=half_scratch,
        compiler_params=params(),
        cost_estimate=cost(),
    )(place, fields, courant, edge, middle, near, far)
    near_code = lax.ppermute(own_code, "lat", near_pairs)
    other, other_winds, other_code = pl.pallas_call(
        functools.partial(other_kernel, z),
        name="other",
        in_specs=[scalars()] + [whole()] * 6,
        out_specs=[whole()] * 3,
        out_shape=[
            shape(2, 2, z.half, z.pad),
            shape(3 * z.rows + 1, z.half, lon),
            codes(tall, 2 * z.code),
        ],
        scratch_shapes=half_scratch,
        compiler_params=params(),
        cost_estimate=cost(),
    )(place, courant, edge, middle, last, near, u)
    far_code = lax.ppermute(other_code, "lat", far_pairs)

    tables = jnp.asarray(filter_tables(lon))
    new, inner = pl.pallas_call(
        functools.partial(inner_kernel, z),
        name="inner",
        in_specs=[scalars(), scalars()] + [whole()] * 6,
        out_specs=[whole()] * 2,
        out_shape=[shape(z.band, 2, z.half, z.pad), shape(z.rows, 2, z.half, lon)],
        compiler_params=params(),
        cost_estimate=cost(),
    )(place, cutoffs, mine, other, u, own_winds, other_winds, tables)

    column = lon // parts
    blocks = pl.pallas_call(
        functools.partial(outer_kernel, z, parts),
        name="outer",
        in_specs=[scalars(), scalars()] + [whole()] * 7,
        out_specs=[whole()] * (2 * parts),
        out_shape=[codes(tall, rows * column + LANE)] * (2 * parts),
        scratch_shapes=[
            pltpu.VMEM((6, 2, z.half, z.pad), f32),
            pltpu.VMEM((z.rows, 2, z.half, lon), f32),
        ],
        compiler_params=params(),
        cost_estimate=cost(),
    )(place, cutoffs, new, inner, own_winds, other_winds, near_code, far_code, tables)
    got = []
    for i, block in enumerate(blocks):
        b, across = i % parts, int(i < parts)
        pairs = [
            (k * parts + j, (k ^ across) * parts + (j ^ b)) for k in range(lats) for j in range(parts)
        ]
        got.append(lax.ppermute(block, ("lat", "lev"), pairs) if i != parts else block)
    far = [i for i in range(parts) if i % 2 == 0]
    scales = pl.pallas_call(
        functools.partial(scale_kernel, rows * column),
        name="scales",
        in_specs=[whole()] * len(far),
        out_specs=whole(),
        out_shape=shape(len(far), tall, LANE),
        compiler_params=params(),
        cost_estimate=cost(),
    )(*[got[i] for i in far])

    count = remap_weights.shape[0]
    upward = np.triu(np.ones((count, count), np.float32), 1) + 0.5 * np.eye(count, dtype=np.float32)
    upward = jnp.asarray(np.concatenate([upward, 0.0 * upward, upward], axis=1))
    surface = lax.dynamic_slice_in_dim(surface, lev * column, column, 1)
    remapped, geopotential = pl.pallas_call(
        functools.partial(column_kernel, z, parts, far),
        name="columns",
        in_specs=[scalars()] + [whole()] * (len(got) + 4),
        out_specs=[far_memory()] * 2,
        out_shape=[shape(2, rows, count, column), shape(rows, count, column)],
        scratch_shapes=[
            pltpu.VMEM((rows, 2, count, column), f32),
            pltpu.VMEM((2, rows, count, column), f32),
            pltpu.VMEM((rows, count, column), f32),
            pltpu.SemaphoreType.DMA((3 * rows,)),
        ],
        compiler_params=params(),
        cost_estimate=cost(),
    )(place, *got, scales, remap_weights, upward, surface[:, None, :])
    return remapped, geopotential


def with_halo(shard, width):
    size, length = lax.axis_size("lat"), shard.shape[1]
    up = [(i, (i + 1) % size) for i in range(size - 1)]
    down = [(j, i) for i, j in up]
    before = lax.ppermute(lax.slice_in_dim(shard, length - width, length, axis=1), "lat", up)
    after = lax.ppermute(lax.slice_in_dim(shard, 0, width, axis=1), "lat", down)
    return jnp.concatenate([before, shard, after], axis=1)


def plain_shards(fields, courant, cutoffs, surface, remap_weights):
    _, rows, _, lon = fields.shape
    exact = lax.Precision.HIGHEST
    cut = lax.dynamic_slice_in_dim(cutoffs, lax.axis_index("lat") * rows, rows)
    waves = np.arange(KMAX)
    angle = (np.arange(lon)[:, None] * waves[None, :] % lon) * (2.0 * math.pi / lon)
    table = jnp.asarray(np.concatenate([np.cos(angle), np.sin(angle)], axis=1).astype(np.float32))
    number = jnp.asarray(np.concatenate([waves, waves]).astype(np.int32))
    weight = jnp.where(number[None] <= cut[:, None], jnp.where(number == 0, 1.0, 2.0)[None] / lon, 0.0)
    flagged = cut < lon // 2

    def smooth(values):
        wave = jnp.einsum("frln,nk->frlk", values, table, precision=exact) * weight[None, :, None]
        low = jnp.einsum("frlk,nk->frln", wave, table, precision=exact)
        return jnp.where(flagged[None, :, None, None], low, values)

    winds = with_halo(courant, 1).astype(jnp.float32)
    east, north = winds[0, 1:-1], winds[1]
    face_x = (east + jnp.roll(east, -1, -1)) / 24.0
    face_y = (north[:-1] + north[1:]) / 24.0
    u = fields
    for _ in range(2):
        wide = with_halo(u, 2)
        pair = u + jnp.roll(u, -1, -1)
        fx = face_x * (8.0 * pair - (jnp.roll(pair, 1, -1) + jnp.roll(pair, -1, -1)))
        pair = wide[:, :-1] + wide[:, 1:]
        fy = face_y * (8.0 * pair[:, 1:-1] - (pair[:, :-2] + pair[:, 2:]))
        u = u - (fx - jnp.roll(fx, 1, -1)) - (fy[:, 1:] - fy[:, :-1])
        u = lax.cond(jnp.any(flagged), smooth, lambda values: values, u)
    columns = lax.all_to_all(u, "lev", split_axis=3, concat_axis=2, tiled=True)
    remapped = jnp.einsum("pk,fjkn->fjpn", remap_weights, columns, precision=exact)
    count = remap_weights.shape[0]
    upward = np.triu(np.ones((count, count), np.float32), 1) + 0.5 * np.eye(count, dtype=np.float32)
    upward = jnp.einsum("kl,jln->jkn", jnp.asarray(upward), columns[1], precision=exact)
    width = lon // lax.axis_size("lev")
    mine = lax.dynamic_slice_in_dim(surface, lax.axis_index("lev") * width, width, 1)
    return remapped, mine[:, None] + count**-0.5 * upward


def solution(mesh):
    def program(fields, courant, cutoffs, surface, remap_weights):
        lats, parts = mesh.shape["lat"], mesh.shape["lev"]
        rows, levels = fields.shape[1] // lats, fields.shape[2] // parts
        polar = fields.shape[1] // 8
        paired = (
            lats % 2 == 0
            and rows == 4
            and levels % 16 == 0
            and polar <= 2 * rows - 2
            and fields.shape[3] % (LANE * parts) == 0
            and parts & (parts - 1) == 0
            and fields.shape[3] % (4 * KMAX) == 0
        )
        return jax.shard_map(
            shards if paired else plain_shards,
            mesh=mesh,
            in_specs=(
                P(None, "lat", "lev", None),
                P(None, "lat", "lev", None),
                P(),
                P("lat", None),
                P(),
            ),
            out_specs=(P(None, "lat", None, "lev"), P("lat", None, "lev")),
            check_vma=False,
        )(fields, courant, cutoffs, surface, remap_weights)

    return program
```

profile of v0, /device:TPU:0, one launch (start us, length us, event | category | flops | bytes accessed | tf_op | source)
XLA Modules:
  0.0 55.8 jit_solution(4363553192077633375)
XLA Ops:
  0.6 0.0 copy-start
  0.6 1.9 %edge.1 = s16[16,7936]{1,0:T(8,128)(2,1)} custom-call(f32[2,4,16,3072]{3,2,1,0:T(8,128)} %fields_ref.5, bf16[2,4,16,3072]{3,2,1,0:T(8,128)(2,1)} %courant_ref.7), custom_call_target="tpu_custom_call" | custom-call | flops 1000 | bytes 1000 | tf_op jit(solution)/shard_map/edge/pallas_call | solution.py:541
  2.5 3.0 %collective-permute-start = (s16[16,7936]{1,0:T(8,128)(2,1)}, s16[16,7936]{1,0:T(8,128)(2,1)S(1)}, u32[]{:S(2)}, u32[]{:S(2)}) collective-permute-start(s16[16,7936]{1,0:T(8,128)(2,1)} %edge.1), channel_id=1, source_target_pairs={{0,4},{4,0},{8,12},{12,8},{16,20},{20,16},{24,28},{28,24},{1,5},{5... | collective-permute-start | bytes 761864 | tf_op jit(solution)/shard_map/ppermute | solution.py:555
  5.5 0.1 pad_add_fusion.par_ref
  5.6 0.0 copy-start.1
  5.6 1.4 %copy-done.1 = f32[2,4,16,3072]{3,2,1,0:T(8,128)S(1)} copy-done((f32[2,4,16,3072]{3,2,1,0:T(8,128)S(1)}, f32[2,4,16,3072]{3,2,1,0:T(8,128)}, u32[]{:S(2)}) %copy-start.1) | copy-done | bytes 1572888
  7.0 0.0 copy-start.3
  7.0 1.1 %copy-done.3 = bf16[2,4,16,3072]{3,2,1,0:T(8,128)(2,1)S(1)} copy-done((bf16[2,4,16,3072]{3,2,1,0:T(8,128)(2,1)S(1)}, bf16[2,4,16,3072]{3,2,1,0:T(8,128)(2,1)}, u32[]{:S(2)}) %copy-start.3) | copy-done | bytes 786456
  8.2 1.0 %rest.1 = (s16[16,9472]{1,0:T(8,128)(2,1)S(1)}, s16[16,7680]{1,0:T(8,128)(2,1)S(1)}, s16[16,7936]{1,0:T(8,128)(2,1)S(1)}) custom-call(s32[3]{0:T(128)S(1)} %pad_add_fusion.par_ref, f32[2,4,16,3072]{3,2,1,0:T(8,128)S(1)} %copy-done.1, bf16[2,4,16,3072]{3,2,1,0:T(8,128)(2,1)S(1)} %copy-done.3), custom_call_target="tpu_custom_call" | custom-call | flops 1000 | bytes 1000 | tf_op jit(solution)/shard_map/rest/pallas_call | solution.py:556
  9.1 0.1 collective-permute-start.1
  9.2 1.3 %collective-permute-start.2 = (s16[16,7936]{1,0:T(8,128)(2,1)S(1)}, s16[16,7936]{1,0:T(8,128)(2,1)S(1)}, u32[]{:S(2)}, u32[]{:S(2)}) collective-permute-start(s16[16,7936]{1,0:T(8,128)(2,1)S(1)} %get-tuple-element.23), channel_id=1, source_target_pairs={{8,0},{4,12},{16,8},{12,20},{24,16},{20,28},{9,1},{5,13},{17,9},{1... | collective-permute-start | bytes 761864 | tf_op jit(solution)/shard_map/ppermute | solution.py:565
  10.5 1.9 %collective-permute-done.edge_ref = s16[16,7936]{1,0:T(8,128)(2,1)S(1)} collective-permute-done((s16[16,7936]{1,0:T(8,128)(2,1)}, s16[16,7936]{1,0:T(8,128)(2,1)S(1)}, u32[]{:S(2)}, u32[]{:S(2)}) %collective-permute-start) | collective-permute-done | bytes 253984 | tf_op jit(solution)/shard_map/ppermute | solution.py:555
  12.4 3.9 %collective-permute-start.3 = (s16[16,7936]{1,0:T(8,128)(2,1)S(1)}, s16[16,7936]{1,0:T(8,128)(2,1)S(1)}, u32[]{:S(2)}, u32[]{:S(2)}) collective-permute-start(s16[16,7936]{1,0:T(8,128)(2,1)S(1)} %collective-permute-done.edge_ref), channel_id=1, source_target_pairs={{0,8},{12,4},{8,16},{20,12},{16,24},{28,20},{1,9},{13,5},{9,17},{2... | collective-permute-start | bytes 761864 | tf_op jit(solution)/shard_map/ppermute | solution.py:567
  16.3 0.0 copy-start.4
  16.4 0.1 collective-permute-start.4
  16.4 2.3 %collective-permute-done.2.near_ref = s16[16,7936]{1,0:T(8,128)(2,1)S(1)} collective-permute-done((s16[16,7936]{1,0:T(8,128)(2,1)S(1)}, s16[16,7936]{1,0:T(8,128)(2,1)S(1)}, u32[]{:S(2)}, u32[]{:S(2)}) %collective-permute-start.2) | collective-permute-done | bytes 253984 | tf_op jit(solution)/shard_map/ppermute | solution.py:565
  18.8 0.5 collective-permute-done.1.middle_ref
  19.3 0.8 %collective-permute-done.3.far_ref = s16[16,7936]{1,0:T(8,128)(2,1)S(1)} collective-permute-done((s16[16,7936]{1,0:T(8,128)(2,1)S(1)}, s16[16,7936]{1,0:T(8,128)(2,1)S(1)}, u32[]{:S(2)}, u32[]{:S(2)}) %collective-permute-start.3) | collective-permute-done | bytes 253984 | tf_op jit(solution)/shard_map/ppermute | solution.py:567
  20.1 2.2 %own.1 = (f32[4,2,8,3328]{3,2,1,0:T(8,128)S(1)}, f32[13,8,3072]{2,1,0:T(8,128)S(1)}, s16[16,6400]{1,0:T(8,128)(2,1)S(1)}, f32[12,2,8,3328]{3,2,1,0:T(8,128)S(1)}) custom-call(s32[3]{0:T(128)S(1)} %pad_add_fusion.par_ref, f32[2,4,16,3072]{3,2,1,0:T(8,128)S(1)} %copy-done.1, bf16[2,4,16,3072]{3,2,1,0:T(8,128)(2,1)S(1)} %copy-done.3, ...), custom_call_target="tpu_custom_call" | custom-call | flops 1000 | bytes 1000 | tf_op jit(solution)/shard_map/own/pallas_call | solution.py:574
  22.4 1.3 %collective-permute-done.4.last_ref = s16[16,7680]{1,0:T(8,128)(2,1)S(1)} collective-permute-done((s16[16,7680]{1,0:T(8,128)(2,1)S(1)}, s16[16,7680]{1,0:T(8,128)(2,1)S(1)}, u32[]{:S(2)}, u32[]{:S(2)}) %collective-permute-start.4) | collective-permute-done | bytes 245792 | tf_op jit(solution)/shard_map/ppermute | solution.py:568
  23.7 0.0 copy-done.4
  23.7 1.5 %other.1 = (f32[2,2,8,3328]{3,2,1,0:T(8,128)S(1)}, f32[13,8,3072]{2,1,0:T(8,128)S(1)}, s16[16,6400]{1,0:T(8,128)(2,1)S(1)}) custom-call(s32[3]{0:T(128)S(1)} %pad_add_fusion.par_ref, bf16[2,4,16,3072]{3,2,1,0:T(8,128)(2,1)S(1)} %copy-done.4, s16[16,7936]{1,0:T(8,128)(2,1)S(1)} %collective-permute-done.edge_ref, ...), custom_call_target="tpu_custom_call" | custom-call | flops 1000 | bytes 1000 | tf_op jit(solution)/shard_map/other/pallas_call | solution.py:590
  25.2 3.7 %collective-permute-start.6 = (s16[16,6400]{1,0:T(8,128)(2,1)S(1)}, s16[16,6400]{1,0:T(8,128)(2,1)S(1)}, u32[]{:S(2)}, u32[]{:S(2)}) collective-permute-start(s16[16,6400]{1,0:T(8,128)(2,1)S(1)} %get-tuple-element.33), channel_id=1, source_target_pairs={{0,8},{12,4},{8,16},{20,12},{16,24},{28,20},{1,9},{13,5},{9,17},{2... | collective-permute-start | bytes 614408 | tf_op jit(solution)/shard_map/ppermute | solution.py:604
  28.9 1.3 %collective-permute-start.5 = (s16[16,6400]{1,0:T(8,128)(2,1)S(1)}, s16[16,6400]{1,0:T(8,128)(2,1)S(1)}, u32[]{:S(2)}, u32[]{:S(2)}) collective-permute-start(s16[16,6400]{1,0:T(8,128)(2,1)S(1)} %get-tuple-element.32), channel_id=1, source_target_pairs={{8,0},{4,12},{16,8},{12,20},{24,16},{20,28},{9,1},{5,13},{17,9},{1... | collective-permute-start | bytes 614408 | tf_op jit(solution)/shard_map/ppermute | solution.py:589
  30.2 0.0 copy-done.2
  30.2 0.0 copy-done.7
  30.2 3.3 %inner.1 = (f32[8,2,8,3328]{3,2,1,0:T(8,128)S(1)}, f32[4,2,8,3072]{3,2,1,0:T(8,128)S(1)}) custom-call(s32[3]{0:T(128)S(1)} %pad_add_fusion.par_ref, s32[32]{0:T(128)S(1)} %copy-done.7, f32[4,2,8,3328]{3,2,1,0:T(8,128)S(1)} %get-tuple-element.24.own_ref, f32[2,2,8,3328]{3,2,1,0:T(8,128)S(1)} %get-tuple-element.27.other_ref, ...), custom_call_target="tpu_custom_call" | custom-call | flops 1000 | bytes 1000 | tf_op jit(solution)/shard_map/inner/pallas_call | solution.py:607
  33.5 0.0 collective-permute-done.6.far_ref
  33.5 3.1 %collective-permute-done.5.near_ref = s16[16,6400]{1,0:T(8,128)(2,1)S(1)} collective-permute-done((s16[16,6400]{1,0:T(8,128)(2,1)S(1)}, s16[16,6400]{1,0:T(8,128)(2,1)S(1)}, u32[]{:S(2)}, u32[]{:S(2)}) %collective-permute-start.5) | collective-permute-done | bytes 204832 | tf_op jit(solution)/shard_map/ppermute | solution.py:589
  36.6 3.4 %outer.1 = (s16[16,3200]{1,0:T(8,128)(2,1)S(1)}, s16[16,3200]{1,0:T(8,128)(2,1)S(1)}, s16[16,3200]{1,0:T(8,128)(2,1)S(1)}, s16[16,3200]{1,0:T(8,128)(2,1)S(1)}, ...) custom-call(s32[3]{0:T(128)S(1)} %pad_add_fusion.par_ref, ...), custom_call_target="tpu_custom_call" | custom-call | flops 1000 | bytes 1000 | tf_op jit(solution)/shard_map/outer/pallas_call | solution.py:618
  40.0 0.2 collective-permute-start.7
  40.2 2.9 %collective-permute-start.9 = (s16[16,3200]{1,0:T(8,128)(2,1)S(1)}, s16[16,3200]{1,0:T(8,128)(2,1)S(1)}, u32[]{:S(2)}, u32[]{:S(2)}) collective-permute-start(s16[16,3200]{1,0:T(8,128)(2,1)S(1)} %get-tuple-element.36), channel_id=1, source_target_pairs={{0,6},{1,7},{2,4},{3,5},{4,2},{5,3},{6,0},{7,1},{8,14},{9,15},{10,... | collective-permute-start | bytes 307208 | tf_op jit(solution)/shard_map/ppermute | solution.py:637
  43.0 0.0 collective-permute-start.10
  43.0 0.2 collective-permute-start.11
  43.2 1.5 %collective-permute-start.12 = (s16[16,3200]{1,0:T(8,128)(2,1)S(1)}, s16[16,3200]{1,0:T(8,128)(2,1)S(1)}, u32[]{:S(2)}, u32[]{:S(2)}) collective-permute-start(s16[16,3200]{1,0:T(8,128)(2,1)S(1)} %get-tuple-element.40), channel_id=1, source_target_pairs={{0,2},{1,3},{2,0},{3,1},{4,6},{5,7},{6,4},{7,5},{8,10},{9,11},{10,... | collective-permute-start | bytes 307208 | tf_op jit(solution)/shard_map/ppermute | solution.py:637
  44.7 0.0 collective-permute-done.7.refs_0_
  44.7 0.2 collective-permute-start.13
  44.9 1.9 %collective-permute-done.9.refs_1_.refs_2_ = s16[16,3200]{1,0:T(8,128)(2,1)S(1)} collective-permute-done((s16[16,3200]{1,0:T(8,128)(2,1)S(1)}, s16[16,3200]{1,0:T(8,128)(2,1)S(1)}, u32[]{:S(2)}, u32[]{:S(2)}) %collective-permute-start.9) | collective-permute-done | bytes 102432 | tf_op jit(solution)/shard_map/ppermute | solution.py:637
  46.8 0.0 collective-permute-start.8
  46.9 0.0 copy-done
  46.9 2.2 %collective-permute-done.10.refs_3_ = s16[16,3200]{1,0:T(8,128)(2,1)S(1)} collective-permute-done((s16[16,3200]{1,0:T(8,128)(2,1)S(1)}, s16[16,3200]{1,0:T(8,128)(2,1)S(1)}, u32[]{:S(2)}, u32[]{:S(2)}) %collective-permute-start.10) | collective-permute-done | bytes 102432 | tf_op jit(solution)/shard_map/ppermute | solution.py:637
  49.1 0.0 collective-permute-done.11.refs_5_
  49.1 2.1 %collective-permute-done.12.refs_6_ = s16[16,3200]{1,0:T(8,128)(2,1)S(1)} collective-permute-done((s16[16,3200]{1,0:T(8,128)(2,1)S(1)}, s16[16,3200]{1,0:T(8,128)(2,1)S(1)}, u32[]{:S(2)}, u32[]{:S(2)}) %collective-permute-start.12) | collective-permute-done | bytes 102432 | tf_op jit(solution)/shard_map/ppermute | solution.py:637
  51.2 2.1 %collective-permute-done.13.refs_7_ = s16[16,3200]{1,0:T(8,128)(2,1)S(1)} collective-permute-done((s16[16,3200]{1,0:T(8,128)(2,1)S(1)}, s16[16,3200]{1,0:T(8,128)(2,1)S(1)}, u32[]{:S(2)}, u32[]{:S(2)}) %collective-permute-start.13) | collective-permute-done | bytes 102432 | tf_op jit(solution)/shard_map/ppermute | solution.py:637
  53.3 0.0 collective-permute-done.8.refs_1_
  53.3 0.0 copy-done.5
  53.3 0.0 copy-done.6
  53.3 2.5 %columns.1 = (f32[2,4,64,768]{3,2,1,0:T(8,128)}, f32[4,64,768]{2,1,0:T(8,128)}) custom-call(s32[3]{0:T(128)S(1)} %pad_add_fusion.par_ref, s16[16,3200]{1,0:T(8,128)(2,1)S(1)} %collective-permute-done.7.refs_0_, s16[16,3200]{1,0:T(8,128)(2,1)S(1)} %collective-permute-done.8.refs_1_, s16[16,3200]{1,0:T(8,128)(2,1)S(1)} %collective-permute-done.9.refs_1_.refs_2_, ...), custom_call_target="tpu_custom_call" | custom-call | flops 1000 | bytes 1000 | tf_op jit(solution)/shard_map/columns/pallas_call | solution.py:653
  (7 shorter events, 0.0 us)
Async XLA Ops:
  0.6 46.3 %copy-start = (f32[4,3072]{1,0:T(4,128)S(1)}, f32[4,3072]{1,0:T(4,128)}, u32[]{:S(2)}) copy-start(f32[4,3072]{1,0:T(4,128)} %param.10) | copy-start | bytes 147460
  2.5 9.9 %collective-permute-start = (s16[16,7936]{1,0:T(8,128)(2,1)}, s16[16,7936]{1,0:T(8,128)(2,1)S(1)}, u32[]{:S(2)}, u32[]{:S(2)}) collective-permute-start(s16[16,7936]{1,0:T(8,128)(2,1)} %edge.1), channel_id=1, source_target_pairs={{0,4},{4,0},{8,12},{12,8},{16,20},{20,16},{24,28},{28,24},{1,5},{5... | collective-permute-start | bytes 761864 | tf_op jit(solution)/shard_map/ppermute | solution.py:555
  5.6 1.4 %copy-start.1 = (f32[2,4,16,3072]{3,2,1,0:T(8,128)S(1)}, f32[2,4,16,3072]{3,2,1,0:T(8,128)}, u32[]{:S(2)}) copy-start(f32[2,4,16,3072]{3,2,1,0:T(8,128)} %fields_ref.5) | copy-start | bytes 4718596
  7.0 1.1 %copy-start.3 = (bf16[2,4,16,3072]{3,2,1,0:T(8,128)(2,1)S(1)}, bf16[2,4,16,3072]{3,2,1,0:T(8,128)(2,1)}, u32[]{:S(2)}) copy-start(bf16[2,4,16,3072]{3,2,1,0:T(8,128)(2,1)} %courant_ref.7) | copy-start | bytes 2359300
  9.1 10.2 %collective-permute-start.1 = (s16[16,9472]{1,0:T(8,128)(2,1)S(1)}, s16[16,9472]{1,0:T(8,128)(2,1)S(1)}, u32[]{:S(2)}, u32[]{:S(2)}) collective-permute-start(s16[16,9472]{1,0:T(8,128)(2,1)S(1)} %get-tuple-element.22), channel_id=1, source_target_pairs={{0,4},{4,0},{8,12},{12,8},{16,20},{20,16},{24,28},{28,24},{1,5},{5... | collective-permute-start | bytes 909320 | tf_op jit(solution)/shard_map/ppermute | solution.py:566
  9.2 9.5 %collective-permute-start.2 = (s16[16,7936]{1,0:T(8,128)(2,1)S(1)}, s16[16,7936]{1,0:T(8,128)(2,1)S(1)}, u32[]{:S(2)}, u32[]{:S(2)}) collective-permute-start(s16[16,7936]{1,0:T(8,128)(2,1)S(1)} %get-tuple-element.23), channel_id=1, source_target_pairs={{8,0},{4,12},{16,8},{12,20},{24,16},{20,28},{9,1},{5,13},{17,9},{1... | collective-permute-start | bytes 761864 | tf_op jit(solution)/shard_map/ppermute | solution.py:565
  12.4 7.7 %collective-permute-start.3 = (s16[16,7936]{1,0:T(8,128)(2,1)S(1)}, s16[16,7936]{1,0:T(8,128)(2,1)S(1)}, u32[]{:S(2)}, u32[]{:S(2)}) collective-permute-start(s16[16,7936]{1,0:T(8,128)(2,1)S(1)} %collective-permute-done.edge_ref), channel_id=1, source_target_pairs={{0,8},{12,4},{8,16},{20,12},{16,24},{28,20},{1,9},{13,5},{9,17},{2... | collective-permute-start | bytes 761864 | tf_op jit(solution)/shard_map/ppermute | solution.py:567
  16.3 7.3 %copy-start.4 = (bf16[2,4,16,3072]{3,2,1,0:T(8,128)(2,1)S(1)}, bf16[2,4,16,3072]{3,2,1,0:T(8,128)(2,1)}, u32[]{:S(2)}) copy-start(bf16[2,4,16,3072]{3,2,1,0:T(8,128)(2,1)} %courant_ref.7) | copy-start | bytes 2359300
  16.4 7.3 %collective-permute-start.4 = (s16[16,7680]{1,0:T(8,128)(2,1)S(1)}, s16[16,7680]{1,0:T(8,128)(2,1)S(1)}, u32[]{:S(2)}, u32[]{:S(2)}) collective-permute-start(s16[16,7680]{1,0:T(8,128)(2,1)S(1)} %get-tuple-element.25), channel_id=1, source_target_pairs={{0,4},{4,0},{8,12},{12,8},{16,20},{20,16},{24,28},{28,24},{1,5},{5... | collective-permute-start | bytes 737288 | tf_op jit(solution)/shard_map/ppermute | solution.py:568
  23.7 6.6 %copy-start.2 = (bf16[4,1536,256]{2,1,0:T(8,128)(2,1)S(1)}, bf16[4,1536,256]{2,1,0:T(8,128)(2,1)}, u32[]{:S(2)}) copy-start(bf16[4,1536,256]{2,1,0:T(8,128)(2,1)} %constant.33.clone.table_ref) | copy-start | bytes 9437188
  23.7 6.6 %copy-start.7 = (s32[32]{0:T(128)S(1)}, s32[32]{0:T(128)}, u32[]{:S(2)}) copy-start(s32[32]{0:T(128)} %cut_ref.3) | copy-start | bytes 388
  25.2 8.3 %collective-permute-start.6 = (s16[16,6400]{1,0:T(8,128)(2,1)S(1)}, s16[16,6400]{1,0:T(8,128)(2,1)S(1)}, u32[]{:S(2)}, u32[]{:S(2)}) collective-permute-start(s16[16,6400]{1,0:T(8,128)(2,1)S(1)} %get-tuple-element.33), channel_id=1, source_target_pairs={{0,8},{12,4},{8,16},{20,12},{16,24},{28,20},{1,9},{13,5},{9,17},{2... | collective-permute-start | bytes 614408 | tf_op jit(solution)/shard_map/ppermute | solution.py:604
  28.9 7.7 %collective-permute-start.5 = (s16[16,6400]{1,0:T(8,128)(2,1)S(1)}, s16[16,6400]{1,0:T(8,128)(2,1)S(1)}, u32[]{:S(2)}, u32[]{:S(2)}) collective-permute-start(s16[16,6400]{1,0:T(8,128)(2,1)S(1)} %get-tuple-element.32), channel_id=1, source_target_pairs={{8,0},{4,12},{16,8},{12,20},{24,16},{20,28},{9,1},{5,13},{17,9},{1... | collective-permute-start | bytes 614408 | tf_op jit(solution)/shard_map/ppermute | solution.py:589
  36.6 16.7 %copy-start.5 = (f32[64,192]{1,0:T(8,128)S(1)}, f32[64,192]{1,0:T(8,128)}, u32[]{:S(2)}) copy-start(f32[64,192]{1,0:T(8,128)} %constant.34.clone.refs_10_) | copy-start | bytes 147460
  36.6 16.7 %copy-start.6 = (f32[64,64]{1,0:T(8,128)S(1)}, f32[64,64]{1,0:T(8,128)}, u32[]{:S(2)}) copy-start(f32[64,64]{1,0:T(8,128)} %refs_9_.1) | copy-start | bytes 49156
  40.0 4.7 %collective-permute-start.7 = (s16[16,3200]{1,0:T(8,128)(2,1)S(1)}, s16[16,3200]{1,0:T(8,128)(2,1)S(1)}, u32[]{:S(2)}, u32[]{:S(2)}) collective-permute-start(s16[16,3200]{1,0:T(8,128)(2,1)S(1)} %get-tuple-element.34), channel_id=1, source_target_pairs={{0,4},{1,5},{2,6},{3,7},{4,0},{5,1},{6,2},{7,3},{8,12},{9,13},{10,... | collective-permute-start | bytes 307208 | tf_op jit(solution)/shard_map/ppermute | solution.py:637
  40.2 6.7 %collective-permute-start.9 = (s16[16,3200]{1,0:T(8,128)(2,1)S(1)}, s16[16,3200]{1,0:T(8,128)(2,1)S(1)}, u32[]{:S(2)}, u32[]{:S(2)}) collective-permute-start(s16[16,3200]{1,0:T(8,128)(2,1)S(1)} %get-tuple-element.36), channel_id=1, source_target_pairs={{0,6},{1,7},{2,4},{3,5},{4,2},{5,3},{6,0},{7,1},{8,14},{9,15},{10,... | collective-permute-start | bytes 307208 | tf_op jit(solution)/shard_map/ppermute | solution.py:637
  43.0 6.0 %collective-permute-start.10 = (s16[16,3200]{1,0:T(8,128)(2,1)S(1)}, s16[16,3200]{1,0:T(8,128)(2,1)S(1)}, u32[]{:S(2)}, u32[]{:S(2)}) collective-permute-start(s16[16,3200]{1,0:T(8,128)(2,1)S(1)} %get-tuple-element.37), channel_id=1, source_target_pairs={{0,7},{1,6},{2,5},{3,4},{4,3},{5,2},{6,1},{7,0},{8,15},{9,14},{10,... | collective-permute-start | bytes 307208 | tf_op jit(solution)/shard_map/ppermute | solution.py:637
  43.0 6.0 %collective-permute-start.11 = (s16[16,3200]{1,0:T(8,128)(2,1)S(1)}, s16[16,3200]{1,0:T(8,128)(2,1)S(1)}, u32[]{:S(2)}, u32[]{:S(2)}) collective-permute-start(s16[16,3200]{1,0:T(8,128)(2,1)S(1)} %get-tuple-element.39), channel_id=1, source_target_pairs={{0,1},{1,0},{2,3},{3,2},{4,5},{5,4},{6,7},{7,6},{8,9},{9,8},{10,11... | collective-permute-start | bytes 307208 | tf_op jit(solution)/shard_map/ppermute | solution.py:637
  43.2 8.0 %collective-permute-start.12 = (s16[16,3200]{1,0:T(8,128)(2,1)S(1)}, s16[16,3200]{1,0:T(8,128)(2,1)S(1)}, u32[]{:S(2)}, u32[]{:S(2)}) collective-permute-start(s16[16,3200]{1,0:T(8,128)(2,1)S(1)} %get-tuple-element.40), channel_id=1, source_target_pairs={{0,2},{1,3},{2,0},{3,1},{4,6},{5,7},{6,4},{7,5},{8,10},{9,11},{10,... | collective-permute-start | bytes 307208 | tf_op jit(solution)/shard_map/ppermute | solution.py:637
  44.7 8.6 %collective-permute-start.13 = (s16[16,3200]{1,0:T(8,128)(2,1)S(1)}, s16[16,3200]{1,0:T(8,128)(2,1)S(1)}, u32[]{:S(2)}, u32[]{:S(2)}) collective-permute-start(s16[16,3200]{1,0:T(8,128)(2,1)S(1)} %get-tuple-element.41), channel_id=1, source_target_pairs={{0,3},{1,2},{2,1},{3,0},{4,7},{5,6},{6,5},{7,4},{8,11},{9,10},{10,... | collective-permute-start | bytes 307208 | tf_op jit(solution)/shard_map/ppermute | solution.py:637
  46.8 6.5 %collective-permute-start.8 = (s16[16,3200]{1,0:T(8,128)(2,1)S(1)}, s16[16,3200]{1,0:T(8,128)(2,1)S(1)}, u32[]{:S(2)}, u32[]{:S(2)}) collective-permute-start(s16[16,3200]{1,0:T(8,128)(2,1)S(1)} %get-tuple-element.35), channel_id=1, source_target_pairs={{0,5},{1,4},{2,7},{3,6},{4,1},{5,0},{6,3},{7,2},{8,13},{9,12},{10,... | collective-permute-start | bytes 307208 | tf_op jit(solution)/shard_map/ppermute | solution.py:637
where the time goes:
time: 56.1 us; the launch traced here: 55.8 us
  starting transfers between devices  18.4 us (33%)
  waiting for transfers between devices  18.2 us (32%)
  Pallas kernels  15.8 us (28%)
  local copies, waits for them, and re-layouts  2.59 us (5%)
  between operations  0.78 us (1%)
    ppermute x7, waiting for transfers between devices, shards(): lax.ppermute(block, ('lat', 'lev'), pairs)  8.31 us
    ppermute x7, starting transfers between devices, shards(): lax.ppermute(block, ('lat', 'lev'), pairs)  4.95 us
    ppermute x1, starting transfers between devices, shards(): far = lax.ppermute(edge, 'lat', far_pairs)  3.94 us
    ppermute x1, starting transfers between devices, shards(): far_code = lax.ppermute(other_code, 'lat', far_pairs)  3.74 us
    pallas_call x1, Pallas kernels, shards(): pl.pallas_call(functools.partial(outer_kernel, z, parts), name='outer', i...  3.4 us
    pallas_call x1, Pallas kernels, shards(): pl.pallas_call(functools.partial(inner_kernel, z), name='inner', in_specs...  3.26 us
    ppermute x1, waiting for transfers between devices, shards(): near_code = lax.ppermute(own_code, 'lat', near_pairs)  3.05 us
    ppermute x1, starting transfers between devices, shards(): edge = lax.ppermute(edge, 'lat', swap)  3 us
  transfers between devices with their start and end apart: 14, of which 10 were waited for; matrix products, arithmetic and copies ran while one was open for 0% of the time, Pallas kernels for 12%

commit v1 on v0

--- a/solution.py
+++ b/solution.py
@@ -349,8 +349,8 @@
 
 
 def other_kernel(
-    z, par_ref, courant_ref, edge_ref, middle_ref, last_ref, near_ref, u_ref,
-    new_ref, winds_ref, code_ref, cx_ref, cy_ref,
+    z, par_ref, courant_ref, edge_ref, middle_ref, last_ref, near_ref, u_ref, own_code_ref,
+    new_ref, winds_ref, one_ref, two_ref, cx_ref, cy_ref,
 ):
     p = par_ref[0]
     lon, half = z.lon, z.half
@@ -368,7 +368,14 @@
     outer = 2 * (1 - p)
     start = z.rows * (1 - p) + outer
     substep(z, 2, outer, lambda j, f, piece: u_ref[start + j, f, :, piece], winds_ref, writer(new_ref))
-    encode_new(z, new_ref, 0, code_ref)
+
+    def put_codes(own_ref, other_ref):
+        own_ref[...] = own_code_ref[...]
+        encode_new(z, new_ref, 0, other_ref)
+
+    swapped = p + par_ref[3] == 1
+    pl.when(swapped)(lambda: put_codes(one_ref, two_ref))
+    pl.when(jnp.logical_not(swapped))(lambda: put_codes(two_ref, one_ref))
     wrap(z, new_ref, range(2))
 
 
@@ -408,29 +415,36 @@
 
 
 def outer_kernel(
-    z, parts, par_ref, cut_ref, new_ref, inner_ref, own_winds_ref, other_winds_ref, near_ref, far_ref, table_ref, *refs
+    z, parts, par_ref, cut_ref, new_ref, inner_ref, own_winds_ref, other_winds_ref, one_ref, two_ref, table_ref, *refs
 ):
-    out_refs, (u_ref, v_ref) = refs[: 2 * parts], refs[2 * parts :]
+    out_refs, scratch = refs[: 2 * parts], refs[2 * parts :]
     p = par_ref[0]
+    halos = (one_ref, two_ref)
     outer_half(
-        z, parts, 1 - p, 2, par_ref, cut_ref, new_ref, inner_ref, other_winds_ref, near_ref, table_ref,
-        out_refs[:parts], u_ref, v_ref,
+        z, parts, 1 - p, 2, par_ref, cut_ref, new_ref, inner_ref, other_winds_ref, halos, table_ref,
+        out_refs[:parts], *scratch,
     )
     outer_half(
-        z, parts, p, 0, par_ref, cut_ref, new_ref, inner_ref, own_winds_ref, far_ref, table_ref,
-        out_refs[parts:], u_ref, v_ref,
+        z, parts, p, 0, par_ref, cut_ref, new_ref, inner_ref, own_winds_ref, halos, table_ref,
+        out_refs[parts:], *scratch,
     )
 
 
 def outer_half(
-    z, parts, side, inner_at, par_ref, cut_ref, new_ref, inner_ref, winds_ref, halo_ref, table_ref,
+    z, parts, side, inner_at, par_ref, cut_ref, new_ref, inner_ref, winds_ref, halos, table_ref,
     out_refs, u_ref, v_ref,
 ):
     lon = z.lon
     tall = 2 * z.half
     base = z.rows * side
-    for r in range(2):
-        place_row(z, u_ref, 4 * side, halo_ref, r)
+
+    def halo(in_ref):
+        for r in range(2):
+            place_row(z, u_ref, 4 * side, in_ref, r)
+
+    first_swap = side + par_ref[3] == 1
+    pl.when(first_swap)(lambda: halo(halos[0]))
+    pl.when(jnp.logical_not(first_swap))(lambda: halo(halos[1]))
     for r in range(4):
         u_ref[2 * (1 - side) + r] = new_ref[base + r]
     for r in range(2):
@@ -524,13 +538,17 @@
     me = lax.axis_index("lat")
     parity = me % 2
     lev = lax.axis_index("lev")
-    place = jnp.stack([parity, (me - parity) * rows, lev]).astype(jnp.int32)
+    place = jnp.stack([parity, (me - parity) * rows, lev, (me // 2) % 2]).astype(jnp.int32)
     tall = 2 * z.half
     i16, f32 = jnp.int16, jnp.float32
     swap = [(i, i ^ 1) for i in range(lats)]
     rising = [(i, i + 2) for i in range(lats - 2)]
     near_pairs = [(i, j) if i % 2 else (j, i) for i, j in rising]
     far_pairs = [(j, i) if i % 2 else (i, j) for i, j in rising]
+
+    ones, twos = [
+        [pair for i, j in rising if i // 2 % 2 == odd for pair in ((i, j), (j, i))] for odd in range(2)
+    ]
 
     def shape(*dims):
         return jax.ShapeDtypeStruct(dims, f32)
@@ -586,22 +604,23 @@
         compiler_params=params(),
         cost_estimate=cost(),
     )(place, fields, courant, edge, middle, near, far)
-    near_code = lax.ppermute(own_code, "lat", near_pairs)
-    other, other_winds, other_code = pl.pallas_call(
+    other, other_winds, one, two = pl.pallas_call(
         functools.partial(other_kernel, z),
         name="other",
-        in_specs=[scalars()] + [whole()] * 6,
-        out_specs=[whole()] * 3,
+        in_specs=[scalars()] + [whole()] * 7,
+        out_specs=[whole()] * 4,
         out_shape=[
             shape(2, 2, z.half, z.pad),
             shape(3 * z.rows + 1, z.half, lon),
+            codes(tall, 2 * z.code),
             codes(tall, 2 * z.code),
         ],
         scratch_shapes=half_scratch,
         compiler_params=params(),
         cost_estimate=cost(),
-    )(place, courant, edge, middle, last, near, u)
-    far_code = lax.ppermute(other_code, "lat", far_pairs)
+    )(place, courant, edge, middle, last, near, u, own_code)
+    one = lax.ppermute(one, "lat", ones)
+    two = lax.ppermute(two, "lat", twos)
 
     tables = jnp.asarray(filter_tables(lon))
     new, inner = pl.pallas_call(
@@ -627,7 +646,7 @@
         ],
         compiler_params=params(),
         cost_estimate=cost(),
-    )(place, cutoffs, new, inner, own_winds, other_winds, near_code, far_code, tables)
+    )(place, cutoffs, new, inner, own_winds, other_winds, one, two, tables)
     got = []
     for i, block in enumerate(blocks):
         b, across = i % parts, int(i < parts)
@@ -635,7 +654,7 @@
             (k * parts + j, (k ^ across) * parts + (j ^ b)) for k in range(lats) for j in range(parts)
         ]
         got.append(lax.ppermute(block, ("lat", "lev"), pairs) if i != parts else block)
-    far = [i for i in range(parts) if i % 2 == 0]
+    far = [i for i in range(2 * parts) if i % 2 == 0 and i != parts]
     scales = pl.pallas_call(
         functools.partial(scale_kernel, rows * column),
         name="scales",

time: 56.1 us -> 51.9 us (0.925)
  the two profiles are of different devices: /device:TPU:0 before, /device:TPU:17 now
where the time goes in v1:
time: 51.9 us; the launch traced here: 51.6 us
  starting transfers between devices  21.4 us (41%)
  Pallas kernels  14 us (27%)
  waiting for transfers between devices  12.8 us (25%)
  local copies, waits for them, and re-layouts  2.59 us (5%)
  between operations  0.78 us (2%)
    ppermute x7, starting transfers between devices, shards(): lax.ppermute(block, ('lat', 'lev'), pairs)  9.3 us
    ppermute x7, waiting for transfers between devices, shards(): lax.ppermute(block, ('lat', 'lev'), pairs)  5.23 us
    ppermute x1, starting transfers between devices, shards(): far = lax.ppermute(edge, 'lat', far_pairs)  3.22 us
    ppermute x1, waiting for transfers between devices, shards(): two = lax.ppermute(two, 'lat', twos)  2.79 us
    unnamed x16, local copies, waits for them, and re-layouts  2.57 us
    pallas_call x1, Pallas kernels, shards(): pl.pallas_call(functools.partial(column_kernel, z, parts, far), name='col...  2.55 us
    pallas_call x1, Pallas kernels, shards(): pl.pallas_call(functools.partial(outer_kernel, z, parts), name='outer', i...  2.37 us
    pallas_call x1, Pallas kernels, shards(): pl.pallas_call(functools.partial(inner_kernel, z), name='inner', in_specs...  2.32 us
  transfers between devices with their start and end apart: 14, of which 7 were waited for; matrix products, arithmetic and copies ran while one was open for 0% of the time, Pallas kernels for 11%

profile of v1, /device:TPU:17, one launch (start us, length us, event | category | flops | bytes accessed | tf_op | source)
XLA Modules:
  0.0 51.6 jit_solution(12915467304709772917)
XLA Ops:
  0.6 0.0 copy-start
  0.6 1.9 %edge.1 = s16[16,7936]{1,0:T(8,128)(2,1)} custom-call(f32[2,4,16,3072]{3,2,1,0:T(8,128)} %fields_ref.5, bf16[2,4,16,3072]{3,2,1,0:T(8,128)(2,1)} %courant_ref.7), custom_call_target="tpu_custom_call" | custom-call | flops 1000 | bytes 1000 | tf_op jit(solution)/shard_map/edge/pallas_call | solution.py:559
  2.5 1.3 %collective-permute-start = (s16[16,7936]{1,0:T(8,128)(2,1)}, s16[16,7936]{1,0:T(8,128)(2,1)S(1)}, u32[]{:S(2)}, u32[]{:S(2)}) collective-permute-start(s16[16,7936]{1,0:T(8,128)(2,1)} %edge.1), channel_id=1, source_target_pairs={{0,4},{4,0},{8,12},{12,8},{16,20},{20,16},{24,28},{28,24},{1,5},{5... | collective-permute-start | bytes 761864 | tf_op jit(solution)/shard_map/ppermute | solution.py:573
  3.8 0.1 pad_add_fusion.par_ref
  3.9 0.0 copy-start.1
  3.9 1.4 %copy-done.1 = f32[2,4,16,3072]{3,2,1,0:T(8,128)S(1)} copy-done((f32[2,4,16,3072]{3,2,1,0:T(8,128)S(1)}, f32[2,4,16,3072]{3,2,1,0:T(8,128)}, u32[]{:S(2)}) %copy-start.1) | copy-done | bytes 1572888
  5.3 0.0 copy-start.3
  5.3 1.1 %copy-done.3 = bf16[2,4,16,3072]{3,2,1,0:T(8,128)(2,1)S(1)} copy-done((bf16[2,4,16,3072]{3,2,1,0:T(8,128)(2,1)S(1)}, bf16[2,4,16,3072]{3,2,1,0:T(8,128)(2,1)}, u32[]{:S(2)}) %copy-start.3) | copy-done | bytes 786456
  6.4 1.0 %rest.1 = (s16[16,9472]{1,0:T(8,128)(2,1)S(1)}, s16[16,7680]{1,0:T(8,128)(2,1)S(1)}, s16[16,7936]{1,0:T(8,128)(2,1)S(1)}) custom-call(s32[4]{0:T(128)S(1)} %pad_add_fusion.par_ref, f32[2,4,16,3072]{3,2,1,0:T(8,128)S(1)} %copy-done.1, bf16[2,4,16,3072]{3,2,1,0:T(8,128)(2,1)S(1)} %copy-done.3), custom_call_target="tpu_custom_call" | custom-call | flops 1000 | bytes 1000 | tf_op jit(solution)/shard_map/rest/pallas_call | solution.py:574
  7.4 0.3 collective-permute-start.1
  7.7 2.1 %collective-permute-start.2 = (s16[16,7936]{1,0:T(8,128)(2,1)S(1)}, s16[16,7936]{1,0:T(8,128)(2,1)S(1)}, u32[]{:S(2)}, u32[]{:S(2)}) collective-permute-start(s16[16,7936]{1,0:T(8,128)(2,1)S(1)} %get-tuple-element.24), channel_id=1, source_target_pairs={{8,0},{4,12},{16,8},{12,20},{24,16},{20,28},{9,1},{5,13},{17,9},{1... | collective-permute-start | bytes 761864 | tf_op jit(solution)/shard_map/ppermute | solution.py:583
  9.8 0.0 collective-permute-done.edge_ref
  9.8 3.2 %collective-permute-start.3 = (s16[16,7936]{1,0:T(8,128)(2,1)S(1)}, s16[16,7936]{1,0:T(8,128)(2,1)S(1)}, u32[]{:S(2)}, u32[]{:S(2)}) collective-permute-start(s16[16,7936]{1,0:T(8,128)(2,1)S(1)} %collective-permute-done.edge_ref), channel_id=1, source_target_pairs={{0,8},{12,4},{8,16},{20,12},{16,24},{28,20},{1,9},{13,5},{9,17},{2... | collective-permute-start | bytes 761864 | tf_op jit(solution)/shard_map/ppermute | solution.py:585
  13.0 0.0 copy-start.4
  13.1 1.3 %collective-permute-start.4 = (s16[16,7680]{1,0:T(8,128)(2,1)S(1)}, s16[16,7680]{1,0:T(8,128)(2,1)S(1)}, u32[]{:S(2)}, u32[]{:S(2)}) collective-permute-start(s16[16,7680]{1,0:T(8,128)(2,1)S(1)} %get-tuple-element.26), channel_id=1, source_target_pairs={{0,4},{4,0},{8,12},{12,8},{16,20},{20,16},{24,28},{28,24},{1,5},{5... | collective-permute-start | bytes 737288 | tf_op jit(solution)/shard_map/ppermute | solution.py:586
  14.3 1.7 %collective-permute-done.2.near_ref = s16[16,7936]{1,0:T(8,128)(2,1)S(1)} collective-permute-done((s16[16,7936]{1,0:T(8,128)(2,1)S(1)}, s16[16,7936]{1,0:T(8,128)(2,1)S(1)}, u32[]{:S(2)}, u32[]{:S(2)}) %collective-permute-start.2) | collective-permute-done | bytes 253984 | tf_op jit(solution)/shard_map/ppermute | solution.py:583
  16.0 0.7 %collective-permute-done.1.middle_ref = s16[16,9472]{1,0:T(8,128)(2,1)S(1)} collective-permute-done((s16[16,9472]{1,0:T(8,128)(2,1)S(1)}, s16[16,9472]{1,0:T(8,128)(2,1)S(1)}, u32[]{:S(2)}, u32[]{:S(2)}) %collective-permute-start.1) | collective-permute-done | bytes 303136 | tf_op jit(solution)/shard_map/ppermute | solution.py:584
  16.7 0.4 collective-permute-done.3.far_ref
  17.1 2.3 %own.1 = (f32[4,2,8,3328]{3,2,1,0:T(8,128)S(1)}, f32[13,8,3072]{2,1,0:T(8,128)S(1)}, s16[16,6400]{1,0:T(8,128)(2,1)S(1)}, f32[12,2,8,3328]{3,2,1,0:T(8,128)S(1)}) custom-call(s32[4]{0:T(128)S(1)} %pad_add_fusion.par_ref, f32[2,4,16,3072]{3,2,1,0:T(8,128)S(1)} %copy-done.1, bf16[2,4,16,3072]{3,2,1,0:T(8,128)(2,1)S(1)} %copy-done.3, ...), custom_call_target="tpu_custom_call" | custom-call | flops 1000 | bytes 1000 | tf_op jit(solution)/shard_map/own/pallas_call | solution.py:592
  19.4 1.9 %collective-permute-done.4.last_ref = s16[16,7680]{1,0:T(8,128)(2,1)S(1)} collective-permute-done((s16[16,7680]{1,0:T(8,128)(2,1)S(1)}, s16[16,7680]{1,0:T(8,128)(2,1)S(1)}, u32[]{:S(2)}, u32[]{:S(2)}) %collective-permute-start.4) | collective-permute-done | bytes 245792 | tf_op jit(solution)/shard_map/ppermute | solution.py:586
  21.3 0.0 copy-done.4
  21.3 1.6 %other.1 = (f32[2,2,8,3328]{3,2,1,0:T(8,128)S(1)}, f32[13,8,3072]{2,1,0:T(8,128)S(1)}, s16[16,6400]{1,0:T(8,128)(2,1)S(1)}, s16[16,6400]{1,0:T(8,128)(2,1)S(1)}) custom-call(s32[4]{0:T(128)S(1)} %pad_add_fusion.par_ref, bf16[2,4,16,3072]{3,2,1,0:T(8,128)(2,1)S(1)} %copy-done.4, s16[16,7936]{1,0:T(8,128)(2,1)S(1)} %collective-permute-done.edge_ref, ...), custom_call_target="tpu_custom_call" | custom-call | flops 1000 | bytes 1000 | tf_op jit(solution)/shard_map/other/pallas_call | solution.py:607
  22.9 2.1 %collective-permute-start.5 = (s16[16,6400]{1,0:T(8,128)(2,1)S(1)}, s16[16,6400]{1,0:T(8,128)(2,1)S(1)}, u32[]{:S(2)}, u32[]{:S(2)}) collective-permute-start(s16[16,6400]{1,0:T(8,128)(2,1)S(1)} %get-tuple-element.34), channel_id=1, source_target_pairs={{0,8},{8,0},{4,12},{12,4},{16,24},{24,16},{20,28},{28,20},{1,9},{9... | collective-permute-start | bytes 614408 | tf_op jit(solution)/shard_map/ppermute | solution.py:622
  25.0 1.9 %collective-permute-start.6 = (s16[16,6400]{1,0:T(8,128)(2,1)S(1)}, s16[16,6400]{1,0:T(8,128)(2,1)S(1)}, u32[]{:S(2)}, u32[]{:S(2)}) collective-permute-start(s16[16,6400]{1,0:T(8,128)(2,1)S(1)} %get-tuple-element.35), channel_id=1, source_target_pairs={{8,16},{16,8},{12,20},{20,12},{9,17},{17,9},{13,21},{21,13},{10,18... | collective-permute-start | bytes 614408 | tf_op jit(solution)/shard_map/ppermute | solution.py:623
  26.9 0.0 copy-done.2
  26.9 0.0 copy-done.7
  26.9 2.3 %inner.1 = (f32[8,2,8,3328]{3,2,1,0:T(8,128)S(1)}, f32[4,2,8,3072]{3,2,1,0:T(8,128)S(1)}) custom-call(s32[4]{0:T(128)S(1)} %pad_add_fusion.par_ref, s32[32]{0:T(128)S(1)} %copy-done.7, f32[4,2,8,3328]{3,2,1,0:T(8,128)S(1)} %get-tuple-element.25.own_ref, f32[2,2,8,3328]{3,2,1,0:T(8,128)S(1)} %get-tuple-element.29.other_ref, ...), custom_call_target="tpu_custom_call" | custom-call | flops 1000 | bytes 1000 | tf_op jit(solution)/shard_map/inner/pallas_call | solution.py:626
  29.3 0.0 collective-permute-done.5.one_ref
  29.3 2.8 %collective-permute-done.6.two_ref = s16[16,6400]{1,0:T(8,128)(2,1)S(1)} collective-permute-done((s16[16,6400]{1,0:T(8,128)(2,1)S(1)}, s16[16,6400]{1,0:T(8,128)(2,1)S(1)}, u32[]{:S(2)}, u32[]{:S(2)}) %collective-permute-start.6) | collective-permute-done | bytes 204832 | tf_op jit(solution)/shard_map/ppermute | solution.py:623
  32.1 2.4 %outer.1 = (s16[16,3200]{1,0:T(8,128)(2,1)S(1)}, s16[16,3200]{1,0:T(8,128)(2,1)S(1)}, s16[16,3200]{1,0:T(8,128)(2,1)S(1)}, s16[16,3200]{1,0:T(8,128)(2,1)S(1)}, ...) custom-call(s32[4]{0:T(128)S(1)} %pad_add_fusion.par_ref, ...), custom_call_target="tpu_custom_call" | custom-call | flops 1000 | bytes 1000 | tf_op jit(solution)/shard_map/outer/pallas_call | solution.py:637
  34.4 1.3 %collective-permute-start.12 = (s16[16,3200]{1,0:T(8,128)(2,1)S(1)}, s16[16,3200]{1,0:T(8,128)(2,1)S(1)}, u32[]{:S(2)}, u32[]{:S(2)}) collective-permute-start(s16[16,3200]{1,0:T(8,128)(2,1)S(1)} %get-tuple-element.42), channel_id=1, source_target_pairs={{0,2},{1,3},{2,0},{3,1},{4,6},{5,7},{6,4},{7,5},{8,10},{9,11},{10,... | collective-permute-start | bytes 307208 | tf_op jit(solution)/shard_map/ppermute | solution.py:656
  35.7 0.2 collective-permute-start.7
  35.9 1.2 %collective-permute-start.9 = (s16[16,3200]{1,0:T(8,128)(2,1)S(1)}, s16[16,3200]{1,0:T(8,128)(2,1)S(1)}, u32[]{:S(2)}, u32[]{:S(2)}) collective-permute-start(s16[16,3200]{1,0:T(8,128)(2,1)S(1)} %get-tuple-element.38), channel_id=1, source_target_pairs={{0,6},{1,7},{2,4},{3,5},{4,2},{5,3},{6,0},{7,1},{8,14},{9,15},{10,... | collective-permute-start | bytes 307208 | tf_op jit(solution)/shard_map/ppermute | solution.py:656
  37.1 4.9 %collective-permute-start.10 = (s16[16,3200]{1,0:T(8,128)(2,1)S(1)}, s16[16,3200]{1,0:T(8,128)(2,1)S(1)}, u32[]{:S(2)}, u32[]{:S(2)}) collective-permute-start(s16[16,3200]{1,0:T(8,128)(2,1)S(1)} %get-tuple-element.39), channel_id=1, source_target_pairs={{0,7},{1,6},{2,5},{3,4},{4,3},{5,2},{6,1},{7,0},{8,15},{9,14},{10,... | collective-permute-start | bytes 307208 | tf_op jit(solution)/shard_map/ppermute | solution.py:656
  42.0 0.0 collective-permute-start.11
  42.0 0.0 collective-permute-done.12.refs_2_.refs_6_
  42.0 1.2 %collective-permute-start.13 = (s16[16,3200]{1,0:T(8,128)(2,1)S(1)}, s16[16,3200]{1,0:T(8,128)(2,1)S(1)}, u32[]{:S(2)}, u32[]{:S(2)}) collective-permute-start(s16[16,3200]{1,0:T(8,128)(2,1)S(1)} %get-tuple-element.43), channel_id=1, source_target_pairs={{0,3},{1,2},{2,1},{3,0},{4,7},{5,6},{6,5},{7,4},{8,11},{9,10},{10,... | collective-permute-start | bytes 307208 | tf_op jit(solution)/shard_map/ppermute | solution.py:656
  43.2 0.0 collective-permute-done.7.refs_0_
  43.2 0.5 %collective-permute-start.8 = (s16[16,3200]{1,0:T(8,128)(2,1)S(1)}, s16[16,3200]{1,0:T(8,128)(2,1)S(1)}, u32[]{:S(2)}, u32[]{:S(2)}) collective-permute-start(s16[16,3200]{1,0:T(8,128)(2,1)S(1)} %get-tuple-element.37), channel_id=1, source_target_pairs={{0,5},{1,4},{2,7},{3,6},{4,1},{5,0},{6,3},{7,2},{8,13},{9,12},{10,... | collective-permute-start | bytes 307208 | tf_op jit(solution)/shard_map/ppermute | solution.py:656
  43.7 0.0 copy-done
  43.8 0.0 collective-permute-done.9.refs_1_.refs_2_
  43.8 3.3 %collective-permute-done.10.refs_3_ = s16[16,3200]{1,0:T(8,128)(2,1)S(1)} collective-permute-done((s16[16,3200]{1,0:T(8,128)(2,1)S(1)}, s16[16,3200]{1,0:T(8,128)(2,1)S(1)}, u32[]{:S(2)}, u32[]{:S(2)}) %collective-permute-start.10) | collective-permute-done | bytes 102432 | tf_op jit(solution)/shard_map/ppermute | solution.py:656
  47.1 0.0 collective-permute-done.11.refs_5_
  47.1 1.9 %collective-permute-done.13.refs_7_ = s16[16,3200]{1,0:T(8,128)(2,1)S(1)} collective-permute-done((s16[16,3200]{1,0:T(8,128)(2,1)S(1)}, s16[16,3200]{1,0:T(8,128)(2,1)S(1)}, u32[]{:S(2)}, u32[]{:S(2)}) %collective-permute-start.13) | collective-permute-done | bytes 102432 | tf_op jit(solution)/shard_map/ppermute | solution.py:656
  49.0 0.0 collective-permute-done.8.refs_1_
  49.0 0.0 copy-done.5
  49.0 0.0 copy-done.6
  49.0 2.6 %columns.1 = (f32[2,4,64,768]{3,2,1,0:T(8,128)}, f32[4,64,768]{2,1,0:T(8,128)}) custom-call(s32[4]{0:T(128)S(1)} %pad_add_fusion.par_ref, s16[16,3200]{1,0:T(8,128)(2,1)S(1)} %collective-permute-done.7.refs_0_, s16[16,3200]{1,0:T(8,128)(2,1)S(1)} %collective-permute-done.8.refs_1_, s16[16,3200]{1,0:T(8,128)(2,1)S(1)} %collective-permute-done.9.refs_1_.refs_2_, ...), custom_call_target="tpu_custom_call" | custom-call | flops 1000 | bytes 1000 | tf_op jit(solution)/shard_map/columns/pallas_call | solution.py:672
  (7 shorter events, 0.0 us)
Async XLA Ops:
  0.6 43.1 %copy-start = (f32[4,3072]{1,0:T(4,128)S(1)}, f32[4,3072]{1,0:T(4,128)}, u32[]{:S(2)}) copy-start(f32[4,3072]{1,0:T(4,128)} %param.10) | copy-start | bytes 147460
  2.5 7.3 %collective-permute-start = (s16[16,7936]{1,0:T(8,128)(2,1)}, s16[16,7936]{1,0:T(8,128)(2,1)S(1)}, u32[]{:S(2)}, u32[]{:S(2)}) collective-permute-start(s16[16,7936]{1,0:T(8,128)(2,1)} %edge.1), channel_id=1, source_target_pairs={{0,4},{4,0},{8,12},{12,8},{16,20},{20,16},{24,28},{28,24},{1,5},{5... | collective-permute-start | bytes 761864 | tf_op jit(solution)/shard_map/ppermute | solution.py:573
  3.9 1.4 %copy-start.1 = (f32[2,4,16,3072]{3,2,1,0:T(8,128)S(1)}, f32[2,4,16,3072]{3,2,1,0:T(8,128)}, u32[]{:S(2)}) copy-start(f32[2,4,16,3072]{3,2,1,0:T(8,128)} %fields_ref.5) | copy-start | bytes 4718596
  5.3 1.1 %copy-start.3 = (bf16[2,4,16,3072]{3,2,1,0:T(8,128)(2,1)S(1)}, bf16[2,4,16,3072]{3,2,1,0:T(8,128)(2,1)}, u32[]{:S(2)}) copy-start(bf16[2,4,16,3072]{3,2,1,0:T(8,128)(2,1)} %courant_ref.7) | copy-start | bytes 2359300
  7.4 9.3 %collective-permute-start.1 = (s16[16,9472]{1,0:T(8,128)(2,1)S(1)}, s16[16,9472]{1,0:T(8,128)(2,1)S(1)}, u32[]{:S(2)}, u32[]{:S(2)}) collective-permute-start(s16[16,9472]{1,0:T(8,128)(2,1)S(1)} %get-tuple-element.23), channel_id=1, source_target_pairs={{0,4},{4,0},{8,12},{12,8},{16,20},{20,16},{24,28},{28,24},{1,5},{5... | collective-permute-start | bytes 909320 | tf_op jit(solution)/shard_map/ppermute | solution.py:584
  7.7 8.3 %collective-permute-start.2 = (s16[16,7936]{1,0:T(8,128)(2,1)S(1)}, s16[16,7936]{1,0:T(8,128)(2,1)S(1)}, u32[]{:S(2)}, u32[]{:S(2)}) collective-permute-start(s16[16,7936]{1,0:T(8,128)(2,1)S(1)} %get-tuple-element.24), channel_id=1, source_target_pairs={{8,0},{4,12},{16,8},{12,20},{24,16},{20,28},{9,1},{5,13},{17,9},{1... | collective-permute-start | bytes 761864 | tf_op jit(solution)/shard_map/ppermute | solution.py:583
  9.8 7.3 %collective-permute-start.3 = (s16[16,7936]{1,0:T(8,128)(2,1)S(1)}, s16[16,7936]{1,0:T(8,128)(2,1)S(1)}, u32[]{:S(2)}, u32[]{:S(2)}) collective-permute-start(s16[16,7936]{1,0:T(8,128)(2,1)S(1)} %collective-permute-done.edge_ref), channel_id=1, source_target_pairs={{0,8},{12,4},{8,16},{20,12},{16,24},{28,20},{1,9},{13,5},{9,17},{2... | collective-permute-start | bytes 761864 | tf_op jit(solution)/shard_map/ppermute | solution.py:585
  13.0 8.3 %copy-start.4 = (bf16[2,4,16,3072]{3,2,1,0:T(8,128)(2,1)S(1)}, bf16[2,4,16,3072]{3,2,1,0:T(8,128)(2,1)}, u32[]{:S(2)}) copy-start(bf16[2,4,16,3072]{3,2,1,0:T(8,128)(2,1)} %courant_ref.7) | copy-start | bytes 2359300
  13.1 8.3 %collective-permute-start.4 = (s16[16,7680]{1,0:T(8,128)(2,1)S(1)}, s16[16,7680]{1,0:T(8,128)(2,1)S(1)}, u32[]{:S(2)}, u32[]{:S(2)}) collective-permute-start(s16[16,7680]{1,0:T(8,128)(2,1)S(1)} %get-tuple-element.26), channel_id=1, source_target_pairs={{0,4},{4,0},{8,12},{12,8},{16,20},{20,16},{24,28},{28,24},{1,5},{5... | collective-permute-start | bytes 737288 | tf_op jit(solution)/shard_map/ppermute | solution.py:586
  21.3 5.6 %copy-start.2 = (bf16[4,1536,256]{2,1,0:T(8,128)(2,1)S(1)}, bf16[4,1536,256]{2,1,0:T(8,128)(2,1)}, u32[]{:S(2)}) copy-start(bf16[4,1536,256]{2,1,0:T(8,128)(2,1)} %constant.48.clone.table_ref) | copy-start | bytes 9437188
  21.3 5.6 %copy-start.7 = (s32[32]{0:T(128)S(1)}, s32[32]{0:T(128)}, u32[]{:S(2)}) copy-start(s32[32]{0:T(128)} %cut_ref.3) | copy-start | bytes 388
  22.9 6.3 %collective-permute-start.5 = (s16[16,6400]{1,0:T(8,128)(2,1)S(1)}, s16[16,6400]{1,0:T(8,128)(2,1)S(1)}, u32[]{:S(2)}, u32[]{:S(2)}) collective-permute-start(s16[16,6400]{1,0:T(8,128)(2,1)S(1)} %get-tuple-element.34), channel_id=1, source_target_pairs={{0,8},{8,0},{4,12},{12,4},{16,24},{24,16},{20,28},{28,20},{1,9},{9... | collective-permute-start | bytes 614408 | tf_op jit(solution)/shard_map/ppermute | solution.py:622
  25.0 7.1 %collective-permute-start.6 = (s16[16,6400]{1,0:T(8,128)(2,1)S(1)}, s16[16,6400]{1,0:T(8,128)(2,1)S(1)}, u32[]{:S(2)}, u32[]{:S(2)}) collective-permute-start(s16[16,6400]{1,0:T(8,128)(2,1)S(1)} %get-tuple-element.35), channel_id=1, source_target_pairs={{8,16},{16,8},{12,20},{20,12},{9,17},{17,9},{13,21},{21,13},{10,18... | collective-permute-start | bytes 614408 | tf_op jit(solution)/shard_map/ppermute | solution.py:623
  32.1 17.0 %copy-start.5 = (f32[64,192]{1,0:T(8,128)S(1)}, f32[64,192]{1,0:T(8,128)}, u32[]{:S(2)}) copy-start(f32[64,192]{1,0:T(8,128)} %constant.49.clone.refs_10_) | copy-start | bytes 147460
  32.1 17.0 %copy-start.6 = (f32[64,64]{1,0:T(8,128)S(1)}, f32[64,64]{1,0:T(8,128)}, u32[]{:S(2)}) copy-start(f32[64,64]{1,0:T(8,128)} %refs_9_.1) | copy-start | bytes 49156
  34.4 7.6 %collective-permute-start.12 = (s16[16,3200]{1,0:T(8,128)(2,1)S(1)}, s16[16,3200]{1,0:T(8,128)(2,1)S(1)}, u32[]{:S(2)}, u32[]{:S(2)}) collective-permute-start(s16[16,3200]{1,0:T(8,128)(2,1)S(1)} %get-tuple-element.42), channel_id=1, source_target_pairs={{0,2},{1,3},{2,0},{3,1},{4,6},{5,7},{6,4},{7,5},{8,10},{9,11},{10,... | collective-permute-start | bytes 307208 | tf_op jit(solution)/shard_map/ppermute | solution.py:656
  35.7 7.5 %collective-permute-start.7 = (s16[16,3200]{1,0:T(8,128)(2,1)S(1)}, s16[16,3200]{1,0:T(8,128)(2,1)S(1)}, u32[]{:S(2)}, u32[]{:S(2)}) collective-permute-start(s16[16,3200]{1,0:T(8,128)(2,1)S(1)} %get-tuple-element.36), channel_id=1, source_target_pairs={{0,4},{1,5},{2,6},{3,7},{4,0},{5,1},{6,2},{7,3},{8,12},{9,13},{10,... | collective-permute-start | bytes 307208 | tf_op jit(solution)/shard_map/ppermute | solution.py:656
  35.9 7.8 %collective-permute-start.9 = (s16[16,3200]{1,0:T(8,128)(2,1)S(1)}, s16[16,3200]{1,0:T(8,128)(2,1)S(1)}, u32[]{:S(2)}, u32[]{:S(2)}) collective-permute-start(s16[16,3200]{1,0:T(8,128)(2,1)S(1)} %get-tuple-element.38), channel_id=1, source_target_pairs={{0,6},{1,7},{2,4},{3,5},{4,2},{5,3},{6,0},{7,1},{8,14},{9,15},{10,... | collective-permute-start | bytes 307208 | tf_op jit(solution)/shard_map/ppermute | solution.py:656
  37.1 10.0 %collective-permute-start.10 = (s16[16,3200]{1,0:T(8,128)(2,1)S(1)}, s16[16,3200]{1,0:T(8,128)(2,1)S(1)}, u32[]{:S(2)}, u32[]{:S(2)}) collective-permute-start(s16[16,3200]{1,0:T(8,128)(2,1)S(1)} %get-tuple-element.39), channel_id=1, source_target_pairs={{0,7},{1,6},{2,5},{3,4},{4,3},{5,2},{6,1},{7,0},{8,15},{9,14},{10,... | collective-permute-start | bytes 307208 | tf_op jit(solution)/shard_map/ppermute | solution.py:656
  42.0 5.1 %collective-permute-start.11 = (s16[16,3200]{1,0:T(8,128)(2,1)S(1)}, s16[16,3200]{1,0:T(8,128)(2,1)S(1)}, u32[]{:S(2)}, u32[]{:S(2)}) collective-permute-start(s16[16,3200]{1,0:T(8,128)(2,1)S(1)} %get-tuple-element.41), channel_id=1, source_target_pairs={{0,1},{1,0},{2,3},{3,2},{4,5},{5,4},{6,7},{7,6},{8,9},{9,8},{10,11... | collective-permute-start | bytes 307208 | tf_op jit(solution)/shard_map/ppermute | solution.py:656
  42.0 7.0 %collective-permute-start.13 = (s16[16,3200]{1,0:T(8,128)(2,1)S(1)}, s16[16,3200]{1,0:T(8,128)(2,1)S(1)}, u32[]{:S(2)}, u32[]{:S(2)}) collective-permute-start(s16[16,3200]{1,0:T(8,128)(2,1)S(1)} %get-tuple-element.43), channel_id=1, source_target_pairs={{0,3},{1,2},{2,1},{3,0},{4,7},{5,6},{6,5},{7,4},{8,11},{9,10},{10,... | collective-permute-start | bytes 307208 | tf_op jit(solution)/shard_map/ppermute | solution.py:656
  43.2 5.8 %collective-permute-start.8 = (s16[16,3200]{1,0:T(8,128)(2,1)S(1)}, s16[16,3200]{1,0:T(8,128)(2,1)S(1)}, u32[]{:S(2)}, u32[]{:S(2)}) collective-permute-start(s16[16,3200]{1,0:T(8,128)(2,1)S(1)} %get-tuple-element.37), channel_id=1, source_target_pairs={{0,5},{1,4},{2,7},{3,6},{4,1},{5,0},{6,3},{7,2},{8,13},{9,12},{10,... | collective-permute-start | bytes 307208 | tf_op jit(solution)/shard_map/ppermute | solution.py:656

commit v2 on v1

--- a/solution.py
+++ b/solution.py
@@ -414,37 +414,52 @@
         substep(z, 2, base, lambda j, f, piece: new_ref[low + j, f, :, piece], winds_ref, keep)
 
 
-def outer_kernel(
-    z, parts, par_ref, cut_ref, new_ref, inner_ref, own_winds_ref, other_winds_ref, one_ref, two_ref, table_ref, *refs
-):
-    out_refs, scratch = refs[: 2 * parts], refs[2 * parts :]
-    p = par_ref[0]
-    halos = (one_ref, two_ref)
-    outer_half(
-        z, parts, 1 - p, 2, par_ref, cut_ref, new_ref, inner_ref, other_winds_ref, halos, table_ref,
-        out_refs[:parts], *scratch,
-    )
-    outer_half(
-        z, parts, p, 0, par_ref, cut_ref, new_ref, inner_ref, own_winds_ref, halos, table_ref,
-        out_refs[parts:], *scratch,
-    )
+def early_kernel(z, parts, par_ref, cut_ref, new_ref, inner_ref, own_winds_ref, other_winds_ref, one_ref, table_ref, *refs):
+    side = 1 - par_ref[3]
+    out_refs, scratch = refs[:parts], refs[parts:]
+    halves(z, parts, side, par_ref, cut_ref, new_ref, inner_ref, own_winds_ref, other_winds_ref, one_ref, table_ref, out_refs, scratch)
+
+
+def late_kernel(z, parts, par_ref, cut_ref, new_ref, inner_ref, own_winds_ref, other_winds_ref, two_ref, table_ref, *refs):
+    side = par_ref[3]
+    early_refs, out_refs, scratch = refs[:parts], refs[parts : 3 * parts], refs[3 * parts :]
+    out_refs, other_refs = out_refs[:parts], out_refs[parts:]
+    own = side == par_ref[0]
+
+    def hand_on(mine_refs, rest_refs):
+        halves(z, parts, side, par_ref, cut_ref, new_ref, inner_ref, own_winds_ref, other_winds_ref, two_ref, table_ref, mine_refs, scratch)
+        for a, b in zip(early_refs, rest_refs):
+            b[...] = a[...]
+
+    pl.when(own)(lambda: hand_on(other_refs, out_refs))
+    pl.when(jnp.logical_not(own))(lambda: hand_on(out_refs, other_refs))
+
+
+def halves(z, parts, side, par_ref, cut_ref, new_ref, inner_ref, own_winds_ref, other_winds_ref, halo_ref, table_ref, out_refs, scratch):
+    winds_ref, u_ref, v_ref = scratch
+    own = side == par_ref[0]
+    inner_at = jnp.where(own, 0, 2)
+    rows = [offset + 2 * side + r for offset, n in ((0, 2), (z.rows, 2), (2 * z.rows, 3)) for r in range(n)]
+
+    def take(from_ref):
+        for row in rows:
+            winds_ref[row] = from_ref[row]
+
+    pl.when(own)(lambda: take(own_winds_ref))
+    pl.when(jnp.logical_not(own))(lambda: take(other_winds_ref))
+    outer_half(z, parts, side, inner_at, par_ref, cut_ref, new_ref, inner_ref, winds_ref, halo_ref, table_ref, out_refs, u_ref, v_ref)
 
 
 def outer_half(
-    z, parts, side, inner_at, par_ref, cut_ref, new_ref, inner_ref, winds_ref, halos, table_ref,
+    z, parts, side, inner_at, par_ref, cut_ref, new_ref, inner_ref, winds_ref, halo_ref, table_ref,
     out_refs, u_ref, v_ref,
 ):
     lon = z.lon
     tall = 2 * z.half
     base = z.rows * side
 
-    def halo(in_ref):
-        for r in range(2):
-            place_row(z, u_ref, 4 * side, in_ref, r)
-
-    first_swap = side + par_ref[3] == 1
-    pl.when(first_swap)(lambda: halo(halos[0]))
-    pl.when(jnp.logical_not(first_swap))(lambda: halo(halos[1]))
+    for r in range(2):
+        place_row(z, u_ref, 4 * side, halo_ref, r)
     for r in range(4):
         u_ref[2 * (1 - side) + r] = new_ref[base + r]
     for r in range(2):
@@ -634,19 +649,25 @@
     )(place, cutoffs, mine, other, u, own_winds, other_winds, tables)
 
     column = lon // parts
-    blocks = pl.pallas_call(
-        functools.partial(outer_kernel, z, parts),
-        name="outer",
-        in_specs=[scalars(), scalars()] + [whole()] * 7,
-        out_specs=[whole()] * (2 * parts),
-        out_shape=[codes(tall, rows * column + LANE)] * (2 * parts),
-        scratch_shapes=[
-            pltpu.VMEM((6, 2, z.half, z.pad), f32),
-            pltpu.VMEM((z.rows, 2, z.half, lon), f32),
-        ],
-        compiler_params=params(),
-        cost_estimate=cost(),
-    )(place, cutoffs, new, inner, own_winds, other_winds, one, two, tables)
+    def outer(kernel, name, halo, early):
+        count = parts + len(early)
+        return pl.pallas_call(
+            functools.partial(kernel, z, parts),
+            name=name,
+            in_specs=[scalars(), scalars()] + [whole()] * (6 + len(early)),
+            out_specs=[whole()] * count,
+            out_shape=[codes(tall, rows * column + LANE)] * count,
+            scratch_shapes=[
+                pltpu.VMEM((3 * z.rows + 1, z.half, lon), f32),
+                pltpu.VMEM((6, 2, z.half, z.pad), f32),
+                pltpu.VMEM((z.rows, 2, z.half, lon), f32),
+            ],
+            compiler_params=params(),
+            cost_estimate=cost(),
+        )(place, cutoffs, new, inner, own_winds, other_winds, halo, tables, *early)
+
+    blocks = outer(late_kernel, "late", two, outer(early_kernel, "early", one, []))
+
     got = []
     for i, block in enumerate(blocks):
         b, across = i % parts, int(i < parts)

time: 51.9 us -> 51.4 us (level)
  waiting for transfers between devices: 12.8 us -> 11.2 us
  Pallas kernels: 14 us -> 14.8 us
    ppermute x1, waiting for transfers between devices: 2.79 us -> 1.17 us  [shards(): two = lax.ppermute(two, 'lat', twos)]
    pallas_call x1 -> x2, Pallas kernels: 2.37 us -> 3.16 us  [outer(): pl.pallas_call(functools.partial(kernel, z, parts), name=name, in_specs=[...]
  transfers between devices with their start and end apart: 14 -> 14, of which waited for: 7 -> 7; matrix products, arithmetic and copies ran while one was open for 0% -> 0% of each run, Pallas kernels for 11% -> 14%
where the time goes in v2:
time: 51.4 us; the launch traced here: 50.8 us
  starting transfers between devices  21.4 us (42%)
  Pallas kernels  14.8 us (29%)
  waiting for transfers between devices  11.2 us (22%)
  local copies, waits for them, and re-layouts  2.59 us (5%)
  between operations  0.78 us (2%)
    ppermute x7, starting transfers between devices, shards(): lax.ppermute(block, ('lat', 'lev'), pairs)  9.3 us
    ppermute x7, waiting for transfers between devices, shards(): lax.ppermute(block, ('lat', 'lev'), pairs)  5.23 us
    ppermute x1, starting transfers between devices, shards(): far = lax.ppermute(edge, 'lat', far_pairs)  3.22 us
    pallas_call x2, Pallas kernels, outer(): pl.pallas_call(functools.partial(kernel, z, parts), name=name, in_specs=[...  3.16 us
    unnamed x16, local copies, waits for them, and re-layouts  2.57 us
    pallas_call x1, Pallas kernels, shards(): pl.pallas_call(functools.partial(column_kernel, z, parts, far), name='col...  2.56 us
    pallas_call x1, Pallas kernels, shards(): pl.pallas_call(functools.partial(inner_kernel, z), name='inner', in_specs...  2.35 us
    pallas_call x1, Pallas kernels, shards(): pl.pallas_call(functools.partial(own_kernel, z), name='own', in_specs=[sc...  2.24 us
  transfers between devices with their start and end apart: 14, of which 7 were waited for; matrix products, arithmetic and copies ran while one was open for 0% of the time, Pallas kernels for 14%

profile of v2, /device:TPU:17, one launch (start us, length us, event | category | flops | bytes accessed | tf_op | source)
XLA Modules:
  0.0 50.8 jit_solution(16102433618110330589)
XLA Ops:
  0.6 0.0 copy-start
  0.6 1.9 %edge.1 = s16[16,7936]{1,0:T(8,128)(2,1)} custom-call(f32[2,4,16,3072]{3,2,1,0:T(8,128)} %fields_ref.5, bf16[2,4,16,3072]{3,2,1,0:T(8,128)(2,1)} %courant_ref.7), custom_call_target="tpu_custom_call" | custom-call | flops 1000 | bytes 1000 | tf_op jit(solution)/shard_map/edge/pallas_call | solution.py:574
  2.5 1.3 %collective-permute-start = (s16[16,7936]{1,0:T(8,128)(2,1)}, s16[16,7936]{1,0:T(8,128)(2,1)S(1)}, u32[]{:S(2)}, u32[]{:S(2)}) collective-permute-start(s16[16,7936]{1,0:T(8,128)(2,1)} %edge.1), channel_id=1, source_target_pairs={{0,4},{4,0},{8,12},{12,8},{16,20},{20,16},{24,28},{28,24},{1,5},{5... | collective-permute-start | bytes 761864 | tf_op jit(solution)/shard_map/ppermute | solution.py:588
  3.8 0.1 pad_add_fusion.par_ref
  3.9 0.0 copy-start.2
  3.9 1.4 %copy-done.2 = f32[2,4,16,3072]{3,2,1,0:T(8,128)S(1)} copy-done((f32[2,4,16,3072]{3,2,1,0:T(8,128)S(1)}, f32[2,4,16,3072]{3,2,1,0:T(8,128)}, u32[]{:S(2)}) %copy-start.2) | copy-done | bytes 1572888
  5.3 1.1 %copy-done.3 = bf16[2,4,16,3072]{3,2,1,0:T(8,128)(2,1)S(1)} copy-done((bf16[2,4,16,3072]{3,2,1,0:T(8,128)(2,1)S(1)}, bf16[2,4,16,3072]{3,2,1,0:T(8,128)(2,1)}, u32[]{:S(2)}) %copy-start.3) | copy-done | bytes 786456
  6.4 1.0 %rest.1 = (s16[16,9472]{1,0:T(8,128)(2,1)S(1)}, s16[16,7680]{1,0:T(8,128)(2,1)S(1)}, s16[16,7936]{1,0:T(8,128)(2,1)S(1)}) custom-call(s32[4]{0:T(128)S(1)} %pad_add_fusion.par_ref, f32[2,4,16,3072]{3,2,1,0:T(8,128)S(1)} %copy-done.2, bf16[2,4,16,3072]{3,2,1,0:T(8,128)(2,1)S(1)} %copy-done.3), custom_call_target="tpu_custom_call" | custom-call | flops 1000 | bytes 1000 | tf_op jit(solution)/shard_map/rest/pallas_call | solution.py:589
  7.4 0.3 collective-permute-start.1
  7.7 2.1 %collective-permute-start.2 = (s16[16,7936]{1,0:T(8,128)(2,1)S(1)}, s16[16,7936]{1,0:T(8,128)(2,1)S(1)}, u32[]{:S(2)}, u32[]{:S(2)}) collective-permute-start(s16[16,7936]{1,0:T(8,128)(2,1)S(1)} %get-tuple-element.28), channel_id=1, source_target_pairs={{8,0},{4,12},{16,8},{12,20},{24,16},{20,28},{9,1},{5,13},{17,9},{1... | collective-permute-start | bytes 761864 | tf_op jit(solution)/shard_map/ppermute | solution.py:598
  9.8 0.0 collective-permute-done.edge_ref
  9.8 3.2 %collective-permute-start.3 = (s16[16,7936]{1,0:T(8,128)(2,1)S(1)}, s16[16,7936]{1,0:T(8,128)(2,1)S(1)}, u32[]{:S(2)}, u32[]{:S(2)}) collective-permute-start(s16[16,7936]{1,0:T(8,128)(2,1)S(1)} %collective-permute-done.edge_ref), channel_id=1, source_target_pairs={{0,8},{12,4},{8,16},{20,12},{16,24},{28,20},{1,9},{13,5},{9,17},{2... | collective-permute-start | bytes 761864 | tf_op jit(solution)/shard_map/ppermute | solution.py:600
  13.0 0.0 copy-start.4
  13.1 1.3 %collective-permute-start.4 = (s16[16,7680]{1,0:T(8,128)(2,1)S(1)}, s16[16,7680]{1,0:T(8,128)(2,1)S(1)}, u32[]{:S(2)}, u32[]{:S(2)}) collective-permute-start(s16[16,7680]{1,0:T(8,128)(2,1)S(1)} %get-tuple-element.30), channel_id=1, source_target_pairs={{0,4},{4,0},{8,12},{12,8},{16,20},{20,16},{24,28},{28,24},{1,5},{5... | collective-permute-start | bytes 737288 | tf_op jit(solution)/shard_map/ppermute | solution.py:601
  14.3 1.7 %collective-permute-done.2.near_ref = s16[16,7936]{1,0:T(8,128)(2,1)S(1)} collective-permute-done((s16[16,7936]{1,0:T(8,128)(2,1)S(1)}, s16[16,7936]{1,0:T(8,128)(2,1)S(1)}, u32[]{:S(2)}, u32[]{:S(2)}) %collective-permute-start.2) | collective-permute-done | bytes 253984 | tf_op jit(solution)/shard_map/ppermute | solution.py:598
  16.0 0.7 %collective-permute-done.1.middle_ref = s16[16,9472]{1,0:T(8,128)(2,1)S(1)} collective-permute-done((s16[16,9472]{1,0:T(8,128)(2,1)S(1)}, s16[16,9472]{1,0:T(8,128)(2,1)S(1)}, u32[]{:S(2)}, u32[]{:S(2)}) %collective-permute-start.1) | collective-permute-done | bytes 303136 | tf_op jit(solution)/shard_map/ppermute | solution.py:599
  16.7 0.4 collective-permute-done.3.far_ref
  17.1 2.2 %own.1 = (f32[4,2,8,3328]{3,2,1,0:T(8,128)S(1)}, f32[13,8,3072]{2,1,0:T(8,128)S(1)}, s16[16,6400]{1,0:T(8,128)(2,1)S(1)}, f32[12,2,8,3328]{3,2,1,0:T(8,128)S(1)}) custom-call(s32[4]{0:T(128)S(1)} %pad_add_fusion.par_ref, f32[2,4,16,3072]{3,2,1,0:T(8,128)S(1)} %copy-done.2, bf16[2,4,16,3072]{3,2,1,0:T(8,128)(2,1)S(1)} %copy-done.3, ...), custom_call_target="tpu_custom_call" | custom-call | flops 1000 | bytes 1000 | tf_op jit(solution)/shard_map/own/pallas_call | solution.py:607
  19.4 1.9 %collective-permute-done.4.last_ref = s16[16,7680]{1,0:T(8,128)(2,1)S(1)} collective-permute-done((s16[16,7680]{1,0:T(8,128)(2,1)S(1)}, s16[16,7680]{1,0:T(8,128)(2,1)S(1)}, u32[]{:S(2)}, u32[]{:S(2)}) %collective-permute-start.4) | collective-permute-done | bytes 245792 | tf_op jit(solution)/shard_map/ppermute | solution.py:601
  21.3 0.0 copy-done.4
  21.3 1.6 %other.1 = (f32[2,2,8,3328]{3,2,1,0:T(8,128)S(1)}, f32[13,8,3072]{2,1,0:T(8,128)S(1)}, s16[16,6400]{1,0:T(8,128)(2,1)S(1)}, s16[16,6400]{1,0:T(8,128)(2,1)S(1)}) custom-call(s32[4]{0:T(128)S(1)} %pad_add_fusion.par_ref, bf16[2,4,16,3072]{3,2,1,0:T(8,128)(2,1)S(1)} %copy-done.4, s16[16,7936]{1,0:T(8,128)(2,1)S(1)} %collective-permute-done.edge_ref, ...), custom_call_target="tpu_custom_call" | custom-call | flops 1000 | bytes 1000 | tf_op jit(solution)/shard_map/other/pallas_call | solution.py:622
  22.9 2.1 %collective-permute-start.6 = (s16[16,6400]{1,0:T(8,128)(2,1)S(1)}, s16[16,6400]{1,0:T(8,128)(2,1)S(1)}, u32[]{:S(2)}, u32[]{:S(2)}) collective-permute-start(s16[16,6400]{1,0:T(8,128)(2,1)S(1)} %get-tuple-element.39), channel_id=1, source_target_pairs={{0,8},{8,0},{4,12},{12,4},{16,24},{24,16},{20,28},{28,20},{1,9},{9... | collective-permute-start | bytes 614408 | tf_op jit(solution)/shard_map/ppermute | solution.py:637
  25.0 1.9 %collective-permute-start.5 = (s16[16,6400]{1,0:T(8,128)(2,1)S(1)}, s16[16,6400]{1,0:T(8,128)(2,1)S(1)}, u32[]{:S(2)}, u32[]{:S(2)}) collective-permute-start(s16[16,6400]{1,0:T(8,128)(2,1)S(1)} %get-tuple-element.38), channel_id=1, source_target_pairs={{8,16},{16,8},{12,20},{20,12},{9,17},{17,9},{13,21},{21,13},{10,18... | collective-permute-start | bytes 614408 | tf_op jit(solution)/shard_map/ppermute | solution.py:638
  26.9 0.0 copy-done.1
  26.9 0.0 copy-done.7
  26.9 2.4 %inner.1 = (f32[8,2,8,3328]{3,2,1,0:T(8,128)S(1)}, f32[4,2,8,3072]{3,2,1,0:T(8,128)S(1)}) custom-call(s32[4]{0:T(128)S(1)} %pad_add_fusion.par_ref, s32[32]{0:T(128)S(1)} %copy-done.7, f32[4,2,8,3328]{3,2,1,0:T(8,128)S(1)} %get-tuple-element.29.own_ref, f32[2,2,8,3328]{3,2,1,0:T(8,128)S(1)} %get-tuple-element.33.other_ref, ...), custom_call_target="tpu_custom_call" | custom-call | flops 1000 | bytes 1000 | tf_op jit(solution)/shard_map/inner/pallas_call | solution.py:641
  29.3 0.0 collective-permute-done.6.one_ref
  29.3 1.6 %early.1 = (s16[16,3200]{1,0:T(8,128)(2,1)S(1)}, s16[16,3200]{1,0:T(8,128)(2,1)S(1)}, s16[16,3200]{1,0:T(8,128)(2,1)S(1)}, s16[16,3200]{1,0:T(8,128)(2,1)S(1)}) custom-call(s32[4]{0:T(128)S(1)} %pad_add_fusion.par_ref, s32[32]{0:T(128)S(1)} %copy-done.7, f32[8,2,8,3328]{3,2,1,0:T(8,128)S(1)} %get-tuple-element.36.new_ref, ...), custom_call_target="tpu_custom_call" | custom-call | flops 1000 | bytes 1000 | tf_op jit(solution)/shard_map/early/pallas_call | solution.py:654
  30.9 1.2 %collective-permute-done.5.two_ref = s16[16,6400]{1,0:T(8,128)(2,1)S(1)} collective-permute-done((s16[16,6400]{1,0:T(8,128)(2,1)S(1)}, s16[16,6400]{1,0:T(8,128)(2,1)S(1)}, u32[]{:S(2)}, u32[]{:S(2)}) %collective-permute-start.5) | collective-permute-done | bytes 204832 | tf_op jit(solution)/shard_map/ppermute | solution.py:638
  32.0 1.6 %late.1 = (s16[16,3200]{1,0:T(8,128)(2,1)S(1)}, s16[16,3200]{1,0:T(8,128)(2,1)S(1)}, s16[16,3200]{1,0:T(8,128)(2,1)S(1)}, s16[16,3200]{1,0:T(8,128)(2,1)S(1)}, s...) custom-call(s32[4]{0:T(128)S(1)} %pad_add_fusion.par_ref, ...), custom_call_target="tpu_custom_call" | custom-call | flops 1000 | bytes 1000 | tf_op jit(solution)/shard_map/late/pallas_call | solution.py:654
  33.6 1.3 %collective-permute-start.12 = (s16[16,3200]{1,0:T(8,128)(2,1)S(1)}, s16[16,3200]{1,0:T(8,128)(2,1)S(1)}, u32[]{:S(2)}, u32[]{:S(2)}) collective-permute-start(s16[16,3200]{1,0:T(8,128)(2,1)S(1)} %get-tuple-element.50), channel_id=1, source_target_pairs={{0,2},{1,3},{2,0},{3,1},{4,6},{5,7},{6,4},{7,5},{8,10},{9,11},{10,... | collective-permute-start | bytes 307208 | tf_op jit(solution)/shard_map/ppermute | solution.py:677
  34.9 0.2 collective-permute-start.7
  35.2 1.2 %collective-permute-start.9 = (s16[16,3200]{1,0:T(8,128)(2,1)S(1)}, s16[16,3200]{1,0:T(8,128)(2,1)S(1)}, u32[]{:S(2)}, u32[]{:S(2)}) collective-permute-start(s16[16,3200]{1,0:T(8,128)(2,1)S(1)} %get-tuple-element.46), channel_id=1, source_target_pairs={{0,6},{1,7},{2,4},{3,5},{4,2},{5,3},{6,0},{7,1},{8,14},{9,15},{10,... | collective-permute-start | bytes 307208 | tf_op jit(solution)/shard_map/ppermute | solution.py:677
  36.4 4.9 %collective-permute-start.10 = (s16[16,3200]{1,0:T(8,128)(2,1)S(1)}, s16[16,3200]{1,0:T(8,128)(2,1)S(1)}, u32[]{:S(2)}, u32[]{:S(2)}) collective-permute-start(s16[16,3200]{1,0:T(8,128)(2,1)S(1)} %get-tuple-element.47), channel_id=1, source_target_pairs={{0,7},{1,6},{2,5},{3,4},{4,3},{5,2},{6,1},{7,0},{8,15},{9,14},{10,... | collective-permute-start | bytes 307208 | tf_op jit(solution)/shard_map/ppermute | solution.py:677
  41.2 0.0 collective-permute-start.11
  41.2 0.0 collective-permute-done.12.refs_2_.refs_6_
  41.2 1.2 %collective-permute-start.13 = (s16[16,3200]{1,0:T(8,128)(2,1)S(1)}, s16[16,3200]{1,0:T(8,128)(2,1)S(1)}, u32[]{:S(2)}, u32[]{:S(2)}) collective-permute-start(s16[16,3200]{1,0:T(8,128)(2,1)S(1)} %get-tuple-element.51), channel_id=1, source_target_pairs={{0,3},{1,2},{2,1},{3,0},{4,7},{5,6},{6,5},{7,4},{8,11},{9,10},{10,... | collective-permute-start | bytes 307208 | tf_op jit(solution)/shard_map/ppermute | solution.py:677
  42.4 0.0 collective-permute-done.7.refs_0_
  42.4 0.5 %collective-permute-start.8 = (s16[16,3200]{1,0:T(8,128)(2,1)S(1)}, s16[16,3200]{1,0:T(8,128)(2,1)S(1)}, u32[]{:S(2)}, u32[]{:S(2)}) collective-permute-start(s16[16,3200]{1,0:T(8,128)(2,1)S(1)} %get-tuple-element.45), channel_id=1, source_target_pairs={{0,5},{1,4},{2,7},{3,6},{4,1},{5,0},{6,3},{7,2},{8,13},{9,12},{10,... | collective-permute-start | bytes 307208 | tf_op jit(solution)/shard_map/ppermute | solution.py:677
  43.0 0.0 copy-done
  43.0 0.0 collective-permute-done.9.refs_1_.refs_2_
  43.0 3.3 %collective-permute-done.10.refs_3_ = s16[16,3200]{1,0:T(8,128)(2,1)S(1)} collective-permute-done((s16[16,3200]{1,0:T(8,128)(2,1)S(1)}, s16[16,3200]{1,0:T(8,128)(2,1)S(1)}, u32[]{:S(2)}, u32[]{:S(2)}) %collective-permute-start.10) | collective-permute-done | bytes 102432 | tf_op jit(solution)/shard_map/ppermute | solution.py:677
  46.3 0.0 collective-permute-done.11.refs_5_
  46.3 1.9 %collective-permute-done.13.refs_7_ = s16[16,3200]{1,0:T(8,128)(2,1)S(1)} collective-permute-done((s16[16,3200]{1,0:T(8,128)(2,1)S(1)}, s16[16,3200]{1,0:T(8,128)(2,1)S(1)}, u32[]{:S(2)}, u32[]{:S(2)}) %collective-permute-start.13) | collective-permute-done | bytes 102432 | tf_op jit(solution)/shard_map/ppermute | solution.py:677
  48.2 0.0 collective-permute-done.8.refs_1_
  48.2 0.0 copy-done.5
  48.2 0.0 copy-done.6
  48.2 2.6 %columns.1 = (f32[2,4,64,768]{3,2,1,0:T(8,128)}, f32[4,64,768]{2,1,0:T(8,128)}) custom-call(s32[4]{0:T(128)S(1)} %pad_add_fusion.par_ref, s16[16,3200]{1,0:T(8,128)(2,1)S(1)} %collective-permute-done.7.refs_0_, s16[16,3200]{1,0:T(8,128)(2,1)S(1)} %collective-permute-done.8.refs_1_, s16[16,3200]{1,0:T(8,128)(2,1)S(1)} %collective-permute-done.9.refs_1_.refs_2_, ...), custom_call_target="tpu_custom_call" | custom-call | flops 1000 | bytes 1000 | tf_op jit(solution)/shard_map/columns/pallas_call | solution.py:693
  (8 shorter events, 0.0 us)
Async XLA Ops:
  0.6 42.3 %copy-start = (f32[4,3072]{1,0:T(4,128)S(1)}, f32[4,3072]{1,0:T(4,128)}, u32[]{:S(2)}) copy-start(f32[4,3072]{1,0:T(4,128)} %param.10) | copy-start | bytes 147460
  2.5 7.3 %collective-permute-start = (s16[16,7936]{1,0:T(8,128)(2,1)}, s16[16,7936]{1,0:T(8,128)(2,1)S(1)}, u32[]{:S(2)}, u32[]{:S(2)}) collective-permute-start(s16[16,7936]{1,0:T(8,128)(2,1)} %edge.1), channel_id=1, source_target_pairs={{0,4},{4,0},{8,12},{12,8},{16,20},{20,16},{24,28},{28,24},{1,5},{5... | collective-permute-start | bytes 761864 | tf_op jit(solution)/shard_map/ppermute | solution.py:588
  3.9 1.4 %copy-start.2 = (f32[2,4,16,3072]{3,2,1,0:T(8,128)S(1)}, f32[2,4,16,3072]{3,2,1,0:T(8,128)}, u32[]{:S(2)}) copy-start(f32[2,4,16,3072]{3,2,1,0:T(8,128)} %fields_ref.5) | copy-start | bytes 4718596
  5.3 1.1 %copy-start.3 = (bf16[2,4,16,3072]{3,2,1,0:T(8,128)(2,1)S(1)}, bf16[2,4,16,3072]{3,2,1,0:T(8,128)(2,1)}, u32[]{:S(2)}) copy-start(bf16[2,4,16,3072]{3,2,1,0:T(8,128)(2,1)} %courant_ref.7) | copy-start | bytes 2359300
  7.4 9.3 %collective-permute-start.1 = (s16[16,9472]{1,0:T(8,128)(2,1)S(1)}, s16[16,9472]{1,0:T(8,128)(2,1)S(1)}, u32[]{:S(2)}, u32[]{:S(2)}) collective-permute-start(s16[16,9472]{1,0:T(8,128)(2,1)S(1)} %get-tuple-element.27), channel_id=1, source_target_pairs={{0,4},{4,0},{8,12},{12,8},{16,20},{20,16},{24,28},{28,24},{1,5},{5... | collective-permute-start | bytes 909320 | tf_op jit(solution)/shard_map/ppermute | solution.py:599
  7.7 8.3 %collective-permute-start.2 = (s16[16,7936]{1,0:T(8,128)(2,1)S(1)}, s16[16,7936]{1,0:T(8,128)(2,1)S(1)}, u32[]{:S(2)}, u32[]{:S(2)}) collective-permute-start(s16[16,7936]{1,0:T(8,128)(2,1)S(1)} %get-tuple-element.28), channel_id=1, source_target_pairs={{8,0},{4,12},{16,8},{12,20},{24,16},{20,28},{9,1},{5,13},{17,9},{1... | collective-permute-start | bytes 761864 | tf_op jit(solution)/shard_map/ppermute | solution.py:598
  9.8 7.3 %collective-permute-start.3 = (s16[16,7936]{1,0:T(8,128)(2,1)S(1)}, s16[16,7936]{1,0:T(8,128)(2,1)S(1)}, u32[]{:S(2)}, u32[]{:S(2)}) collective-permute-start(s16[16,7936]{1,0:T(8,128)(2,1)S(1)} %collective-permute-done.edge_ref), channel_id=1, source_target_pairs={{0,8},{12,4},{8,16},{20,12},{16,24},{28,20},{1,9},{13,5},{9,17},{2... | collective-permute-start | bytes 761864 | tf_op jit(solution)/shard_map/ppermute | solution.py:600
  13.0 8.3 %copy-start.4 = (bf16[2,4,16,3072]{3,2,1,0:T(8,128)(2,1)S(1)}, bf16[2,4,16,3072]{3,2,1,0:T(8,128)(2,1)}, u32[]{:S(2)}) copy-start(bf16[2,4,16,3072]{3,2,1,0:T(8,128)(2,1)} %courant_ref.7) | copy-start | bytes 2359300
  13.1 8.3 %collective-permute-start.4 = (s16[16,7680]{1,0:T(8,128)(2,1)S(1)}, s16[16,7680]{1,0:T(8,128)(2,1)S(1)}, u32[]{:S(2)}, u32[]{:S(2)}) collective-permute-start(s16[16,7680]{1,0:T(8,128)(2,1)S(1)} %get-tuple-element.30), channel_id=1, source_target_pairs={{0,4},{4,0},{8,12},{12,8},{16,20},{20,16},{24,28},{28,24},{1,5},{5... | collective-permute-start | bytes 737288 | tf_op jit(solution)/shard_map/ppermute | solution.py:601
  21.3 5.6 %copy-start.1 = (bf16[4,1536,256]{2,1,0:T(8,128)(2,1)S(1)}, bf16[4,1536,256]{2,1,0:T(8,128)(2,1)}, u32[]{:S(2)}) copy-start(bf16[4,1536,256]{2,1,0:T(8,128)(2,1)} %constant.48.clone.table_ref) | copy-start | bytes 9437188
  21.3 5.6 %copy-start.7 = (s32[32]{0:T(128)S(1)}, s32[32]{0:T(128)}, u32[]{:S(2)}) copy-start(s32[32]{0:T(128)} %cut_ref.5) | copy-start | bytes 388
  22.9 6.4 %collective-permute-start.6 = (s16[16,6400]{1,0:T(8,128)(2,1)S(1)}, s16[16,6400]{1,0:T(8,128)(2,1)S(1)}, u32[]{:S(2)}, u32[]{:S(2)}) collective-permute-start(s16[16,6400]{1,0:T(8,128)(2,1)S(1)} %get-tuple-element.39), channel_id=1, source_target_pairs={{0,8},{8,0},{4,12},{12,4},{16,24},{24,16},{20,28},{28,20},{1,9},{9... | collective-permute-start | bytes 614408 | tf_op jit(solution)/shard_map/ppermute | solution.py:637
  25.0 7.1 %collective-permute-start.5 = (s16[16,6400]{1,0:T(8,128)(2,1)S(1)}, s16[16,6400]{1,0:T(8,128)(2,1)S(1)}, u32[]{:S(2)}, u32[]{:S(2)}) collective-permute-start(s16[16,6400]{1,0:T(8,128)(2,1)S(1)} %get-tuple-element.38), channel_id=1, source_target_pairs={{8,16},{16,8},{12,20},{20,12},{9,17},{17,9},{13,21},{21,13},{10,18... | collective-permute-start | bytes 614408 | tf_op jit(solution)/shard_map/ppermute | solution.py:638
  32.0 16.2 %copy-start.5 = (f32[64,192]{1,0:T(8,128)S(1)}, f32[64,192]{1,0:T(8,128)}, u32[]{:S(2)}) copy-start(f32[64,192]{1,0:T(8,128)} %constant.49.clone.refs_10_) | copy-start | bytes 147460
  32.0 16.2 %copy-start.6 = (f32[64,64]{1,0:T(8,128)S(1)}, f32[64,64]{1,0:T(8,128)}, u32[]{:S(2)}) copy-start(f32[64,64]{1,0:T(8,128)} %refs_9_.1) | copy-start | bytes 49156
  33.6 7.6 %collective-permute-start.12 = (s16[16,3200]{1,0:T(8,128)(2,1)S(1)}, s16[16,3200]{1,0:T(8,128)(2,1)S(1)}, u32[]{:S(2)}, u32[]{:S(2)}) collective-permute-start(s16[16,3200]{1,0:T(8,128)(2,1)S(1)} %get-tuple-element.50), channel_id=1, source_target_pairs={{0,2},{1,3},{2,0},{3,1},{4,6},{5,7},{6,4},{7,5},{8,10},{9,11},{10,... | collective-permute-start | bytes 307208 | tf_op jit(solution)/shard_map/ppermute | solution.py:677
  34.9 7.5 %collective-permute-start.7 = (s16[16,3200]{1,0:T(8,128)(2,1)S(1)}, s16[16,3200]{1,0:T(8,128)(2,1)S(1)}, u32[]{:S(2)}, u32[]{:S(2)}) collective-permute-start(s16[16,3200]{1,0:T(8,128)(2,1)S(1)} %get-tuple-element.44), channel_id=1, source_target_pairs={{0,4},{1,5},{2,6},{3,7},{4,0},{5,1},{6,2},{7,3},{8,12},{9,13},{10,... | collective-permute-start | bytes 307208 | tf_op jit(solution)/shard_map/ppermute | solution.py:677
  35.2 7.8 %collective-permute-start.9 = (s16[16,3200]{1,0:T(8,128)(2,1)S(1)}, s16[16,3200]{1,0:T(8,128)(2,1)S(1)}, u32[]{:S(2)}, u32[]{:S(2)}) collective-permute-start(s16[16,3200]{1,0:T(8,128)(2,1)S(1)} %get-tuple-element.46), channel_id=1, source_target_pairs={{0,6},{1,7},{2,4},{3,5},{4,2},{5,3},{6,0},{7,1},{8,14},{9,15},{10,... | collective-permute-start | bytes 307208 | tf_op jit(solution)/shard_map/ppermute | solution.py:677
  36.4 10.0 %collective-permute-start.10 = (s16[16,3200]{1,0:T(8,128)(2,1)S(1)}, s16[16,3200]{1,0:T(8,128)(2,1)S(1)}, u32[]{:S(2)}, u32[]{:S(2)}) collective-permute-start(s16[16,3200]{1,0:T(8,128)(2,1)S(1)} %get-tuple-element.47), channel_id=1, source_target_pairs={{0,7},{1,6},{2,5},{3,4},{4,3},{5,2},{6,1},{7,0},{8,15},{9,14},{10,... | collective-permute-start | bytes 307208 | tf_op jit(solution)/shard_map/ppermute | solution.py:677
  41.2 5.1 %collective-permute-start.11 = (s16[16,3200]{1,0:T(8,128)(2,1)S(1)}, s16[16,3200]{1,0:T(8,128)(2,1)S(1)}, u32[]{:S(2)}, u32[]{:S(2)}) collective-permute-start(s16[16,3200]{1,0:T(8,128)(2,1)S(1)} %get-tuple-element.49), channel_id=1, source_target_pairs={{0,1},{1,0},{2,3},{3,2},{4,5},{5,4},{6,7},{7,6},{8,9},{9,8},{10,11... | collective-permute-start | bytes 307208 | tf_op jit(solution)/shard_map/ppermute | solution.py:677
  41.2 7.0 %collective-permute-start.13 = (s16[16,3200]{1,0:T(8,128)(2,1)S(1)}, s16[16,3200]{1,0:T(8,128)(2,1)S(1)}, u32[]{:S(2)}, u32[]{:S(2)}) collective-permute-start(s16[16,3200]{1,0:T(8,128)(2,1)S(1)} %get-tuple-element.51), channel_id=1, source_target_pairs={{0,3},{1,2},{2,1},{3,0},{4,7},{5,6},{6,5},{7,4},{8,11},{9,10},{10,... | collective-permute-start | bytes 307208 | tf_op jit(solution)/shard_map/ppermute | solution.py:677
  42.4 5.8 %collective-permute-start.8 = (s16[16,3200]{1,0:T(8,128)(2,1)S(1)}, s16[16,3200]{1,0:T(8,128)(2,1)S(1)}, u32[]{:S(2)}, u32[]{:S(2)}) collective-permute-start(s16[16,3200]{1,0:T(8,128)(2,1)S(1)} %get-tuple-element.45), channel_id=1, source_target_pairs={{0,5},{1,4},{2,7},{3,6},{4,1},{5,0},{6,3},{7,2},{8,13},{9,12},{10,... | collective-permute-start | bytes 307208 | tf_op jit(solution)/shard_map/ppermute | solution.py:677

commit v3 on v2

--- a/solution.py
+++ b/solution.py
@@ -490,28 +490,33 @@
 
 def column_kernel(z, parts, far, par_ref, *refs):
     got, refs = refs[: 2 * parts], refs[2 * parts :]
-    scales_ref, remap_ref, upward_ref, surface_ref, out_ref, geo_ref, x_ref, sums_ref, geo_sums_ref, sems = refs
+    scales_ref, remap_ref, upward_ref, surface_ref, out_ref, geo_ref, sums_ref, geo_sums_ref, sems = refs
     p, lev = par_ref[0], par_ref[2]
     count, column = sums_ref.shape[-2:]
+    level = lax.broadcasted_iota(jnp.int32, (count, count), 1)
+    within, group = level % z.half, level // z.half
+    for i in range(len(got)):
+        start = jnp.bitwise_xor(lev, i % parts) * z.levels + (1 - p if i < parts else p) * z.half
+        level = jnp.where(group == i, start + within, level)
+    order = jnp.where(lax.broadcasted_iota(jnp.int32, (count, count), 0) == level, 1.0, 0.0).astype(jnp.bfloat16)
     high, low = split(remap_ref[...])
+    rows = jnp.concatenate([high, low, upward_ref[...].astype(jnp.bfloat16)], axis=0)
+    rows = jnp.dot(rows, order, preferred_element_type=jnp.float32).astype(jnp.bfloat16)
+    high, low, upward = (rows[i * count : (i + 1) * count] for i in range(3))
     remap = jnp.concatenate([high, low, high], axis=1)
-    both = jnp.concatenate([remap, upward_ref[...].astype(jnp.bfloat16)], axis=0)
+    both = jnp.concatenate([remap, jnp.concatenate([upward, jnp.zeros_like(upward), upward], axis=1)], axis=0)
     scales = [
         scales_ref[far.index(i)] if i in far else decoder(ref[:, z.rows * column :])
         for i, ref in enumerate(got)
     ]
     copies = []
     for row in range(z.rows):
+        tiles = []
         for i, ref in enumerate(got):
-            side = 1 - p if i < parts else p
-            s = jnp.bitwise_xor(lev, i % parts)
             codes = ref[:, row * column : (row + 1) * column].astype(jnp.int32).astype(jnp.float32)
-            values = codes * tiled(scales[i], column)
-            level = pl.multiple_of(s * z.levels + side * z.half, z.half)
-            for f in range(2):
-                x_ref[row, f, pl.ds(level, z.half)] = values[f * z.half : (f + 1) * z.half]
+            tiles.append(codes * tiled(scales[i], column))
         for f in range(2):
-            high, low = split(x_ref[row, f])
+            high, low = split(jnp.concatenate([t[f * z.half : (f + 1) * z.half] for t in tiles], axis=0))
             stacked = jnp.concatenate([high, high, low], axis=0)
             result = jnp.dot(both if f else remap, stacked, preferred_element_type=jnp.float32)
             sums_ref[f, row] = result[:count]
@@ -688,7 +693,7 @@
 
     count = remap_weights.shape[0]
     upward = np.triu(np.ones((count, count), np.float32), 1) + 0.5 * np.eye(count, dtype=np.float32)
-    upward = jnp.asarray(np.concatenate([upward, 0.0 * upward, upward], axis=1))
+    upward = jnp.asarray(upward)
     surface = lax.dynamic_slice_in_dim(surface, lev * column, column, 1)
     remapped, geopotential = pl.pallas_call(
         functools.partial(column_kernel, z, parts, far),
@@ -697,7 +702,6 @@
         out_specs=[far_memory()] * 2,
         out_shape=[shape(2, rows, count, column), shape(rows, count, column)],
         scratch_shapes=[
-            pltpu.VMEM((rows, 2, count, column), f32),
             pltpu.VMEM((2, rows, count, column), f32),
             pltpu.VMEM((rows, count, column), f32),
             pltpu.SemaphoreType.DMA((3 * rows,)),

time: 51.4 us -> 51.3 us (level)
  no operation moved by 1% of the time
where the time goes in v3:
time: 51.3 us; the launch traced here: 50.7 us
  starting transfers between devices  21.4 us (42%)
  Pallas kernels  14.7 us (29%)
  waiting for transfers between devices  11.2 us (22%)
  local copies, waits for them, and re-layouts  2.59 us (5%)
  between operations  0.78 us (2%)
    ppermute x7, starting transfers between devices, shards(): lax.ppermute(block, ('lat', 'lev'), pairs)  9.3 us
    ppermute x7, waiting for transfers between devices, shards(): lax.ppermute(block, ('lat', 'lev'), pairs)  5.23 us
    ppermute x1, starting transfers between devices, shards(): far = lax.ppermute(edge, 'lat', far_pairs)  3.22 us
    pallas_call x2, Pallas kernels, outer(): pl.pallas_call(functools.partial(kernel, z, parts), name=name, in_specs=[...  3.16 us
    unnamed x16, local copies, waits for them, and re-layouts  2.57 us
    pallas_call x1, Pallas kernels, shards(): pl.pallas_call(functools.partial(column_kernel, z, parts, far), name='col...  2.48 us
    pallas_call x1, Pallas kernels, shards(): pl.pallas_call(functools.partial(inner_kernel, z), name='inner', in_specs...  2.35 us
    pallas_call x1, Pallas kernels, shards(): pl.pallas_call(functools.partial(own_kernel, z), name='own', in_specs=[sc...  2.24 us
  transfers between devices with their start and end apart: 14, of which 7 were waited for; matrix products, arithmetic and copies ran while one was open for 0% of the time, Pallas kernels for 14%

profile of v3, /device:TPU:17, one launch (start us, length us, event | category | flops | bytes accessed | tf_op | source)
XLA Modules:
  0.0 50.7 jit_solution(9882571776549872647)
XLA Ops:
  0.6 0.0 copy-start
  0.6 1.9 %edge.1 = s16[16,7936]{1,0:T(8,128)(2,1)} custom-call(f32[2,4,16,3072]{3,2,1,0:T(8,128)} %fields_ref.5, bf16[2,4,16,3072]{3,2,1,0:T(8,128)(2,1)} %courant_ref.7), custom_call_target="tpu_custom_call" | custom-call | flops 1000 | bytes 1000 | tf_op jit(solution)/shard_map/edge/pallas_call | solution.py:579
  2.5 1.3 %collective-permute-start = (s16[16,7936]{1,0:T(8,128)(2,1)}, s16[16,7936]{1,0:T(8,128)(2,1)S(1)}, u32[]{:S(2)}, u32[]{:S(2)}) collective-permute-start(s16[16,7936]{1,0:T(8,128)(2,1)} %edge.1), channel_id=1, source_target_pairs={{0,4},{4,0},{8,12},{12,8},{16,20},{20,16},{24,28},{28,24},{1,5},{5... | collective-permute-start | bytes 761864 | tf_op jit(solution)/shard_map/ppermute | solution.py:593
  3.8 0.1 pad_add_fusion.par_ref
  3.9 0.0 copy-start.2
  3.9 1.4 %copy-done.2 = f32[2,4,16,3072]{3,2,1,0:T(8,128)S(1)} copy-done((f32[2,4,16,3072]{3,2,1,0:T(8,128)S(1)}, f32[2,4,16,3072]{3,2,1,0:T(8,128)}, u32[]{:S(2)}) %copy-start.2) | copy-done | bytes 1572888
  5.3 1.1 %copy-done.3 = bf16[2,4,16,3072]{3,2,1,0:T(8,128)(2,1)S(1)} copy-done((bf16[2,4,16,3072]{3,2,1,0:T(8,128)(2,1)S(1)}, bf16[2,4,16,3072]{3,2,1,0:T(8,128)(2,1)}, u32[]{:S(2)}) %copy-start.3) | copy-done | bytes 786456
  6.4 1.0 %rest.1 = (s16[16,9472]{1,0:T(8,128)(2,1)S(1)}, s16[16,7680]{1,0:T(8,128)(2,1)S(1)}, s16[16,7936]{1,0:T(8,128)(2,1)S(1)}) custom-call(s32[4]{0:T(128)S(1)} %pad_add_fusion.par_ref, f32[2,4,16,3072]{3,2,1,0:T(8,128)S(1)} %copy-done.2, bf16[2,4,16,3072]{3,2,1,0:T(8,128)(2,1)S(1)} %copy-done.3), custom_call_target="tpu_custom_call" | custom-call | flops 1000 | bytes 1000 | tf_op jit(solution)/shard_map/rest/pallas_call | solution.py:594
  7.4 0.3 collective-permute-start.1
  7.7 2.1 %collective-permute-start.2 = (s16[16,7936]{1,0:T(8,128)(2,1)S(1)}, s16[16,7936]{1,0:T(8,128)(2,1)S(1)}, u32[]{:S(2)}, u32[]{:S(2)}) collective-permute-start(s16[16,7936]{1,0:T(8,128)(2,1)S(1)} %get-tuple-element.28), channel_id=1, source_target_pairs={{8,0},{4,12},{16,8},{12,20},{24,16},{20,28},{9,1},{5,13},{17,9},{1... | collective-permute-start | bytes 761864 | tf_op jit(solution)/shard_map/ppermute | solution.py:603
  9.8 0.0 collective-permute-done.edge_ref
  9.8 3.2 %collective-permute-start.3 = (s16[16,7936]{1,0:T(8,128)(2,1)S(1)}, s16[16,7936]{1,0:T(8,128)(2,1)S(1)}, u32[]{:S(2)}, u32[]{:S(2)}) collective-permute-start(s16[16,7936]{1,0:T(8,128)(2,1)S(1)} %collective-permute-done.edge_ref), channel_id=1, source_target_pairs={{0,8},{12,4},{8,16},{20,12},{16,24},{28,20},{1,9},{13,5},{9,17},{2... | collective-permute-start | bytes 761864 | tf_op jit(solution)/shard_map/ppermute | solution.py:605
  13.0 0.0 copy-start.4
  13.1 1.3 %collective-permute-start.4 = (s16[16,7680]{1,0:T(8,128)(2,1)S(1)}, s16[16,7680]{1,0:T(8,128)(2,1)S(1)}, u32[]{:S(2)}, u32[]{:S(2)}) collective-permute-start(s16[16,7680]{1,0:T(8,128)(2,1)S(1)} %get-tuple-element.30), channel_id=1, source_target_pairs={{0,4},{4,0},{8,12},{12,8},{16,20},{20,16},{24,28},{28,24},{1,5},{5... | collective-permute-start | bytes 737288 | tf_op jit(solution)/shard_map/ppermute | solution.py:606
  14.3 1.7 %collective-permute-done.2.near_ref = s16[16,7936]{1,0:T(8,128)(2,1)S(1)} collective-permute-done((s16[16,7936]{1,0:T(8,128)(2,1)S(1)}, s16[16,7936]{1,0:T(8,128)(2,1)S(1)}, u32[]{:S(2)}, u32[]{:S(2)}) %collective-permute-start.2) | collective-permute-done | bytes 253984 | tf_op jit(solution)/shard_map/ppermute | solution.py:603
  16.0 0.7 %collective-permute-done.1.middle_ref = s16[16,9472]{1,0:T(8,128)(2,1)S(1)} collective-permute-done((s16[16,9472]{1,0:T(8,128)(2,1)S(1)}, s16[16,9472]{1,0:T(8,128)(2,1)S(1)}, u32[]{:S(2)}, u32[]{:S(2)}) %collective-permute-start.1) | collective-permute-done | bytes 303136 | tf_op jit(solution)/shard_map/ppermute | solution.py:604
  16.7 0.4 collective-permute-done.3.far_ref
  17.1 2.2 %own.1 = (f32[4,2,8,3328]{3,2,1,0:T(8,128)S(1)}, f32[13,8,3072]{2,1,0:T(8,128)S(1)}, s16[16,6400]{1,0:T(8,128)(2,1)S(1)}, f32[12,2,8,3328]{3,2,1,0:T(8,128)S(1)}) custom-call(s32[4]{0:T(128)S(1)} %pad_add_fusion.par_ref, f32[2,4,16,3072]{3,2,1,0:T(8,128)S(1)} %copy-done.2, bf16[2,4,16,3072]{3,2,1,0:T(8,128)(2,1)S(1)} %copy-done.3, ...), custom_call_target="tpu_custom_call" | custom-call | flops 1000 | bytes 1000 | tf_op jit(solution)/shard_map/own/pallas_call | solution.py:612
  19.4 1.9 %collective-permute-done.4.last_ref = s16[16,7680]{1,0:T(8,128)(2,1)S(1)} collective-permute-done((s16[16,7680]{1,0:T(8,128)(2,1)S(1)}, s16[16,7680]{1,0:T(8,128)(2,1)S(1)}, u32[]{:S(2)}, u32[]{:S(2)}) %collective-permute-start.4) | collective-permute-done | bytes 245792 | tf_op jit(solution)/shard_map/ppermute | solution.py:606
  21.3 0.0 copy-done.4
  21.3 1.6 %other.1 = (f32[2,2,8,3328]{3,2,1,0:T(8,128)S(1)}, f32[13,8,3072]{2,1,0:T(8,128)S(1)}, s16[16,6400]{1,0:T(8,128)(2,1)S(1)}, s16[16,6400]{1,0:T(8,128)(2,1)S(1)}) custom-call(s32[4]{0:T(128)S(1)} %pad_add_fusion.par_ref, bf16[2,4,16,3072]{3,2,1,0:T(8,128)(2,1)S(1)} %copy-done.4, s16[16,7936]{1,0:T(8,128)(2,1)S(1)} %collective-permute-done.edge_ref, ...), custom_call_target="tpu_custom_call" | custom-call | flops 1000 | bytes 1000 | tf_op jit(solution)/shard_map/other/pallas_call | solution.py:627
  22.9 2.1 %collective-permute-start.6 = (s16[16,6400]{1,0:T(8,128)(2,1)S(1)}, s16[16,6400]{1,0:T(8,128)(2,1)S(1)}, u32[]{:S(2)}, u32[]{:S(2)}) collective-permute-start(s16[16,6400]{1,0:T(8,128)(2,1)S(1)} %get-tuple-element.39), channel_id=1, source_target_pairs={{0,8},{8,0},{4,12},{12,4},{16,24},{24,16},{20,28},{28,20},{1,9},{9... | collective-permute-start | bytes 614408 | tf_op jit(solution)/shard_map/ppermute | solution.py:642
  25.0 1.9 %collective-permute-start.5 = (s16[16,6400]{1,0:T(8,128)(2,1)S(1)}, s16[16,6400]{1,0:T(8,128)(2,1)S(1)}, u32[]{:S(2)}, u32[]{:S(2)}) collective-permute-start(s16[16,6400]{1,0:T(8,128)(2,1)S(1)} %get-tuple-element.38), channel_id=1, source_target_pairs={{8,16},{16,8},{12,20},{20,12},{9,17},{17,9},{13,21},{21,13},{10,18... | collective-permute-start | bytes 614408 | tf_op jit(solution)/shard_map/ppermute | solution.py:643
  26.9 0.0 copy-done.1
  26.9 0.0 copy-done.7
  26.9 2.4 %inner.1 = (f32[8,2,8,3328]{3,2,1,0:T(8,128)S(1)}, f32[4,2,8,3072]{3,2,1,0:T(8,128)S(1)}) custom-call(s32[4]{0:T(128)S(1)} %pad_add_fusion.par_ref, s32[32]{0:T(128)S(1)} %copy-done.7, f32[4,2,8,3328]{3,2,1,0:T(8,128)S(1)} %get-tuple-element.29.own_ref, f32[2,2,8,3328]{3,2,1,0:T(8,128)S(1)} %get-tuple-element.33.other_ref, ...), custom_call_target="tpu_custom_call" | custom-call | flops 1000 | bytes 1000 | tf_op jit(solution)/shard_map/inner/pallas_call | solution.py:646
  29.3 0.0 collective-permute-done.6.one_ref
  29.3 1.6 %early.1 = (s16[16,3200]{1,0:T(8,128)(2,1)S(1)}, s16[16,3200]{1,0:T(8,128)(2,1)S(1)}, s16[16,3200]{1,0:T(8,128)(2,1)S(1)}, s16[16,3200]{1,0:T(8,128)(2,1)S(1)}) custom-call(s32[4]{0:T(128)S(1)} %pad_add_fusion.par_ref, s32[32]{0:T(128)S(1)} %copy-done.7, f32[8,2,8,3328]{3,2,1,0:T(8,128)S(1)} %get-tuple-element.36.new_ref, ...), custom_call_target="tpu_custom_call" | custom-call | flops 1000 | bytes 1000 | tf_op jit(solution)/shard_map/early/pallas_call | solution.py:659
  30.9 1.2 %collective-permute-done.5.two_ref = s16[16,6400]{1,0:T(8,128)(2,1)S(1)} collective-permute-done((s16[16,6400]{1,0:T(8,128)(2,1)S(1)}, s16[16,6400]{1,0:T(8,128)(2,1)S(1)}, u32[]{:S(2)}, u32[]{:S(2)}) %collective-permute-start.5) | collective-permute-done | bytes 204832 | tf_op jit(solution)/shard_map/ppermute | solution.py:643
  32.0 1.6 %late.1 = (s16[16,3200]{1,0:T(8,128)(2,1)S(1)}, s16[16,3200]{1,0:T(8,128)(2,1)S(1)}, s16[16,3200]{1,0:T(8,128)(2,1)S(1)}, s16[16,3200]{1,0:T(8,128)(2,1)S(1)}, s...) custom-call(s32[4]{0:T(128)S(1)} %pad_add_fusion.par_ref, ...), custom_call_target="tpu_custom_call" | custom-call | flops 1000 | bytes 1000 | tf_op jit(solution)/shard_map/late/pallas_call | solution.py:659
  33.6 1.3 %collective-permute-start.12 = (s16[16,3200]{1,0:T(8,128)(2,1)S(1)}, s16[16,3200]{1,0:T(8,128)(2,1)S(1)}, u32[]{:S(2)}, u32[]{:S(2)}) collective-permute-start(s16[16,3200]{1,0:T(8,128)(2,1)S(1)} %get-tuple-element.50), channel_id=1, source_target_pairs={{0,2},{1,3},{2,0},{3,1},{4,6},{5,7},{6,4},{7,5},{8,10},{9,11},{10,... | collective-permute-start | bytes 307208 | tf_op jit(solution)/shard_map/ppermute | solution.py:682
  34.9 0.2 collective-permute-start.7
  35.2 1.2 %collective-permute-start.9 = (s16[16,3200]{1,0:T(8,128)(2,1)S(1)}, s16[16,3200]{1,0:T(8,128)(2,1)S(1)}, u32[]{:S(2)}, u32[]{:S(2)}) collective-permute-start(s16[16,3200]{1,0:T(8,128)(2,1)S(1)} %get-tuple-element.46), channel_id=1, source_target_pairs={{0,6},{1,7},{2,4},{3,5},{4,2},{5,3},{6,0},{7,1},{8,14},{9,15},{10,... | collective-permute-start | bytes 307208 | tf_op jit(solution)/shard_map/ppermute | solution.py:682
  36.4 4.9 %collective-permute-start.10 = (s16[16,3200]{1,0:T(8,128)(2,1)S(1)}, s16[16,3200]{1,0:T(8,128)(2,1)S(1)}, u32[]{:S(2)}, u32[]{:S(2)}) collective-permute-start(s16[16,3200]{1,0:T(8,128)(2,1)S(1)} %get-tuple-element.47), channel_id=1, source_target_pairs={{0,7},{1,6},{2,5},{3,4},{4,3},{5,2},{6,1},{7,0},{8,15},{9,14},{10,... | collective-permute-start | bytes 307208 | tf_op jit(solution)/shard_map/ppermute | solution.py:682
  41.2 0.0 collective-permute-start.11
  41.2 0.0 collective-permute-done.12.refs_2_.refs_6_
  41.2 1.2 %collective-permute-start.13 = (s16[16,3200]{1,0:T(8,128)(2,1)S(1)}, s16[16,3200]{1,0:T(8,128)(2,1)S(1)}, u32[]{:S(2)}, u32[]{:S(2)}) collective-permute-start(s16[16,3200]{1,0:T(8,128)(2,1)S(1)} %get-tuple-element.51), channel_id=1, source_target_pairs={{0,3},{1,2},{2,1},{3,0},{4,7},{5,6},{6,5},{7,4},{8,11},{9,10},{10,... | collective-permute-start | bytes 307208 | tf_op jit(solution)/shard_map/ppermute | solution.py:682
  42.4 0.0 collective-permute-done.7.refs_0_
  42.4 0.5 %collective-permute-start.8 = (s16[16,3200]{1,0:T(8,128)(2,1)S(1)}, s16[16,3200]{1,0:T(8,128)(2,1)S(1)}, u32[]{:S(2)}, u32[]{:S(2)}) collective-permute-start(s16[16,3200]{1,0:T(8,128)(2,1)S(1)} %get-tuple-element.45), channel_id=1, source_target_pairs={{0,5},{1,4},{2,7},{3,6},{4,1},{5,0},{6,3},{7,2},{8,13},{9,12},{10,... | collective-permute-start | bytes 307208 | tf_op jit(solution)/shard_map/ppermute | solution.py:682
  43.0 0.0 copy-done
  43.0 0.0 collective-permute-done.9.refs_1_.refs_2_
  43.0 3.3 %collective-permute-done.10.refs_3_ = s16[16,3200]{1,0:T(8,128)(2,1)S(1)} collective-permute-done((s16[16,3200]{1,0:T(8,128)(2,1)S(1)}, s16[16,3200]{1,0:T(8,128)(2,1)S(1)}, u32[]{:S(2)}, u32[]{:S(2)}) %collective-permute-start.10) | collective-permute-done | bytes 102432 | tf_op jit(solution)/shard_map/ppermute | solution.py:682
  46.3 0.0 collective-permute-done.11.refs_5_
  46.3 1.9 %collective-permute-done.13.refs_7_ = s16[16,3200]{1,0:T(8,128)(2,1)S(1)} collective-permute-done((s16[16,3200]{1,0:T(8,128)(2,1)S(1)}, s16[16,3200]{1,0:T(8,128)(2,1)S(1)}, u32[]{:S(2)}, u32[]{:S(2)}) %collective-permute-start.13) | collective-permute-done | bytes 102432 | tf_op jit(solution)/shard_map/ppermute | solution.py:682
  48.2 0.0 collective-permute-done.8.refs_1_
  48.2 0.0 copy-done.5
  48.2 0.0 copy-done.6
  48.2 2.5 %columns.1 = (f32[2,4,64,768]{3,2,1,0:T(8,128)}, f32[4,64,768]{2,1,0:T(8,128)}) custom-call(s32[4]{0:T(128)S(1)} %pad_add_fusion.par_ref, s16[16,3200]{1,0:T(8,128)(2,1)S(1)} %collective-permute-done.7.refs_0_, s16[16,3200]{1,0:T(8,128)(2,1)S(1)} %collective-permute-done.8.refs_1_, s16[16,3200]{1,0:T(8,128)(2,1)S(1)} %collective-permute-done.9.refs_1_.refs_2_, ...), custom_call_target="tpu_custom_call" | custom-call | flops 1000 | bytes 1000 | tf_op jit(solution)/shard_map/columns/pallas_call | solution.py:698
  (8 shorter events, 0.0 us)
Async XLA Ops:
  0.6 42.3 %copy-start = (f32[4,3072]{1,0:T(4,128)S(1)}, f32[4,3072]{1,0:T(4,128)}, u32[]{:S(2)}) copy-start(f32[4,3072]{1,0:T(4,128)} %param.10) | copy-start | bytes 147460
  2.5 7.3 %collective-permute-start = (s16[16,7936]{1,0:T(8,128)(2,1)}, s16[16,7936]{1,0:T(8,128)(2,1)S(1)}, u32[]{:S(2)}, u32[]{:S(2)}) collective-permute-start(s16[16,7936]{1,0:T(8,128)(2,1)} %edge.1), channel_id=1, source_target_pairs={{0,4},{4,0},{8,12},{12,8},{16,20},{20,16},{24,28},{28,24},{1,5},{5... | collective-permute-start | bytes 761864 | tf_op jit(solution)/shard_map/ppermute | solution.py:593
  3.9 1.4 %copy-start.2 = (f32[2,4,16,3072]{3,2,1,0:T(8,128)S(1)}, f32[2,4,16,3072]{3,2,1,0:T(8,128)}, u32[]{:S(2)}) copy-start(f32[2,4,16,3072]{3,2,1,0:T(8,128)} %fields_ref.5) | copy-start | bytes 4718596
  5.3 1.1 %copy-start.3 = (bf16[2,4,16,3072]{3,2,1,0:T(8,128)(2,1)S(1)}, bf16[2,4,16,3072]{3,2,1,0:T(8,128)(2,1)}, u32[]{:S(2)}) copy-start(bf16[2,4,16,3072]{3,2,1,0:T(8,128)(2,1)} %courant_ref.7) | copy-start | bytes 2359300
  7.4 9.3 %collective-permute-start.1 = (s16[16,9472]{1,0:T(8,128)(2,1)S(1)}, s16[16,9472]{1,0:T(8,128)(2,1)S(1)}, u32[]{:S(2)}, u32[]{:S(2)}) collective-permute-start(s16[16,9472]{1,0:T(8,128)(2,1)S(1)} %get-tuple-element.27), channel_id=1, source_target_pairs={{0,4},{4,0},{8,12},{12,8},{16,20},{20,16},{24,28},{28,24},{1,5},{5... | collective-permute-start | bytes 909320 | tf_op jit(solution)/shard_map/ppermute | solution.py:604
  7.7 8.3 %collective-permute-start.2 = (s16[16,7936]{1,0:T(8,128)(2,1)S(1)}, s16[16,7936]{1,0:T(8,128)(2,1)S(1)}, u32[]{:S(2)}, u32[]{:S(2)}) collective-permute-start(s16[16,7936]{1,0:T(8,128)(2,1)S(1)} %get-tuple-element.28), channel_id=1, source_target_pairs={{8,0},{4,12},{16,8},{12,20},{24,16},{20,28},{9,1},{5,13},{17,9},{1... | collective-permute-start | bytes 761864 | tf_op jit(solution)/shard_map/ppermute | solution.py:603
  9.8 7.3 %collective-permute-start.3 = (s16[16,7936]{1,0:T(8,128)(2,1)S(1)}, s16[16,7936]{1,0:T(8,128)(2,1)S(1)}, u32[]{:S(2)}, u32[]{:S(2)}) collective-permute-start(s16[16,7936]{1,0:T(8,128)(2,1)S(1)} %collective-permute-done.edge_ref), channel_id=1, source_target_pairs={{0,8},{12,4},{8,16},{20,12},{16,24},{28,20},{1,9},{13,5},{9,17},{2... | collective-permute-start | bytes 761864 | tf_op jit(solution)/shard_map/ppermute | solution.py:605
  13.0 8.3 %copy-start.4 = (bf16[2,4,16,3072]{3,2,1,0:T(8,128)(2,1)S(1)}, bf16[2,4,16,3072]{3,2,1,0:T(8,128)(2,1)}, u32[]{:S(2)}) copy-start(bf16[2,4,16,3072]{3,2,1,0:T(8,128)(2,1)} %courant_ref.7) | copy-start | bytes 2359300
  13.1 8.3 %collective-permute-start.4 = (s16[16,7680]{1,0:T(8,128)(2,1)S(1)}, s16[16,7680]{1,0:T(8,128)(2,1)S(1)}, u32[]{:S(2)}, u32[]{:S(2)}) collective-permute-start(s16[16,7680]{1,0:T(8,128)(2,1)S(1)} %get-tuple-element.30), channel_id=1, source_target_pairs={{0,4},{4,0},{8,12},{12,8},{16,20},{20,16},{24,28},{28,24},{1,5},{5... | collective-permute-start | bytes 737288 | tf_op jit(solution)/shard_map/ppermute | solution.py:606
  21.3 5.6 %copy-start.1 = (bf16[4,1536,256]{2,1,0:T(8,128)(2,1)S(1)}, bf16[4,1536,256]{2,1,0:T(8,128)(2,1)}, u32[]{:S(2)}) copy-start(bf16[4,1536,256]{2,1,0:T(8,128)(2,1)} %constant.48.clone.table_ref) | copy-start | bytes 9437188
  21.3 5.6 %copy-start.7 = (s32[32]{0:T(128)S(1)}, s32[32]{0:T(128)}, u32[]{:S(2)}) copy-start(s32[32]{0:T(128)} %cut_ref.5) | copy-start | bytes 388
  22.9 6.4 %collective-permute-start.6 = (s16[16,6400]{1,0:T(8,128)(2,1)S(1)}, s16[16,6400]{1,0:T(8,128)(2,1)S(1)}, u32[]{:S(2)}, u32[]{:S(2)}) collective-permute-start(s16[16,6400]{1,0:T(8,128)(2,1)S(1)} %get-tuple-element.39), channel_id=1, source_target_pairs={{0,8},{8,0},{4,12},{12,4},{16,24},{24,16},{20,28},{28,20},{1,9},{9... | collective-permute-start | bytes 614408 | tf_op jit(solution)/shard_map/ppermute | solution.py:642
  25.0 7.1 %collective-permute-start.5 = (s16[16,6400]{1,0:T(8,128)(2,1)S(1)}, s16[16,6400]{1,0:T(8,128)(2,1)S(1)}, u32[]{:S(2)}, u32[]{:S(2)}) collective-permute-start(s16[16,6400]{1,0:T(8,128)(2,1)S(1)} %get-tuple-element.38), channel_id=1, source_target_pairs={{8,16},{16,8},{12,20},{20,12},{9,17},{17,9},{13,21},{21,13},{10,18... | collective-permute-start | bytes 614408 | tf_op jit(solution)/shard_map/ppermute | solution.py:643
  32.0 16.2 %copy-start.5 = (f32[64,64]{1,0:T(8,128)S(1)}, f32[64,64]{1,0:T(8,128)}, u32[]{:S(2)}) copy-start(f32[64,64]{1,0:T(8,128)} %refs_9_.1) | copy-start | bytes 49156
  32.0 16.2 %copy-start.6 = (f32[64,64]{1,0:T(8,128)S(1)}, f32[64,64]{1,0:T(8,128)}, u32[]{:S(2)}) copy-start(f32[64,64]{1,0:T(8,128)} %constant.49.clone.refs_10_) | copy-start | bytes 49156
  33.6 7.6 %collective-permute-start.12 = (s16[16,3200]{1,0:T(8,128)(2,1)S(1)}, s16[16,3200]{1,0:T(8,128)(2,1)S(1)}, u32[]{:S(2)}, u32[]{:S(2)}) collective-permute-start(s16[16,3200]{1,0:T(8,128)(2,1)S(1)} %get-tuple-element.50), channel_id=1, source_target_pairs={{0,2},{1,3},{2,0},{3,1},{4,6},{5,7},{6,4},{7,5},{8,10},{9,11},{10,... | collective-permute-start | bytes 307208 | tf_op jit(solution)/shard_map/ppermute | solution.py:682
  34.9 7.5 %collective-permute-start.7 = (s16[16,3200]{1,0:T(8,128)(2,1)S(1)}, s16[16,3200]{1,0:T(8,128)(2,1)S(1)}, u32[]{:S(2)}, u32[]{:S(2)}) collective-permute-start(s16[16,3200]{1,0:T(8,128)(2,1)S(1)} %get-tuple-element.44), channel_id=1, source_target_pairs={{0,4},{1,5},{2,6},{3,7},{4,0},{5,1},{6,2},{7,3},{8,12},{9,13},{10,... | collective-permute-start | bytes 307208 | tf_op jit(solution)/shard_map/ppermute | solution.py:682
  35.2 7.8 %collective-permute-start.9 = (s16[16,3200]{1,0:T(8,128)(2,1)S(1)}, s16[16,3200]{1,0:T(8,128)(2,1)S(1)}, u32[]{:S(2)}, u32[]{:S(2)}) collective-permute-start(s16[16,3200]{1,0:T(8,128)(2,1)S(1)} %get-tuple-element.46), channel_id=1, source_target_pairs={{0,6},{1,7},{2,4},{3,5},{4,2},{5,3},{6,0},{7,1},{8,14},{9,15},{10,... | collective-permute-start | bytes 307208 | tf_op jit(solution)/shard_map/ppermute | solution.py:682
  36.4 10.0 %collective-permute-start.10 = (s16[16,3200]{1,0:T(8,128)(2,1)S(1)}, s16[16,3200]{1,0:T(8,128)(2,1)S(1)}, u32[]{:S(2)}, u32[]{:S(2)}) collective-permute-start(s16[16,3200]{1,0:T(8,128)(2,1)S(1)} %get-tuple-element.47), channel_id=1, source_target_pairs={{0,7},{1,6},{2,5},{3,4},{4,3},{5,2},{6,1},{7,0},{8,15},{9,14},{10,... | collective-permute-start | bytes 307208 | tf_op jit(solution)/shard_map/ppermute | solution.py:682
  41.2 5.1 %collective-permute-start.11 = (s16[16,3200]{1,0:T(8,128)(2,1)S(1)}, s16[16,3200]{1,0:T(8,128)(2,1)S(1)}, u32[]{:S(2)}, u32[]{:S(2)}) collective-permute-start(s16[16,3200]{1,0:T(8,128)(2,1)S(1)} %get-tuple-element.49), channel_id=1, source_target_pairs={{0,1},{1,0},{2,3},{3,2},{4,5},{5,4},{6,7},{7,6},{8,9},{9,8},{10,11... | collective-permute-start | bytes 307208 | tf_op jit(solution)/shard_map/ppermute | solution.py:682
  41.2 7.0 %collective-permute-start.13 = (s16[16,3200]{1,0:T(8,128)(2,1)S(1)}, s16[16,3200]{1,0:T(8,128)(2,1)S(1)}, u32[]{:S(2)}, u32[]{:S(2)}) collective-permute-start(s16[16,3200]{1,0:T(8,128)(2,1)S(1)} %get-tuple-element.51), channel_id=1, source_target_pairs={{0,3},{1,2},{2,1},{3,0},{4,7},{5,6},{6,5},{7,4},{8,11},{9,10},{10,... | collective-permute-start | bytes 307208 | tf_op jit(solution)/shard_map/ppermute | solution.py:682
  42.4 5.8 %collective-permute-start.8 = (s16[16,3200]{1,0:T(8,128)(2,1)S(1)}, s16[16,3200]{1,0:T(8,128)(2,1)S(1)}, u32[]{:S(2)}, u32[]{:S(2)}) collective-permute-start(s16[16,3200]{1,0:T(8,128)(2,1)S(1)} %get-tuple-element.45), channel_id=1, source_target_pairs={{0,5},{1,4},{2,7},{3,6},{4,1},{5,0},{6,3},{7,2},{8,13},{9,12},{10,... | collective-permute-start | bytes 307208 | tf_op jit(solution)/shard_map/ppermute | solution.py:682

commit v4 on v3

--- a/solution.py
+++ b/solution.py
@@ -18,7 +18,7 @@
 WIND = 81920.0
 ROUND = 1.5 * 2.0**23
 VMEM_LIMIT = 12 * 2**20
-VMEM_MOST = 63 * 2**20 + 2**19
+VMEM_MOST = 63 * 2**20
 
 
 def rounded(values):

time: 51.3 us -> 51 us (level)
  local copies, waits for them, and re-layouts: 2.59 us -> 1.45 us
  waiting for transfers between devices: 11.2 us -> 12.3 us
    unnamed x16 -> x14, local copies, waits for them, and re-layouts: 2.57 us -> 1.44 us
    ppermute x1, waiting for transfers between devices: 0.01 us -> 1.14 us  [shards(): edge = lax.ppermute(edge, 'lat', swap)]
    ppermute x1, starting transfers between devices: 1.27 us -> 0.16 us  [shards(): last = lax.ppermute(last, 'lat', swap)]
    ppermute x7, starting transfers between devices: 9.3 us -> 10.3 us  [shards(): lax.ppermute(block, ('lat', 'lev'), pairs)]
    ppermute x1, waiting for transfers between devices: 0.75 us -> 1.44 us  [shards(): middle = lax.ppermute(middle, 'lat', swap)]
    ppermute x1, waiting for transfers between devices: 1.17 us -> 0.59 us  [shards(): two = lax.ppermute(two, 'lat', twos)]
  transfers between devices with their start and end apart: 14 -> 14, of which waited for: 7 -> 8; matrix products, arithmetic and copies ran while one was open for 0% -> 0% of each run, Pallas kernels for 14% -> 14%
where the time goes in v4:
time: 51 us; the launch traced here: 50.7 us
  starting transfers between devices  21.3 us (42%)
  Pallas kernels  14.8 us (29%)
  waiting for transfers between devices  12.3 us (24%)
  local copies, waits for them, and re-layouts  1.45 us (3%)
  between operations  0.78 us (2%)
    ppermute x7, starting transfers between devices, shards(): lax.ppermute(block, ('lat', 'lev'), pairs)  10.3 us
    ppermute x7, waiting for transfers between devices, shards(): lax.ppermute(block, ('lat', 'lev'), pairs)  5.14 us
    ppermute x1, starting transfers between devices, shards(): far = lax.ppermute(edge, 'lat', far_pairs)  3.19 us
    pallas_call x2, Pallas kernels, outer(): pl.pallas_call(functools.partial(kernel, z, parts), name=name, in_specs=[...  3.16 us
    pallas_call x1, Pallas kernels, shards(): pl.pallas_call(functools.partial(column_kernel, z, parts, far), name='col...  2.48 us
    pallas_call x1, Pallas kernels, shards(): pl.pallas_call(functools.partial(inner_kernel, z), name='inner', in_specs...  2.36 us
    pallas_call x1, Pallas kernels, shards(): pl.pallas_call(functools.partial(own_kernel, z), name='own', in_specs=[sc...  2.26 us
    ppermute x1, starting transfers between devices, shards(): near = lax.ppermute(own, 'lat', near_pairs)  2.07 us
  transfers between devices with their start and end apart: 14, of which 8 were waited for; matrix products, arithmetic and copies ran while one was open for 0% of the time, Pallas kernels for 14%

profile of v4, /device:TPU:17, one launch (start us, length us, event | category | flops | bytes accessed | tf_op | source)
XLA Modules:
  0.0 50.7 jit_solution(3692022641893788059)
XLA Ops:
  0.6 0.0 copy-start
  0.6 0.0 copy-start.3
  0.7 2.0 %edge.1 = s16[16,7936]{1,0:T(8,128)(2,1)} custom-call(f32[2,4,16,3072]{3,2,1,0:T(8,128)} %fields_ref.5, bf16[2,4,16,3072]{3,2,1,0:T(8,128)(2,1)} %courant_ref.7), custom_call_target="tpu_custom_call" | custom-call | flops 1000 | bytes 1000 | tf_op jit(solution)/shard_map/edge/pallas_call | solution.py:579
  2.6 1.3 %collective-permute-start = (s16[16,7936]{1,0:T(8,128)(2,1)}, s16[16,7936]{1,0:T(8,128)(2,1)S(1)}, u32[]{:S(2)}, u32[]{:S(2)}) collective-permute-start(s16[16,7936]{1,0:T(8,128)(2,1)} %edge.1), channel_id=1, source_target_pairs={{0,4},{4,0},{8,12},{12,8},{16,20},{20,16},{24,28},{28,24},{1,5},{5... | collective-permute-start | bytes 761864 | tf_op jit(solution)/shard_map/ppermute | solution.py:593
  3.9 0.1 pad_add_fusion.par_ref
  4.0 0.0 copy-done.3
  4.0 0.0 copy-start.2
  4.0 1.4 %copy-done.2 = f32[2,4,16,3072]{3,2,1,0:T(8,128)S(1)} copy-done((f32[2,4,16,3072]{3,2,1,0:T(8,128)S(1)}, f32[2,4,16,3072]{3,2,1,0:T(8,128)}, u32[]{:S(2)}) %copy-start.2) | copy-done | bytes 1572888
  5.4 1.0 %rest.1 = (s16[16,9472]{1,0:T(8,128)(2,1)S(1)}, s16[16,7680]{1,0:T(8,128)(2,1)S(1)}, s16[16,7936]{1,0:T(8,128)(2,1)S(1)}) custom-call(s32[4]{0:T(128)S(1)} %pad_add_fusion.par_ref, f32[2,4,16,3072]{3,2,1,0:T(8,128)S(1)} %copy-done.2, bf16[2,4,16,3072]{3,2,1,0:T(8,128)(2,1)S(1)} %copy-done.3), custom_call_target="tpu_custom_call" | custom-call | flops 1000 | bytes 1000 | tf_op jit(solution)/shard_map/rest/pallas_call | solution.py:594
  6.4 0.3 collective-permute-start.1
  6.7 2.1 %collective-permute-start.2 = (s16[16,7936]{1,0:T(8,128)(2,1)S(1)}, s16[16,7936]{1,0:T(8,128)(2,1)S(1)}, u32[]{:S(2)}, u32[]{:S(2)}) collective-permute-start(s16[16,7936]{1,0:T(8,128)(2,1)S(1)} %get-tuple-element.28), channel_id=1, source_target_pairs={{8,0},{4,12},{16,8},{12,20},{24,16},{20,28},{9,1},{5,13},{17,9},{1... | collective-permute-start | bytes 761864 | tf_op jit(solution)/shard_map/ppermute | solution.py:603
  8.8 1.1 %collective-permute-done.edge_ref = s16[16,7936]{1,0:T(8,128)(2,1)S(1)} collective-permute-done((s16[16,7936]{1,0:T(8,128)(2,1)}, s16[16,7936]{1,0:T(8,128)(2,1)S(1)}, u32[]{:S(2)}, u32[]{:S(2)}) %collective-permute-start) | collective-permute-done | bytes 253984 | tf_op jit(solution)/shard_map/ppermute | solution.py:593
  9.9 3.2 %collective-permute-start.3 = (s16[16,7936]{1,0:T(8,128)(2,1)S(1)}, s16[16,7936]{1,0:T(8,128)(2,1)S(1)}, u32[]{:S(2)}, u32[]{:S(2)}) collective-permute-start(s16[16,7936]{1,0:T(8,128)(2,1)S(1)} %collective-permute-done.edge_ref), channel_id=1, source_target_pairs={{0,8},{12,4},{8,16},{20,12},{16,24},{28,20},{1,9},{13,5},{9,17},{2... | collective-permute-start | bytes 761864 | tf_op jit(solution)/shard_map/ppermute | solution.py:605
  13.1 0.2 collective-permute-start.4
  13.3 1.7 %collective-permute-done.2.near_ref = s16[16,7936]{1,0:T(8,128)(2,1)S(1)} collective-permute-done((s16[16,7936]{1,0:T(8,128)(2,1)S(1)}, s16[16,7936]{1,0:T(8,128)(2,1)S(1)}, u32[]{:S(2)}, u32[]{:S(2)}) %collective-permute-start.2) | collective-permute-done | bytes 253984 | tf_op jit(solution)/shard_map/ppermute | solution.py:603
  15.0 1.4 %collective-permute-done.1.middle_ref = s16[16,9472]{1,0:T(8,128)(2,1)S(1)} collective-permute-done((s16[16,9472]{1,0:T(8,128)(2,1)S(1)}, s16[16,9472]{1,0:T(8,128)(2,1)S(1)}, u32[]{:S(2)}, u32[]{:S(2)}) %collective-permute-start.1) | collective-permute-done | bytes 303136 | tf_op jit(solution)/shard_map/ppermute | solution.py:604
  16.4 0.8 %collective-permute-done.3.far_ref = s16[16,7936]{1,0:T(8,128)(2,1)S(1)} collective-permute-done((s16[16,7936]{1,0:T(8,128)(2,1)S(1)}, s16[16,7936]{1,0:T(8,128)(2,1)S(1)}, u32[]{:S(2)}, u32[]{:S(2)}) %collective-permute-start.3) | collective-permute-done | bytes 253984 | tf_op jit(solution)/shard_map/ppermute | solution.py:605
  17.2 2.3 %own.1 = (f32[4,2,8,3328]{3,2,1,0:T(8,128)S(1)}, f32[13,8,3072]{2,1,0:T(8,128)S(1)}, s16[16,6400]{1,0:T(8,128)(2,1)S(1)}, f32[12,2,8,3328]{3,2,1,0:T(8,128)S(1)}) custom-call(s32[4]{0:T(128)S(1)} %pad_add_fusion.par_ref, f32[2,4,16,3072]{3,2,1,0:T(8,128)S(1)} %copy-done.2, bf16[2,4,16,3072]{3,2,1,0:T(8,128)(2,1)S(1)} %copy-done.3, ...), custom_call_target="tpu_custom_call" | custom-call | flops 1000 | bytes 1000 | tf_op jit(solution)/shard_map/own/pallas_call | solution.py:612
  19.5 1.5 %collective-permute-done.4.last_ref = s16[16,7680]{1,0:T(8,128)(2,1)S(1)} collective-permute-done((s16[16,7680]{1,0:T(8,128)(2,1)S(1)}, s16[16,7680]{1,0:T(8,128)(2,1)S(1)}, u32[]{:S(2)}, u32[]{:S(2)}) %collective-permute-start.4) | collective-permute-done | bytes 245792 | tf_op jit(solution)/shard_map/ppermute | solution.py:606
  21.0 0.0 copy-start.1
  21.0 1.6 %other.1 = (f32[2,2,8,3328]{3,2,1,0:T(8,128)S(1)}, f32[13,8,3072]{2,1,0:T(8,128)S(1)}, s16[16,6400]{1,0:T(8,128)(2,1)S(1)}, s16[16,6400]{1,0:T(8,128)(2,1)S(1)}) custom-call(s32[4]{0:T(128)S(1)} %pad_add_fusion.par_ref, bf16[2,4,16,3072]{3,2,1,0:T(8,128)(2,1)S(1)} %copy-done.3, s16[16,7936]{1,0:T(8,128)(2,1)S(1)} %collective-permute-done.edge_ref, ...), custom_call_target="tpu_custom_call" | custom-call | flops 1000 | bytes 1000 | tf_op jit(solution)/shard_map/other/pallas_call | solution.py:627
  22.6 2.0 %collective-permute-start.6 = (s16[16,6400]{1,0:T(8,128)(2,1)S(1)}, s16[16,6400]{1,0:T(8,128)(2,1)S(1)}, u32[]{:S(2)}, u32[]{:S(2)}) collective-permute-start(s16[16,6400]{1,0:T(8,128)(2,1)S(1)} %get-tuple-element.39), channel_id=1, source_target_pairs={{0,8},{8,0},{4,12},{12,4},{16,24},{24,16},{20,28},{28,20},{1,9},{9... | collective-permute-start | bytes 614408 | tf_op jit(solution)/shard_map/ppermute | solution.py:642
  24.6 1.9 %collective-permute-start.5 = (s16[16,6400]{1,0:T(8,128)(2,1)S(1)}, s16[16,6400]{1,0:T(8,128)(2,1)S(1)}, u32[]{:S(2)}, u32[]{:S(2)}) collective-permute-start(s16[16,6400]{1,0:T(8,128)(2,1)S(1)} %get-tuple-element.38), channel_id=1, source_target_pairs={{8,16},{16,8},{12,20},{20,12},{9,17},{17,9},{13,21},{21,13},{10,18... | collective-permute-start | bytes 614408 | tf_op jit(solution)/shard_map/ppermute | solution.py:643
  26.6 0.0 copy-done.1
  26.6 0.0 copy-done.6
  26.6 2.4 %inner.1 = (f32[8,2,8,3328]{3,2,1,0:T(8,128)S(1)}, f32[4,2,8,3072]{3,2,1,0:T(8,128)S(1)}) custom-call(s32[4]{0:T(128)S(1)} %pad_add_fusion.par_ref, s32[32]{0:T(128)S(1)} %copy-done.6, f32[4,2,8,3328]{3,2,1,0:T(8,128)S(1)} %get-tuple-element.29.own_ref, f32[2,2,8,3328]{3,2,1,0:T(8,128)S(1)} %get-tuple-element.33.other_ref, ...), custom_call_target="tpu_custom_call" | custom-call | flops 1000 | bytes 1000 | tf_op jit(solution)/shard_map/inner/pallas_call | solution.py:646
  28.9 0.0 collective-permute-done.6.one_ref
  29.0 1.6 %early.1 = (s16[16,3200]{1,0:T(8,128)(2,1)S(1)}, s16[16,3200]{1,0:T(8,128)(2,1)S(1)}, s16[16,3200]{1,0:T(8,128)(2,1)S(1)}, s16[16,3200]{1,0:T(8,128)(2,1)S(1)}) custom-call(s32[4]{0:T(128)S(1)} %pad_add_fusion.par_ref, s32[32]{0:T(128)S(1)} %copy-done.6, f32[8,2,8,3328]{3,2,1,0:T(8,128)S(1)} %get-tuple-element.36.new_ref, ...), custom_call_target="tpu_custom_call" | custom-call | flops 1000 | bytes 1000 | tf_op jit(solution)/shard_map/early/pallas_call | solution.py:659
  30.5 0.6 %collective-permute-done.5.two_ref = s16[16,6400]{1,0:T(8,128)(2,1)S(1)} collective-permute-done((s16[16,6400]{1,0:T(8,128)(2,1)S(1)}, s16[16,6400]{1,0:T(8,128)(2,1)S(1)}, u32[]{:S(2)}, u32[]{:S(2)}) %collective-permute-start.5) | collective-permute-done | bytes 204832 | tf_op jit(solution)/shard_map/ppermute | solution.py:643
  31.1 1.6 %late.1 = (s16[16,3200]{1,0:T(8,128)(2,1)S(1)}, s16[16,3200]{1,0:T(8,128)(2,1)S(1)}, s16[16,3200]{1,0:T(8,128)(2,1)S(1)}, s16[16,3200]{1,0:T(8,128)(2,1)S(1)}, s...) custom-call(s32[4]{0:T(128)S(1)} %pad_add_fusion.par_ref, ...), custom_call_target="tpu_custom_call" | custom-call | flops 1000 | bytes 1000 | tf_op jit(solution)/shard_map/late/pallas_call | solution.py:659
  32.7 1.3 %collective-permute-start.12 = (s16[16,3200]{1,0:T(8,128)(2,1)S(1)}, s16[16,3200]{1,0:T(8,128)(2,1)S(1)}, u32[]{:S(2)}, u32[]{:S(2)}) collective-permute-start(s16[16,3200]{1,0:T(8,128)(2,1)S(1)} %get-tuple-element.50), channel_id=1, source_target_pairs={{0,2},{1,3},{2,0},{3,1},{4,6},{5,7},{6,4},{7,5},{8,10},{9,11},{10,... | collective-permute-start | bytes 307208 | tf_op jit(solution)/shard_map/ppermute | solution.py:682
  34.0 1.2 %collective-permute-start.7 = (s16[16,3200]{1,0:T(8,128)(2,1)S(1)}, s16[16,3200]{1,0:T(8,128)(2,1)S(1)}, u32[]{:S(2)}, u32[]{:S(2)}) collective-permute-start(s16[16,3200]{1,0:T(8,128)(2,1)S(1)} %get-tuple-element.44), channel_id=1, source_target_pairs={{0,4},{1,5},{2,6},{3,7},{4,0},{5,1},{6,2},{7,3},{8,12},{9,13},{10,... | collective-permute-start | bytes 307208 | tf_op jit(solution)/shard_map/ppermute | solution.py:682
  35.2 0.2 collective-permute-start.9
  35.4 5.9 %collective-permute-start.10 = (s16[16,3200]{1,0:T(8,128)(2,1)S(1)}, s16[16,3200]{1,0:T(8,128)(2,1)S(1)}, u32[]{:S(2)}, u32[]{:S(2)}) collective-permute-start(s16[16,3200]{1,0:T(8,128)(2,1)S(1)} %get-tuple-element.47), channel_id=1, source_target_pairs={{0,7},{1,6},{2,5},{3,4},{4,3},{5,2},{6,1},{7,0},{8,15},{9,14},{10,... | collective-permute-start | bytes 307208 | tf_op jit(solution)/shard_map/ppermute | solution.py:682
  41.3 0.0 collective-permute-start.11
  41.3 0.0 collective-permute-done.12.refs_2_.refs_6_
  41.3 0.6 %collective-permute-start.13 = (s16[16,3200]{1,0:T(8,128)(2,1)S(1)}, s16[16,3200]{1,0:T(8,128)(2,1)S(1)}, u32[]{:S(2)}, u32[]{:S(2)}) collective-permute-start(s16[16,3200]{1,0:T(8,128)(2,1)S(1)} %get-tuple-element.51), channel_id=1, source_target_pairs={{0,3},{1,2},{2,1},{3,0},{4,7},{5,6},{6,5},{7,4},{8,11},{9,10},{10,... | collective-permute-start | bytes 307208 | tf_op jit(solution)/shard_map/ppermute | solution.py:682
  41.9 0.0 collective-permute-done.7.refs_0_
  41.9 1.1 %collective-permute-start.8 = (s16[16,3200]{1,0:T(8,128)(2,1)S(1)}, s16[16,3200]{1,0:T(8,128)(2,1)S(1)}, u32[]{:S(2)}, u32[]{:S(2)}) collective-permute-start(s16[16,3200]{1,0:T(8,128)(2,1)S(1)} %get-tuple-element.45), channel_id=1, source_target_pairs={{0,5},{1,4},{2,7},{3,6},{4,1},{5,0},{6,3},{7,2},{8,13},{9,12},{10,... | collective-permute-start | bytes 307208 | tf_op jit(solution)/shard_map/ppermute | solution.py:682
  43.0 0.0 copy-done
  43.1 0.0 collective-permute-done.9.refs_1_.refs_2_
  43.1 3.1 %collective-permute-done.10.refs_3_ = s16[16,3200]{1,0:T(8,128)(2,1)S(1)} collective-permute-done((s16[16,3200]{1,0:T(8,128)(2,1)S(1)}, s16[16,3200]{1,0:T(8,128)(2,1)S(1)}, u32[]{:S(2)}, u32[]{:S(2)}) %collective-permute-start.10) | collective-permute-done | bytes 102432 | tf_op jit(solution)/shard_map/ppermute | solution.py:682
  46.2 0.0 collective-permute-done.11.refs_5_
  46.2 2.0 %collective-permute-done.13.refs_7_ = s16[16,3200]{1,0:T(8,128)(2,1)S(1)} collective-permute-done((s16[16,3200]{1,0:T(8,128)(2,1)S(1)}, s16[16,3200]{1,0:T(8,128)(2,1)S(1)}, u32[]{:S(2)}, u32[]{:S(2)}) %collective-permute-start.13) | collective-permute-done | bytes 102432 | tf_op jit(solution)/shard_map/ppermute | solution.py:682
  48.2 0.0 collective-permute-done.8.refs_1_
  48.2 0.0 copy-done.4
  48.2 0.0 copy-done.5
  48.2 2.5 %columns.1 = (f32[2,4,64,768]{3,2,1,0:T(8,128)}, f32[4,64,768]{2,1,0:T(8,128)}) custom-call(s32[4]{0:T(128)S(1)} %pad_add_fusion.par_ref, s16[16,3200]{1,0:T(8,128)(2,1)S(1)} %collective-permute-done.7.refs_0_, s16[16,3200]{1,0:T(8,128)(2,1)S(1)} %collective-permute-done.8.refs_1_, s16[16,3200]{1,0:T(8,128)(2,1)S(1)} %collective-permute-done.9.refs_1_.refs_2_, ...), custom_call_target="tpu_custom_call" | custom-call | flops 1000 | bytes 1000 | tf_op jit(solution)/shard_map/columns/pallas_call | solution.py:698
  (6 shorter events, 0.0 us)
Async XLA Ops:
  0.6 42.4 %copy-start = (f32[4,3072]{1,0:T(4,128)S(1)}, f32[4,3072]{1,0:T(4,128)}, u32[]{:S(2)}) copy-start(f32[4,3072]{1,0:T(4,128)} %param.10) | copy-start | bytes 147460
  0.6 3.3 %copy-start.3 = (bf16[2,4,16,3072]{3,2,1,0:T(8,128)(2,1)S(1)}, bf16[2,4,16,3072]{3,2,1,0:T(8,128)(2,1)}, u32[]{:S(2)}) copy-start(bf16[2,4,16,3072]{3,2,1,0:T(8,128)(2,1)} %courant_ref.7) | copy-start | bytes 2359300
  2.6 7.3 %collective-permute-start = (s16[16,7936]{1,0:T(8,128)(2,1)}, s16[16,7936]{1,0:T(8,128)(2,1)S(1)}, u32[]{:S(2)}, u32[]{:S(2)}) collective-permute-start(s16[16,7936]{1,0:T(8,128)(2,1)} %edge.1), channel_id=1, source_target_pairs={{0,4},{4,0},{8,12},{12,8},{16,20},{20,16},{24,28},{28,24},{1,5},{5... | collective-permute-start | bytes 761864 | tf_op jit(solution)/shard_map/ppermute | solution.py:593
  4.0 1.4 %copy-start.2 = (f32[2,4,16,3072]{3,2,1,0:T(8,128)S(1)}, f32[2,4,16,3072]{3,2,1,0:T(8,128)}, u32[]{:S(2)}) copy-start(f32[2,4,16,3072]{3,2,1,0:T(8,128)} %fields_ref.5) | copy-start | bytes 4718596
  6.4 10.0 %collective-permute-start.1 = (s16[16,9472]{1,0:T(8,128)(2,1)S(1)}, s16[16,9472]{1,0:T(8,128)(2,1)S(1)}, u32[]{:S(2)}, u32[]{:S(2)}) collective-permute-start(s16[16,9472]{1,0:T(8,128)(2,1)S(1)} %get-tuple-element.27), channel_id=1, source_target_pairs={{0,4},{4,0},{8,12},{12,8},{16,20},{20,16},{24,28},{28,24},{1,5},{5... | collective-permute-start | bytes 909320 | tf_op jit(solution)/shard_map/ppermute | solution.py:604
  6.7 8.3 %collective-permute-start.2 = (s16[16,7936]{1,0:T(8,128)(2,1)S(1)}, s16[16,7936]{1,0:T(8,128)(2,1)S(1)}, u32[]{:S(2)}, u32[]{:S(2)}) collective-permute-start(s16[16,7936]{1,0:T(8,128)(2,1)S(1)} %get-tuple-element.28), channel_id=1, source_target_pairs={{8,0},{4,12},{16,8},{12,20},{24,16},{20,28},{9,1},{5,13},{17,9},{1... | collective-permute-start | bytes 761864 | tf_op jit(solution)/shard_map/ppermute | solution.py:603
  9.9 7.3 %collective-permute-start.3 = (s16[16,7936]{1,0:T(8,128)(2,1)S(1)}, s16[16,7936]{1,0:T(8,128)(2,1)S(1)}, u32[]{:S(2)}, u32[]{:S(2)}) collective-permute-start(s16[16,7936]{1,0:T(8,128)(2,1)S(1)} %collective-permute-done.edge_ref), channel_id=1, source_target_pairs={{0,8},{12,4},{8,16},{20,12},{16,24},{28,20},{1,9},{13,5},{9,17},{2... | collective-permute-start | bytes 761864 | tf_op jit(solution)/shard_map/ppermute | solution.py:605
  13.1 7.9 %collective-permute-start.4 = (s16[16,7680]{1,0:T(8,128)(2,1)S(1)}, s16[16,7680]{1,0:T(8,128)(2,1)S(1)}, u32[]{:S(2)}, u32[]{:S(2)}) collective-permute-start(s16[16,7680]{1,0:T(8,128)(2,1)S(1)} %get-tuple-element.30), channel_id=1, source_target_pairs={{0,4},{4,0},{8,12},{12,8},{16,20},{20,16},{24,28},{28,24},{1,5},{5... | collective-permute-start | bytes 737288 | tf_op jit(solution)/shard_map/ppermute | solution.py:606
  21.0 5.6 %copy-start.1 = (bf16[4,1536,256]{2,1,0:T(8,128)(2,1)S(1)}, bf16[4,1536,256]{2,1,0:T(8,128)(2,1)}, u32[]{:S(2)}) copy-start(bf16[4,1536,256]{2,1,0:T(8,128)(2,1)} %constant.48.clone.table_ref) | copy-start | bytes 9437188
  21.0 5.6 %copy-start.6 = (s32[32]{0:T(128)S(1)}, s32[32]{0:T(128)}, u32[]{:S(2)}) copy-start(s32[32]{0:T(128)} %cut_ref.5) | copy-start | bytes 388
  22.6 6.4 %collective-permute-start.6 = (s16[16,6400]{1,0:T(8,128)(2,1)S(1)}, s16[16,6400]{1,0:T(8,128)(2,1)S(1)}, u32[]{:S(2)}, u32[]{:S(2)}) collective-permute-start(s16[16,6400]{1,0:T(8,128)(2,1)S(1)} %get-tuple-element.39), channel_id=1, source_target_pairs={{0,8},{8,0},{4,12},{12,4},{16,24},{24,16},{20,28},{28,20},{1,9},{9... | collective-permute-start | bytes 614408 | tf_op jit(solution)/shard_map/ppermute | solution.py:642
  24.6 6.5 %collective-permute-start.5 = (s16[16,6400]{1,0:T(8,128)(2,1)S(1)}, s16[16,6400]{1,0:T(8,128)(2,1)S(1)}, u32[]{:S(2)}, u32[]{:S(2)}) collective-permute-start(s16[16,6400]{1,0:T(8,128)(2,1)S(1)} %get-tuple-element.38), channel_id=1, source_target_pairs={{8,16},{16,8},{12,20},{20,12},{9,17},{17,9},{13,21},{21,13},{10,18... | collective-permute-start | bytes 614408 | tf_op jit(solution)/shard_map/ppermute | solution.py:643
  31.1 17.1 %copy-start.4 = (f32[64,64]{1,0:T(8,128)S(1)}, f32[64,64]{1,0:T(8,128)}, u32[]{:S(2)}) copy-start(f32[64,64]{1,0:T(8,128)} %refs_9_.1) | copy-start | bytes 49156
  31.1 17.1 %copy-start.5 = (f32[64,64]{1,0:T(8,128)S(1)}, f32[64,64]{1,0:T(8,128)}, u32[]{:S(2)}) copy-start(f32[64,64]{1,0:T(8,128)} %constant.49.clone.refs_10_) | copy-start | bytes 49156
  32.7 8.6 %collective-permute-start.12 = (s16[16,3200]{1,0:T(8,128)(2,1)S(1)}, s16[16,3200]{1,0:T(8,128)(2,1)S(1)}, u32[]{:S(2)}, u32[]{:S(2)}) collective-permute-start(s16[16,3200]{1,0:T(8,128)(2,1)S(1)} %get-tuple-element.50), channel_id=1, source_target_pairs={{0,2},{1,3},{2,0},{3,1},{4,6},{5,7},{6,4},{7,5},{8,10},{9,11},{10,... | collective-permute-start | bytes 307208 | tf_op jit(solution)/shard_map/ppermute | solution.py:682
  34.0 7.9 %collective-permute-start.7 = (s16[16,3200]{1,0:T(8,128)(2,1)S(1)}, s16[16,3200]{1,0:T(8,128)(2,1)S(1)}, u32[]{:S(2)}, u32[]{:S(2)}) collective-permute-start(s16[16,3200]{1,0:T(8,128)(2,1)S(1)} %get-tuple-element.44), channel_id=1, source_target_pairs={{0,4},{1,5},{2,6},{3,7},{4,0},{5,1},{6,2},{7,3},{8,12},{9,13},{10,... | collective-permute-start | bytes 307208 | tf_op jit(solution)/shard_map/ppermute | solution.py:682
  35.2 7.8 %collective-permute-start.9 = (s16[16,3200]{1,0:T(8,128)(2,1)S(1)}, s16[16,3200]{1,0:T(8,128)(2,1)S(1)}, u32[]{:S(2)}, u32[]{:S(2)}) collective-permute-start(s16[16,3200]{1,0:T(8,128)(2,1)S(1)} %get-tuple-element.46), channel_id=1, source_target_pairs={{0,6},{1,7},{2,4},{3,5},{4,2},{5,3},{6,0},{7,1},{8,14},{9,15},{10,... | collective-permute-start | bytes 307208 | tf_op jit(solution)/shard_map/ppermute | solution.py:682
  35.4 10.8 %collective-permute-start.10 = (s16[16,3200]{1,0:T(8,128)(2,1)S(1)}, s16[16,3200]{1,0:T(8,128)(2,1)S(1)}, u32[]{:S(2)}, u32[]{:S(2)}) collective-permute-start(s16[16,3200]{1,0:T(8,128)(2,1)S(1)} %get-tuple-element.47), channel_id=1, source_target_pairs={{0,7},{1,6},{2,5},{3,4},{4,3},{5,2},{6,1},{7,0},{8,15},{9,14},{10,... | collective-permute-start | bytes 307208 | tf_op jit(solution)/shard_map/ppermute | solution.py:682
  41.3 4.9 %collective-permute-start.11 = (s16[16,3200]{1,0:T(8,128)(2,1)S(1)}, s16[16,3200]{1,0:T(8,128)(2,1)S(1)}, u32[]{:S(2)}, u32[]{:S(2)}) collective-permute-start(s16[16,3200]{1,0:T(8,128)(2,1)S(1)} %get-tuple-element.49), channel_id=1, source_target_pairs={{0,1},{1,0},{2,3},{3,2},{4,5},{5,4},{6,7},{7,6},{8,9},{9,8},{10,11... | collective-permute-start | bytes 307208 | tf_op jit(solution)/shard_map/ppermute | solution.py:682
  41.3 6.9 %collective-permute-start.13 = (s16[16,3200]{1,0:T(8,128)(2,1)S(1)}, s16[16,3200]{1,0:T(8,128)(2,1)S(1)}, u32[]{:S(2)}, u32[]{:S(2)}) collective-permute-start(s16[16,3200]{1,0:T(8,128)(2,1)S(1)} %get-tuple-element.51), channel_id=1, source_target_pairs={{0,3},{1,2},{2,1},{3,0},{4,7},{5,6},{6,5},{7,4},{8,11},{9,10},{10,... | collective-permute-start | bytes 307208 | tf_op jit(solution)/shard_map/ppermute | solution.py:682
  41.9 6.3 %collective-permute-start.8 = (s16[16,3200]{1,0:T(8,128)(2,1)S(1)}, s16[16,3200]{1,0:T(8,128)(2,1)S(1)}, u32[]{:S(2)}, u32[]{:S(2)}) collective-permute-start(s16[16,3200]{1,0:T(8,128)(2,1)S(1)} %get-tuple-element.45), channel_id=1, source_target_pairs={{0,5},{1,4},{2,7},{3,6},{4,1},{5,0},{6,3},{7,2},{8,13},{9,12},{10,... | collective-permute-start | bytes 307208 | tf_op jit(solution)/shard_map/ppermute | solution.py:682
